TPU v7x, 256 devices: a whole 4x4x8 slice. The times are simulated.
256 devices in a mesh: gx: 32 (over x, z), gy: 8 (over y, core).
Axes of the slice: x: 4, y: 4, z: 8, core: 2. Of those that a mesh axis runs over, the one named last changes fastest.
Arguments:
- right_sides: float32 [2, 512, 512, 128], P(None, 'gx', 'gy'), may hold values from -24 to 24, as said below
- diagonal: float32 [512, 512, 128], P('gx', 'gy'), may hold values from 0.5 to 2
- velocity: float32 [3, 512, 512, 128], P(None, 'gx', 'gy'), may hold values from -0.6 to 0.6
Outputs:
- orthonormal: float32 [10, 512, 512, 128], P(None, 'gx', 'gy')
- triangle: float32 [10, 10], replicated
- update: float32 [2, 512, 512, 128], P(None, 'gx', 'gy')
Inputs may be any that keep to these rules, and one draw needn't show every extreme that they name: `right_sides`: 2 right-hand sides.
All inputs are finite; a program needn't handle non-finite values.
Results may differ from a plain program's by a relative error of at most 0.0004.
Values sent between devices are 32-bit elements; how exact they have to be, the bound alone decides.
No kernel may reach another device: no remote copies, remote signals or barrier semaphores. Data moves between devices by JAX's collectives and lax.ppermute only.
A program may use at most 128 MiB of HBM per device.

v0:
```python
import math

import jax
import jax.numpy as jnp
from jax import lax
from jax.sharding import PartitionSpec as P

S = 4
RHS = 2
COLS = 10


def extended(shard, sides, width):
    for axis, dim in sides:
        size, length = (lax.axis_size(axis), shard.shape[dim])
        up = [(i, (i + 1) % size) for i in range(size - 1)]
        down = [(j, i) for i, j in up]
        last = lax.slice_in_dim(shard, length - width, length, axis=dim)
        leading = lax.slice_in_dim(shard, 0, width, axis=dim)
        before = lax.ppermute(last, axis, up)
        after = lax.ppermute(leading, axis, down)
        shard = jnp.concatenate([before, shard, after], axis=dim)
    return shard


def combine(padded, velocity, diagonal):
    summed = (1.0 + velocity[0]) * padded[:, :-2, 1:-1, 1:-1] + (1.0 - velocity[0]) * padded[
        :, 2:, 1:-1, 1:-1
    ]
    summed = (
        summed
        + (1.0 + velocity[1]) * padded[:, 1:-1, :-2, 1:-1]
        + (1.0 - velocity[1]) * padded[:, 1:-1, 2:, 1:-1]
    )
    summed = (
        summed
        + (1.0 + velocity[2]) * padded[:, 1:-1, 1:-1, :-2]
        + (1.0 - velocity[2]) * padded[:, 1:-1, 1:-1, 2:]
    )
    return summed / (6.0 + diagonal)


def orthonormalize(columns):
    count = columns.shape[0]
    vectors = []
    factor = jnp.zeros((count, count), jnp.float32)
    for column in range(count):
        current = columns[column]
        for earlier in range(column):
            weight = jnp.sum(vectors[earlier] * current)
            current = current - weight * vectors[earlier]
            factor = factor.at[earlier, column].set(weight)
        length = jnp.sqrt(jnp.sum(current * current))
        factor = factor.at[column, column].set(length)
        vectors.append(current / length)
    return (jnp.stack(vectors), factor)


def back_substitute(upper, target):
    count = upper.shape[0]
    rows = [None] * count
    for index in reversed(range(count)):
        value = target[index]
        for later in range(index + 1, count):
            value = value - upper[index, later] * rows[later]
        rows[index] = value / upper[index, index]
    return jnp.stack(rows)


def least_squares(triangle):
    image = triangle[:, : RHS * S] - triangle[:, RHS:]
    basis_m, upper = orthonormalize(image.T)
    target = jnp.dot(basis_m, triangle[:, :RHS], precision=lax.Precision.HIGHEST)
    return back_substitute(upper, target)


def body(right_sides, diagonal, velocity):
    width_x = right_sides.shape[1]
    width_y = right_sides.shape[2]
    width_z = right_sides.shape[3]
    count_x = lax.axis_size("gx")
    count_y = lax.axis_size("gy")
    devices = count_x * count_y
    local_cells = width_x * width_y * width_z
    scale = math.sqrt(local_cells * devices)
    current = right_sides
    degrees = [current]
    for degree in range(S):
        padded = extended(current, (("gx", 1), ("gy", 2)), 1)
        padded = jnp.pad(padded, ((0, 0), (0, 0), (0, 0), (1, 1)))
        current = combine(padded, velocity, diagonal)
        degrees.append(current)
    basis = jnp.stack(degrees).reshape(COLS, local_cells)
    local_q, local_r = orthonormalize(basis)
    device_index = lax.axis_index(("gx", "gy"))
    every = lax.all_gather(local_r[None], ("gx", "gy"), axis=0, tiled=True)
    joined_q, merged = orthonormalize(every.reshape(devices * COLS, COLS).T)
    product = lax.dynamic_slice_in_dim(joined_q, device_index * COLS, COLS, 1).T
    triangle = merged / scale
    orthonormal = (jnp.dot(product.T, local_q, precision=lax.Precision.HIGHEST) * scale).reshape(
        COLS, width_x, width_y, width_z
    )
    coefficients = least_squares(triangle)
    update = jnp.dot(coefficients.T, basis[: RHS * S], precision=lax.Precision.HIGHEST).reshape(
        RHS, width_x, width_y, width_z
    )
    return (orthonormal, triangle, update)


def solution(mesh):
    return jax.shard_map(
        body,
        mesh=mesh,
        in_specs=(P(None, "gx", "gy", None), P("gx", "gy", None), P(None, "gx", "gy", None)),
        out_specs=(P(None, "gx", "gy", None), P(), P(None, "gx", "gy", None)),
        check_vma=False,
    )
```

profile of v0, /device:TPU:1, one launch (start us, length us, event | category | flops | bytes accessed | tf_op | source)
XLA Modules:
  0.0 773.3 jit_solution(4897104498002988673)
XLA Ops:
  80.8 5.2 collective-permute-start.12
  91.4 4.8 collective-permute-start.14
  100.7 4.9 slice.3123
  109.2 6.2 reshape.4044
  119.9 18.8 %fusion.61 = (f32[1,131072]{1,0:T(1,128)S(1)}, f32[1,131072]{1,0:T(1,128)S(1)}, f32[1,131072]{1,0:T(1,128)S(1)}, f32[1,131072]{1,0:T(1,128)S(1)}, f32[1,131072]{...) fusion(f32[10,131072]{1,0:T(8,128)} %reshape.4044, ...), kind=kLoop, calls=%fused_computation.496 | loop fusion | flops 131072 | bytes 10485764 | tf_op jit(solution)/shard_map/slice | solution.py:48
  154.6 8.7 %multiply_reduce_fusion.8 = (f32[]{:T(128)}, f32[]{:T(128)}, f32[]{:T(128)}, f32[]{:T(128)}, f32[]{:T(128)}, /*index=5*/f32[]{:T(128)}, f32[]{:T(128)}, f32[]{:T(128)}, f32[131072]{0:T(1024)S(1)}) fusion(f32[131072]{0:T(1024)S(1)} %bitcast.365, f32[131072]{0:T(1024)S(1)} %bitcast.353, f32[]{:T(128)} %get-tuple-element.1802, f32[131072]{0:T(1024)S(1)} %bitcast.368, ...), kind=kLoop, calls=%fused_computation.121 | loop fusion | flops 4587512 | bytes 5767240 | tf_op jit(solution)/shard_map/reduce_sum | solution.py:50
  175.2 12.1 %multiply_reduce_fusion.7 = (f32[]{:T(128)}, f32[]{:T(128)}, f32[]{:T(128)}, f32[]{:T(128)}, f32[]{:T(128)}, /*index=5*/f32[]{:T(128)}, f32[]{:T(128)}, f32[1310...) fusion(f32[131072]{0:T(1024)S(1)} %get-tuple-element.2011, ...), kind=kLoop, calls=%fused_computation.119 | loop fusion | flops 5373945 | bytes 8388692 | tf_op jit(solution)/shard_map/reduce_sum | solution.py:50
  195.0 7.2 multiply_reduce_fusion.6
  215.8 9.7 %multiply_reduce_fusion.5 = (f32[]{:T(128)}, f32[]{:T(128)}, f32[]{:T(128)}, f32[]{:T(128)}, f32[]{:T(128)}, /*index=5*/f32[131072]{0:T(1024)S(1)}, f32[131072]{0:T(1024)}, f32[131072]{0:T(1024)}, f32[131072]{0:T(1024)}) fusion(f32[131072]{0:T(1024)S(1)} %get-tuple-element.2001, f32[]{:T(128)} %sqrt.88, f32[131072]{0:T(1024)S(1)} %get-tuple-element.1999, ...), kind=kLoop, calls=%fused_computation.115 | loop fusion | flops 4325371 | bytes 6291528 | tf_op jit(solution)/shard_map/reduce_sum | solution.py:50
  234.3 5.4 multiply_reduce_fusion.4
  255.8 6.6 multiply_reduce_fusion.3
  302.0 71.5 %all_gather.3 = f32[256,10,10]{2,1,0:T(8,128)S(1)} all-gather(f32[1,10,10]{2,1,0:T(8,128)S(1)} %scatter.564), channel_id=1, replica_groups=mesh['gx'=32,'gy'=8] {'gx','gy'}, dimensions={0}, use_global_device_ids=true | all-gather | bytes 102800 | tf_op jit(solution)/shard_map/all_gather | solution.py:96
  391.1 6.3 multiply_reduce_fusion.63
  408.2 8.7 %multiply_reduce_fusion.62 = (f32[]{:T(128)}, f32[]{:T(128)}, f32[]{:T(128)}, f32[]{:T(128)}, f32[]{:T(128)}, /*index=5*/f32[]{:T(128)}, f32[]{:T(128)}, f32[256...) fusion(f32[2560]{0:T(1024)S(1)} %get-tuple-element.1971, ...), kind=kLoop, calls=%fused_computation.250 | loop fusion | flops 104953 | bytes 163924 | tf_op jit(solution)/shard_map/reduce_sum | solution.py:50
  424.2 5.3 multiply_reduce_fusion.61
  442.9 7.0 multiply_reduce_fusion.60
  563.6 5.1 multiply_reduce_fusion.114
  609.4 50.4 %subtract_divide_fusion = (f32[1,131072]{1,0:T(1,128)S(1)}, f32[1,131072]{1,0:T(1,128)S(1)}, f32[1,131072]{1,0:T(1,128)S(1)}, f32[1,131072]{1,0:T(1,128)S(1)}, f...) fusion(f32[1,131072]{1,0:T(1,128)S(1)} %get-tuple-element.2020,, ...), kind=kLoop, calls=%fused_computation.97 | loop fusion | flops 12976128 | bytes 9961688 | tf_op jit(solution)/shard_map/div | solution.py:55
  664.3 17.3 %subtract_divide_fusion.25 = (f32[1,10]{1,0:T(1,128)S(1)}, f32[1,10]{1,0:T(1,128)S(1)}, f32[1,10]{1,0:T(1,128)S(1)}, f32[1,10]{1,0:T(1,128)S(1)}, f32[1,10]{1,0:...) fusion(f32[1,10]{1,0:T(1,128)S(1)} %get-tuple-element.1934, f32[]{:T(128)S(6)} %sqrt.111, ...), kind=kLoop, calls=%fused_computation.424 | loop fusion | flops 630 | bytes 740 | tf_op jit(solution)/shard_map/div | solution.py:55
  681.8 22.3 %subtract_divide_fusion.18 = (f32[1,2]{0,1:T(2,128)S(1)}, f32[1,2]{0,1:T(2,128)S(1)}, f32[1,2]{0,1:T(2,128)S(1)}, f32[1,2]{0,1:T(2,128)S(1)}, f32[1,2]{0,1:T(2,1...) fusion(f32[8,2]{0,1:T(2,128)S(1)} %fusion.45, f32[]{:T(128)} %bitcast.239, f32[]{:T(128)} %bitcast.238, ...), kind=kLoop, calls=%fused_computation.387 | loop fusion | flops 128 | bytes 272 | tf_op jit(solution)/shard_map/div | solution.py:66
  704.2 6.0 fusion.47
  711.2 28.9 %subtract_divide_fusion.9 = (f32[1,2560]{1,0:T(1,128)S(1)}, f32[1,2560]{1,0:T(1,128)S(1)}, f32[1,2560]{1,0:T(1,128)S(1)}, f32[1,2560]{1,0:T(1,128)S(1)}, f32[1,2...) fusion(f32[1,2560]{1,0:T(1,128)S(1)} %get-tuple-element.1974, ...), kind=kLoop, calls=%fused_computation.335 | loop fusion | flops 253440 | bytes 194776 | tf_op jit(solution)/shard_map/div | solution.py:55
  740.3 17.9 %stack.29 = f32[10,131072]{1,0:T(8,128)} concatenate(f32[1,131072]{1,0:T(1,128)S(1)} %get-tuple-element.2020, f32[1,131072]{1,0:T(1,128)} %get-tuple-element.1983, f32[1,131072]{1,0:T(1,128)} %get-tuple-element.1982, f32[1,131072]{1,0:T(1,128)} %get-tuple-element.1981, f32[1,131072]{1,0:T(1,128)} %get-tuple-element.1980, f32[1,131072]{1,0:T(1,128)S(1)} %get-tuple-element.1979, ...), dimensions={0} | concatenate | bytes 10485760 | tf_op jit(solution)/shard_map/stack | solution.py:56
  758.3 10.3 %convolution_multiply_fusion = f32[10,131072]{1,0:T(8,128)S(1)} fusion(f32[10,131072]{1,0:T(8,128)} %stack.29, f32[10,2560]{1,0:T(8,128)S(1)} %stack.28, s32[]{:T(128)S(6)} %select_n.3), kind=kOutput, calls=%fused_computation | convolution fusion | flops 158597120 | bytes 10493956 | tf_op jit(solution)/shard_map/dot_general | solution.py:100
  (382 shorter events, 357.0 us)
Async XLA Ops:
  1.6 12.0 %collective-permute-start = (f32[2,1,64,128]{3,2,1,0:T(8,128)S(1)}, f32[2,1,64,128]{3,2,1,0:T(8,128)S(1)}, u32[]{:S(2)}, u32[]{:S(2)}) collective-permute-start(f32[2,1,64,128]{3,2,1,0:T(8,128)S(1)} %get-tuple-element.2050), channel_id=1, source_target_pairs={{0,8},{8,16},{16,24},{24,32},{32,40},{40,48},{48,56},{56,64},{64,7... | collective-permute-start | bytes 196616 | tf_op jit(solution)/shard_map/ppermute | solution.py:20
  6.0 7.7 collective-permute-start.1
  9.7 34.3 %copy-start.4 = (f32[16,64,128]{2,1,0:T(8,128)}, f32[16,64,128]{2,1,0:T(8,128)S(1)}, u32[]{:S(2)}) copy-start(f32[16,64,128]{2,1,0:T(8,128)S(1)} %get-tuple-element.2031) | copy-start | bytes 1572868
  9.7 34.3 %copy-start.7 = (f32[16,64,128]{2,1,0:T(8,128)}, f32[16,64,128]{2,1,0:T(8,128)S(1)}, u32[]{:S(2)}) copy-start(f32[16,64,128]{2,1,0:T(8,128)S(1)} %get-tuple-element.2032) | copy-start | bytes 1572868
  9.7 34.3 %copy-start.10 = (f32[16,64,128]{2,1,0:T(8,128)}, f32[16,64,128]{2,1,0:T(8,128)S(1)}, u32[]{:S(2)}) copy-start(f32[16,64,128]{2,1,0:T(8,128)S(1)} %get-tuple-element.2033) | copy-start | bytes 1572868
  9.7 34.3 %copy-start.13 = (f32[16,64,128]{2,1,0:T(8,128)}, f32[16,64,128]{2,1,0:T(8,128)S(1)}, u32[]{:S(2)}) copy-start(f32[16,64,128]{2,1,0:T(8,128)S(1)} %get-tuple-element.2034) | copy-start | bytes 1572868
  9.7 34.3 %copy-start.16 = (f32[16,64,128]{2,1,0:T(8,128)}, f32[16,64,128]{2,1,0:T(8,128)S(1)}, u32[]{:S(2)}) copy-start(f32[16,64,128]{2,1,0:T(8,128)S(1)} %broadcast_add_fusion) | copy-start | bytes 1572868
  13.8 6.0 collective-permute-start.2
  17.9 5.1 collective-permute-start.3
  25.1 6.2 collective-permute-start.4
  29.3 5.2 collective-permute-start.5
  34.6 5.3 collective-permute-start.6
  37.9 5.1 collective-permute-start.7
  48.4 27.7 %copy-start = (f32[2,16,64,128]{3,2,1,0:T(8,128)}, f32[2,16,64,128]{3,2,1,0:T(8,128)S(1)}, u32[]{:S(2)}) copy-start(f32[2,16,64,128]{3,2,1,0:T(8,128)S(1)} %get-tuple-element.2016) | copy-start | bytes 3145732
  48.4 6.3 collective-permute-start.8
  52.8 6.5 collective-permute-start.9
  59.4 15.7 %collective-permute-start.10 = (f32[2,18,1,128]{3,2,1,0:T(1,128)S(1)}, f32[2,18,1,128]{3,2,1,0:T(1,128)S(1)}, u32[]{:S(2)}, u32[]{:S(2)}) collective-permute-start(f32[2,18,1,128]{3,2,1,0:T(1,128)S(1)} %get-tuple-element.2037), channel_id=1, source_target_pairs={{0,1},{1,2},{2,3},{3,4},{4,5},{5,6},{6,7},{8,9},{9,10},{10,11},{11... | collective-permute-start | bytes 55304 | tf_op jit(solution)/shard_map/ppermute | solution.py:20
  62.4 12.6 %collective-permute-start.11 = (f32[2,18,1,128]{3,2,1,0:T(1,128)S(1)}, f32[2,18,1,128]{3,2,1,0:T(1,128)S(1)}, u32[]{:S(2)}, u32[]{:S(2)}) collective-permute-start(f32[2,18,1,128]{3,2,1,0:T(1,128)S(1)} %get-tuple-element.2038), channel_id=1, source_target_pairs={{1,0},{2,1},{3,2},{4,3},{5,4},{6,5},{7,6},{9,8},{10,9},{11,10},{12... | collective-permute-start | bytes 55304 | tf_op jit(solution)/shard_map/ppermute | solution.py:21
  76.2 22.3 %copy-start.1 = (f32[2,16,64,128]{3,2,1,0:T(8,128)S(1)}, f32[2,16,64,128]{3,2,1,0:T(8,128)}, u32[]{:S(2)}) copy-start(f32[2,16,64,128]{3,2,1,0:T(8,128)} %copy-done) | copy-start | bytes 3145732
  80.8 7.1 collective-permute-start.12
  86.0 5.4 collective-permute-start.13
  91.4 14.2 %collective-permute-start.14 = (f32[2,18,1,128]{3,2,1,0:T(1,128)S(1)}, f32[2,18,1,128]{3,2,1,0:T(1,128)S(1)}, u32[]{:S(2)}, u32[]{:S(2)}) collective-permute-start(f32[2,18,1,128]{3,2,1,0:T(1,128)S(1)} %get-tuple-element.2035), channel_id=1, source_target_pairs={{0,1},{1,2},{2,3},{3,4},{4,5},{5,6},{6,7},{8,9},{9,10},{10,11},{11... | collective-permute-start | bytes 55304 | tf_op jit(solution)/shard_map/ppermute | solution.py:20
  96.3 9.3 %collective-permute-start.15 = (f32[2,18,1,128]{3,2,1,0:T(1,128)S(1)}, f32[2,18,1,128]{3,2,1,0:T(1,128)S(1)}, u32[]{:S(2)}, u32[]{:S(2)}) collective-permute-start(f32[2,18,1,128]{3,2,1,0:T(1,128)S(1)} %get-tuple-element.2036), channel_id=1, source_target_pairs={{1,0},{2,1},{3,2},{4,3},{5,4},{6,5},{7,6},{9,8},{10,9},{11,10},{12... | collective-permute-start | bytes 55304 | tf_op jit(solution)/shard_map/ppermute | solution.py:21
  262.4 23.1 %copy-start.27 = (f32[131072]{0:T(1024)S(1)}, f32[131072]{0:T(1024)}, u32[]{:S(2)}) copy-start(f32[131072]{0:T(1024)} %get-tuple-element.1989) | copy-start | bytes 1572868
  (27 other events, 222.8 us)
where the time goes:
time: 788 us; the launch traced here: 773 us
  other arithmetic  346 us (44%)
  local copies, waits for them, and re-layouts  205 us (26%)
  blocking collectives  71.5 us (9%)
  between operations  69.8 us (9%)
  starting transfers between devices  46.6 us (6%)
  waiting for transfers between devices  17.6 us (2%)
  matrix products  16.3 us (2%)
    reduce_sum x37, other arithmetic, orthonormalize(): weight = jnp.sum(vectors[earlier] * current)  148 us
    scatter x115, local copies, waits for them, and re-layouts, orthonormalize(): factor = factor.at[earlier, column].set(weight)  103 us
    div x4, other arithmetic, orthonormalize(): vectors.append(current / length)  96.7 us
    all_gather x1, blocking collectives, body(): every = lax.all_gather(local_r[None], ('gx', 'gy'), axis=0, tiled=True)  71.5 us
    another operation x35, local copies, waits for them, and re-layouts  51.7 us
    ppermute x8, starting transfers between devices, extended(): before = lax.ppermute(last, axis, up)  33.6 us
    reduce_sum x15, other arithmetic, orthonormalize(): length = jnp.sqrt(jnp.sum(current * current))  32.1 us
    div x1, other arithmetic, back_substitute(): rows[index] = value / upper[index, index]  22.3 us
  transfers between devices with their start and end apart: 16, of which 5 were waited for; matrix products, arithmetic and copies ran while one was open for 3% of the time, Pallas kernels for 0%

commit v1 on v0

v1 whole, which is shorter than its diff:
```python
import functools
import math

import jax
import jax.numpy as jnp
from jax import lax
from jax.experimental import pallas as pl
from jax.experimental.pallas import tpu as pltpu
from jax.sharding import PartitionSpec as P

S = 4
RHS = 2
COLS = 10
YP = 16
VMEM_LIMIT = 56 * 1024 * 1024

F32 = jnp.float32
FIELD_CORNER = [(dx, dy) for dx in (1, 2, 3) for dy in (1, 2, 3) if dx + dy <= 4]
COEF_CORNER = [(dx, dy) for dx in (1, 2) for dy in (1, 2) if dx + dy <= 3]
CORNER_ROWS = RHS * len(FIELD_CORNER) + 4 * len(COEF_CORNER)


def slot(i, k):
    return (8 * k if k < 8 else 64 + 16 * (k - 8)) + i


def run_copies(copies):
    for copy in copies:
        copy.start()
    for copy in copies:
        copy.wait()


def pack_x_kernel(X, rhs, vel, diag, low, high, sems):
    copies = []
    for out, at4, at3 in ((high, X - 4, X - 3), (low, 0, 0)):
        for f in range(RHS):
            copies.append((rhs.at[f, pl.ds(at4, 4)], out.at[pl.ds(4 * f, 4)]))
        for c in range(3):
            copies.append((vel.at[c, pl.ds(at3, 3)], out.at[pl.ds(8 + 3 * c, 3)]))
        copies.append((diag.at[pl.ds(at3, 3)], out.at[pl.ds(17, 3)]))
    run_copies([pltpu.make_async_copy(s, d, sems.at[i]) for i, (s, d) in enumerate(copies)])


def pack_y_kernel(X, Y, rhs, vel, diag, low, high, c_ll, c_lh, c_hl, c_hh, stage, sems):
    copies = []
    for out, at in ((high, Y - 8), (low, 0)):
        copies.append((rhs.at[:, :, pl.ds(at, 8)], out.at[pl.ds(0, 2)]))
        copies.append((vel.at[:, :, pl.ds(at, 8)], out.at[pl.ds(2, 3)]))
        copies.append((diag.at[:, pl.ds(at, 8)], out.at[5]))
    for n, (ax, ay) in enumerate(((0, 0), (0, Y - 8), (X - 3, 0), (X - 3, Y - 8))):
        copies.append((rhs.at[:, pl.ds(ax, 3), pl.ds(ay, 8)], stage.at[n, pl.ds(0, 2)]))
        copies.append((vel.at[:, pl.ds(ax, 3), pl.ds(ay, 8)], stage.at[n, pl.ds(2, 3)]))
        copies.append((diag.at[pl.ds(ax, 3), pl.ds(ay, 8)], stage.at[n, 5]))
    run_copies([pltpu.make_async_copy(s, d, sems.at[i]) for i, (s, d) in enumerate(copies)])
    for n, out in enumerate((c_ll, c_lh, c_hl, c_hh)):
        row = 0
        for f in range(6):
            for dx, dy in FIELD_CORNER if f < 2 else COEF_CORNER:
                x = dx - 1 if n < 2 else 3 - dx
                y = dy - 1 if n % 2 == 0 else 8 - dy
                out[row : row + 1, :] = stage[n, f, x, y : y + 1, :]
                row += 1


def total(x):
    return jnp.sum(jnp.sum(x, axis=0, keepdims=True), axis=1, keepdims=True)


def fold8(x):
    rows = x.shape[0]
    parts = [x[8 * i : 8 * i + 8] for i in range(rows // 8)]
    while len(parts) > 1:
        parts = [a + b for a, b in zip(parts[::2], parts[1::2])] + (
            [parts[-1]] if len(parts) % 2 else []
        )
    return parts[0]


def main_kernel(
    X, Y, rhs, vel, diag, xl, xh, yl, yh, c_ll, c_lh, c_hl, c_hh,
    basis, packed, V, V4, U, A, Q, sems, out_sems,
):
    gx, gy = lax.axis_index("gx"), lax.axis_index("gy")
    nx, ny = lax.axis_size("gx"), lax.axis_size("gy")
    XE, YE = X + 8, Y + 2 * YP
    own_x, own_y = pl.ds(4, X), pl.ds(YP, Y)
    copies = [
        (rhs, V.at[0, :, own_x, own_y]),
        (vel, U.at[pl.ds(0, 3), own_x, own_y]),
        (diag, U.at[3, own_x, own_y]),
        (yl.at[pl.ds(0, 2)], V.at[0, :, own_x, pl.ds(YP - 8, 8)]),
        (yl.at[pl.ds(2, 4)], U.at[:, own_x, pl.ds(YP - 8, 8)]),
        (yh.at[pl.ds(0, 2)], V.at[0, :, own_x, pl.ds(YP + Y, 8)]),
        (yh.at[pl.ds(2, 4)], U.at[:, own_x, pl.ds(YP + Y, 8)]),
    ]
    for got, at4, at3 in ((xl, 0, 1), (xh, X + 4, X + 4)):
        for f in range(RHS):
            copies.append((got.at[pl.ds(4 * f, 4)], V.at[0, f, pl.ds(at4, 4), own_y]))
        for c in range(4):
            copies.append((got.at[pl.ds(8 + 3 * c, 3)], U.at[c, pl.ds(at3, 3), own_y]))
    run_copies([pltpu.make_async_copy(s, d, sems.at[i]) for i, (s, d) in enumerate(copies)])
    for n, got in enumerate((c_ll, c_lh, c_hl, c_hh)):
        row = 0
        for f in range(6):
            for dx, dy in FIELD_CORNER if f < 2 else COEF_CORNER:
                x = 4 - dx if n < 2 else X + 3 + dx
                y = YP - dy if n % 2 == 0 else YP + Y - 1 + dy
                value = got[row : row + 1, :]
                if f < 2:
                    V[0, f, x, y : y + 1, :] = value
                else:
                    U[f - 2, x, y : y + 1, :] = value
                row += 1

    WIDE = Y + 16
    inner = pl.ds(YP - 8, WIDE)
    yi = lax.broadcasted_iota(jnp.int32, (WIDE, 128), 0)
    zi = lax.broadcasted_iota(jnp.int32, (WIDE, 128), 1)
    y_in = ((yi >= 8) | (gy > 0)) & ((yi < Y + 8) | (gy < ny - 1))

    def coefficients(x, carry):
        x_in = ((x >= 4) | (gx > 0)) & ((x < X + 4) | (gx < nx - 1))
        g = jnp.where(y_in & x_in, 1.0 / (6.0 + U[3, x, inner, :]), 0.0)
        for c in range(3):
            ug = U[c, x, inner, :] * g
            plus, minus = g + ug, g - ug
            if c == 2:
                plus = jnp.where(zi == 0, 0.0, plus)
                minus = jnp.where(zi == 127, 0.0, minus)
            A[2 * c, x, inner, :] = plus
            A[2 * c + 1, x, inner, :] = minus
        return carry

    lax.fori_loop(1, XE - 1, coefficients, 0)

    def step(source, store, first, last, begin, rows, chunk):
        def row(x, carry):
            for at in range(begin, begin + rows, chunk):
                here = pl.ds(at, chunk)
                a = [A[c, x, here, :] for c in range(6)]
                for f in range(RHS):
                    centre = source[f, x, here, :]
                    value = a[0] * source[f, x - 1, here, :] + a[1] * source[f, x + 1, here, :]
                    value += a[2] * source[f, x, pl.ds(at - 1, chunk), :]
                    value += a[3] * source[f, x, pl.ds(at + 1, chunk), :]
                    value += a[4] * pltpu.roll(centre, 1, 1)
                    value += a[5] * pltpu.roll(centre, 127, 1)
                    store(f, x, at, chunk, value)
            return carry

        lax.fori_loop(first, last, row, 0)

    outs = []

    def send(k, source):
        copy = pltpu.make_async_copy(source, basis.at[pl.ds(2 * (k - 1), 2)], out_sems.at[k - 1])
        copy.start()
        outs.append(copy)

    for k in range(1, S):

        def store(f, x, at, chunk, value, k=k):
            V[k, f, x, pl.ds(at, chunk), :] = value

        step(V.at[k - 1], store, k, XE - k, YP - 8, WIDE, 40)
        send(k, V.at[k, :, own_x, own_y])

    def store4(f, x, at, chunk, value):
        V4[f, x - 4, pl.ds(at - YP, chunk), :] = value

    step(V.at[S - 1], store4, 4, X + 4, YP, Y, 32)
    send(S, V4)

    def original(k, x, at, size):
        if k >= 8:
            return V4[k - 8, x, pl.ds(at, size), :]
        return V[k // 2, k % 2, x + 4, pl.ds(YP + at, size), :]

    CH = 32
    zero = jnp.zeros((8, 128), F32)

    def first_dots(x, accs):
        accs = list(accs)
        for at in range(0, Y, CH):
            q = original(0, x, at, CH)
            for k in range(COLS):
                accs[k] = accs[k] + fold8(q * original(k, x, at, CH))
        return tuple(accs)

    accs = lax.fori_loop(0, X, first_dots, (zero,) * COLS)
    lane = lax.broadcasted_iota(jnp.int32, (1, 128), 1)
    line = jnp.zeros((1, 128), F32)
    for j in range(COLS):
        dots = [total(a) for a in accs]
        norm2 = dots[0]
        live = norm2 > 0.0
        safe = jnp.where(live, norm2, 1.0)
        length = jnp.sqrt(safe)
        inv = jnp.where(live, 1.0 / length, 0.0)
        for k in range(j, COLS):
            entry = dots[k - j] * inv
            line = jnp.where(lane == slot(j, k), entry, line)
        if j == COLS - 1:
            break
        inv2 = inv * inv
        alphas = [jnp.broadcast_to(d * inv2, (8, 128)) for d in dots[1:]]

        def get(k, x, at, size, j=j):
            if j == 0 or k == 0:
                return original(k, x, at, size)
            return Q[k - 1, x, pl.ds(at, size), :]

        def sweep(x, accs, j=j, get=get, alphas=alphas):
            accs = list(accs)
            for at in range(0, Y, CH):
                q = get(j, x, at, CH)
                after = None
                for k in range(j + 1, COLS):
                    alpha = jnp.concatenate([alphas[k - j - 1]] * (CH // 8), axis=0)
                    value = get(k, x, at, CH) - alpha * q
                    Q[k - 1, x, pl.ds(at, CH), :] = value
                    if k == j + 1:
                        after = value
                    accs[k - j - 1] = accs[k - j - 1] + fold8(after * value)
            return tuple(accs)

        accs = lax.fori_loop(0, X, sweep, (zero,) * (COLS - 1 - j))
    packed[...] = jnp.broadcast_to(line, packed.shape)
    for copy in outs:
        copy.wait()


def fold_lanes(x):
    parts = [x[:, i : i + 128] for i in range(0, x.shape[1], 128)]
    return functools.reduce(lambda a, b: a + b, parts)


def merged_factor(gathered):
    g = gathered.T
    cols = []
    for k in range(COLS):
        if k < 8:
            cols.append([g[8 * k : 8 * k + 8]])
        else:
            at = 64 + 16 * (k - 8)
            cols.append([g[at : at + 8], g[at + 8 : at + 16]])
    R = {}
    for j in range(COLS):
        dots = []
        for k in range(j, COLS):
            p = fold_lanes(cols[j][0] * cols[k][0])
            if j >= 8:
                p = p + fold_lanes(cols[j][1] * cols[k][1])
            dots.append(total(p))
        inv = 1.0 / jnp.sqrt(dots[0])
        for k in range(j, COLS):
            R[j, k] = dots[k - j] * inv
        inv2 = inv * inv
        for k in range(j + 1, COLS):
            alpha = dots[k - j] * inv2
            for part in range(len(cols[j])):
                cols[k][part] = cols[k][part] - alpha * cols[j][part]
    return R


def inverse(R):
    T = {}
    recip = [1.0 / R[j, j] for j in range(COLS)]
    for j in range(COLS):
        T[j, j] = recip[j]
        for i in range(j):
            s = T[i, i] * R[i, j]
            for k in range(i + 1, j):
                s = s + T[i, k] * R[k, j]
            T[i, j] = -s * recip[j]
    return T


def least_squares(R):
    n = RHS * S
    cols = []
    for c in range(n):
        col = []
        for i in range(c + RHS + 1):
            minus = R[i, c + RHS]
            col.append(R[i, c] - minus if i <= c else -minus)
        cols.append(col)
    upper, target = {}, {}
    recips = []

    def dot(a, b):
        terms = [x * y for x, y in zip(a, b)]
        while len(terms) > 1:
            terms = [x + y for x, y in zip(terms[::2], terms[1::2])] + (
                [terms[-1]] if len(terms) % 2 else []
            )
        return terms[0]

    for j in range(n):
        inv = 1.0 / jnp.sqrt(dot(cols[j], cols[j]))
        recips.append(inv)
        q = [v * inv for v in cols[j]]
        for c in range(j + 1, n):
            w = dot(q, cols[c])
            upper[j, c] = w
            for i in range(len(q)):
                cols[c][i] = cols[c][i] - w * q[i]
        for e in range(RHS):
            target[j, e] = dot(q, [R[i, e] for i in range(e + 1)])
    coef = {}
    for e in range(RHS):
        for j in reversed(range(n)):
            value = target[j, e]
            for later in range(j + 1, n):
                value = value - upper[j, later] * coef[later, e]
            coef[j, e] = value * recips[j]
    return coef


def final_kernel(
    X, Y, scale, gathered, rhs, basis, ortho, triangle, update,
    B, O, W, in_sems, out_sems,
):
    loads = [
        pltpu.make_async_copy(rhs, B.at[pl.ds(0, 2)], in_sems.at[0]),
        pltpu.make_async_copy(basis, B.at[pl.ds(2, 8)], in_sems.at[1]),
    ]
    for copy in loads:
        copy.start()
    R = merged_factor(gathered[...])
    row = lax.broadcasted_iota(jnp.int32, (16, 128), 0)
    lane = lax.broadcasted_iota(jnp.int32, (16, 128), 1)
    tri = jnp.zeros((16, 128), F32)
    for (i, j), value in R.items():
        tri = jnp.where((row == i) & (lane == j), value * (1.0 / scale), tri)
    triangle[...] = tri[:COLS, :COLS]
    T = inverse(R)
    weights = {}
    for n, ((i, j), value) in enumerate(T.items()):
        weights[i, j] = n
        W[n] = jnp.broadcast_to(value * scale, (8, 128))
    coef = least_squares(R)
    base = len(weights)
    for n, ((k, e), value) in enumerate(coef.items()):
        weights[k, COLS + e] = base + n
        W[base + n] = jnp.broadcast_to(value, (8, 128))
    for copy in loads:
        copy.wait()

    CH = 32
    XB = 2
    outs = []
    for block in range(X // XB):

        def rows(i, carry, block=block):
            x = block * XB + i
            for at in range(0, Y, CH):
                b = [B[k, x, pl.ds(at, CH), :] for k in range(COLS)]
                for j in range(COLS + RHS):
                    value = None
                    for k in range(j + 1 if j < COLS else RHS * S):
                        w = jnp.concatenate([W[weights[k, j]]] * (CH // 8), axis=0)
                        value = w * b[k] if value is None else value + w * b[k]
                    O[j, x, pl.ds(at, CH), :] = value
            return carry

        lax.fori_loop(0, XB, rows, 0)
        here = pl.ds(block * XB, XB)
        for copy in (
            pltpu.make_async_copy(
                O.at[pl.ds(0, COLS), here], ortho.at[:, here], out_sems.at[2 * block]
            ),
            pltpu.make_async_copy(
                O.at[pl.ds(COLS, RHS), here], update.at[:, here], out_sems.at[2 * block + 1]
            ),
        ):
            copy.start()
            outs.append(copy)
    for copy in outs:
        copy.wait()


ANY = pl.BlockSpec(memory_space=pl.ANY)
VMEM = pl.BlockSpec(memory_space=pltpu.VMEM)
PARAMS = pltpu.CompilerParams(vmem_limit_bytes=VMEM_LIMIT)


def body(right_sides, diagonal, velocity):
    _, X, Y, Z = right_sides.shape
    nx, ny = lax.axis_size("gx"), lax.axis_size("gy")
    devices = nx * ny
    scale = math.sqrt(X * Y * Z * devices)
    shape = lambda *s: jax.ShapeDtypeStruct(s, F32)
    inputs = (right_sides, velocity, diagonal)

    x_low, x_high = pl.pallas_call(
        functools.partial(pack_x_kernel, X),
        out_shape=(shape(20, Y, Z),) * 2,
        in_specs=[ANY] * 3,
        out_specs=[VMEM] * 2,
        scratch_shapes=[pltpu.SemaphoreType.DMA((12,))],
        compiler_params=PARAMS,
        name="pack_x",
    )(*inputs)

    def shift(value, dx, dy):
        pairs = []
        for i in range(nx):
            for j in range(ny):
                if 0 <= i + dx < nx and 0 <= j + dy < ny:
                    pairs.append((i * ny + j, (i + dx) * ny + j + dy))
        return lax.ppermute(value, ("gx", "gy"), pairs)

    xl = shift(x_high, 1, 0)
    xh = shift(x_low, -1, 0)
    y_low, y_high, c_ll, c_lh, c_hl, c_hh = pl.pallas_call(
        functools.partial(pack_y_kernel, X, Y),
        out_shape=(shape(6, X, 8, Z),) * 2 + (shape(CORNER_ROWS, Z),) * 4,
        in_specs=[ANY] * 3,
        out_specs=[VMEM] * 6,
        scratch_shapes=[pltpu.VMEM((4, 6, 3, 8, Z), F32), pltpu.SemaphoreType.DMA((18,))],
        compiler_params=PARAMS,
        name="pack_y",
    )(*inputs)
    yl = shift(y_high, 0, 1)
    yh = shift(y_low, 0, -1)
    corners = (shift(c_hh, 1, 1), shift(c_hl, 1, -1), shift(c_lh, -1, 1), shift(c_ll, -1, -1))

    XE, YE = X + 8, Y + 2 * YP
    basis, packed = pl.pallas_call(
        functools.partial(main_kernel, X, Y),
        out_shape=(shape(8, X, Y, Z), shape(devices, 128)),
        in_specs=[ANY] * 7 + [VMEM] * 4,
        out_specs=[ANY, VMEM],
        scratch_shapes=[
            pltpu.VMEM((S, RHS, XE, YE, Z), F32),
            pltpu.VMEM((RHS, X, Y, Z), F32),
            pltpu.VMEM((4, XE, YE, Z), F32),
            pltpu.VMEM((6, XE, YE, Z), F32),
            pltpu.VMEM((COLS - 1, X, Y, Z), F32),
            pltpu.SemaphoreType.DMA((19,)),
            pltpu.SemaphoreType.DMA((4,)),
        ],
        compiler_params=PARAMS,
        name="powers",
    )(*inputs, xl, xh, yl, yh, *corners)

    gathered = lax.all_to_all(packed, ("gx", "gy"), 0, 0, tiled=True)

    ortho, triangle, update = pl.pallas_call(
        functools.partial(final_kernel, X, Y, scale),
        out_shape=(shape(COLS, X, Y, Z), shape(COLS, COLS), shape(RHS, X, Y, Z)),
        in_specs=[VMEM, ANY, ANY],
        out_specs=[ANY, VMEM, ANY],
        scratch_shapes=[
            pltpu.VMEM((COLS, X, Y, Z), F32),
            pltpu.VMEM((COLS + RHS, X, Y, Z), F32),
            pltpu.VMEM((71, 8, 128), F32),
            pltpu.SemaphoreType.DMA((2,)),
            pltpu.SemaphoreType.DMA((X,)),
        ],
        compiler_params=PARAMS,
        name="combine",
    )(gathered, right_sides, basis)
    return ortho, triangle, update


def solution(mesh):
    return jax.shard_map(
        body,
        mesh=mesh,
        in_specs=(P(None, "gx", "gy", None), P("gx", "gy", None), P(None, "gx", "gy", None)),
        out_specs=(P(None, "gx", "gy", None), P(), P(None, "gx", "gy", None)),
        check_vma=False,
    )
```

time: 788 us -> 102 us (0.13); the launches traced: 773 us -> 101 us
  other arithmetic: 346 us -> 0 us
  local copies, waits for them, and re-layouts: 205 us -> 1.87 us
  between operations: 69.8 us -> 0.78 us
  blocking collectives: 71.5 us -> 30.8 us
  Pallas kernels: 0 us -> 30.9 us
  starting transfers between devices: 46.6 us -> 22.8 us
  matrix products: 16.3 us -> 0 us
    reduce_sum x52 -> x0, other arithmetic: 181 us -> none  [the longest x37 148 us: orthonormalize(): weight = jnp.sum(vectors[earlier] * current)]
    div x6 -> x0, other arithmetic: 119 us -> none  [the longest x4 96.7 us: orthonormalize(): vectors.append(current / length)]
    scatter x143 -> x0, local copies, waits for them, and re-layouts: 107 us -> none  [the longest x115 103 us: orthonormalize(): factor = factor.at[earlier, column].set(weight)]
    all_gather x1 -> x0, blocking collectives: 71.5 us -> none  [body(): every = lax.all_gather(local_r[None], ('gx', 'gy'), axis=0, tiled=True)]
    another operation x39 -> x0, local copies, waits for them, and re-layouts: 69.9 us -> none
    pallas_call x0 -> x4, Pallas kernels: none -> 30.9 us  [the longest x1 18.7 us: body(): pl.pallas_call(functools.partial(main_kernel, X, Y), out_shape=(shape(8,...]
    all_to_all x0 -> x1, blocking collectives: none -> 30.8 us  [body(): gathered = lax.all_to_all(packed, ('gx', 'gy'), 0, 0, tiled=True)]
    ppermute x16 -> x8, starting transfers between devices: 46.6 us -> 22.8 us  [shift(): return lax.ppermute(value, ('gx', 'gy'), pairs)]
  transfers between devices with their start and end apart: 16 -> 8, of which waited for: 5 -> 4; matrix products, arithmetic and copies ran while one was open for 3% -> 0% of each run, Pallas kernels for 0% -> 2%
where the time goes in v1:
time: 102 us; the launch traced here: 101 us
  Pallas kernels  30.9 us (30%)
  blocking collectives  30.8 us (30%)
  starting transfers between devices  22.8 us (22%)
  waiting for transfers between devices  14.3 us (14%)
  local copies, waits for them, and re-layouts  1.87 us (2%)
    all_to_all x1, blocking collectives, body(): gathered = lax.all_to_all(packed, ('gx', 'gy'), 0, 0, tiled=True)  30.8 us
    ppermute x8, starting transfers between devices, shift(): return lax.ppermute(value, ('gx', 'gy'), pairs)  22.8 us
    pallas_call x1, Pallas kernels, body(): pl.pallas_call(functools.partial(main_kernel, X, Y), out_shape=(shape(8,...  18.7 us
    ppermute x8, waiting for transfers between devices, shift(): return lax.ppermute(value, ('gx', 'gy'), pairs)  14.3 us
    pallas_call x1, Pallas kernels, body(): pl.pallas_call(functools.partial(final_kernel, X, Y, scale), out_shape=(s...  7.36 us
    pallas_call x1, Pallas kernels, body(): pl.pallas_call(functools.partial(pack_x_kernel, X), out_shape=(shape(20,...  2.52 us
    pallas_call x1, Pallas kernels, body(): pl.pallas_call(functools.partial(pack_y_kernel, X, Y), out_shape=(shape(6...  2.29 us
  transfers between devices with their start and end apart: 8, of which 4 were waited for; matrix products, arithmetic and copies ran while one was open for 0% of the time, Pallas kernels for 2%

profile of v1, /device:TPU:1, one launch (start us, length us, event | category | flops | bytes accessed | tf_op | source)
XLA Modules:
  0.0 101.5 jit_solution(8725591411602653901)
XLA Ops:
  0.6 2.5 %pack_x.1 = (f32[20,64,128]{2,1,0:T(8,128)}, f32[20,64,128]{2,1,0:T(8,128)}) custom-call(f32[2,16,64,128]{3,2,1,0:T(8,128)} %rhs.7, f32[3,16,64,128]{3,2,1,0:T(8,128)} %vel.5, f32[16,64,128]{2,1,0:T(8,128)} %diag.5), custom_call_target="tpu_custom_call" | custom-call | tf_op jit(solution)/shard_map/pack_x/pallas_call | solution.py:397
  3.2 4.4 %collective-permute-start = (f32[20,64,128]{2,1,0:T(8,128)}, f32[20,64,128]{2,1,0:T(8,128)S(1)}, u32[]{:S(2)}, u32[]{:S(2)}) collective-permute-start(f32[20,64,128]{2,1,0:T(8,128)} %get-tuple-element.13), channel_id=1, source_target_pairs={{0,8},{1,9},{2,10},{3,11},{4,12},{5,13},{6,14},{7,15},{8,16},{9,17... | collective-permute-start | bytes 1966088 | tf_op jit(solution)/shard_map/ppermute | solution.py:413
  7.6 1.3 %collective-permute-start.1 = (f32[20,64,128]{2,1,0:T(8,128)}, f32[20,64,128]{2,1,0:T(8,128)S(1)}, u32[]{:S(2)}, u32[]{:S(2)}) collective-permute-start(f32[20,64,128]{2,1,0:T(8,128)} %get-tuple-element.14), channel_id=1, source_target_pairs={{8,0},{9,1},{10,2},{11,3},{12,4},{13,5},{14,6},{15,7},{16,8},{17,9... | collective-permute-start | bytes 1966088 | tf_op jit(solution)/shard_map/ppermute | solution.py:413
  8.9 2.3 %pack_y.1 = (f32[6,16,8,128]{3,2,1,0:T(8,128)}, f32[6,16,8,128]{3,2,1,0:T(8,128)}, f32[24,128]{1,0:T(8,128)}, f32[24,128]{1,0:T(8,128)}, f32[24,128]{1,0:T(8,128)}, /*index=5*/f32[24,128]{1,0:T(8,128)}) custom-call(f32[2,16,64,128]{3,2,1,0:T(8,128)} %rhs.7, f32[3,16,64,128]{3,2,1,0:T(8,128)} %vel.5, f32[16,64,128]{2,1,0:T(8,128)} %diag.5), custom_call_target="tpu_custom_call" | custom-call | tf_op jit(solution)/shard_map/pack_y/pallas_call | solution.py:417
  11.2 4.0 %collective-permute-start.2 = (f32[6,16,8,128]{3,2,1,0:T(8,128)}, f32[6,16,8,128]{3,2,1,0:T(8,128)S(1)}, u32[]{:S(2)}, u32[]{:S(2)}) collective-permute-start(f32[6,16,8,128]{3,2,1,0:T(8,128)} %get-tuple-element.15), channel_id=1, source_target_pairs={{0,1},{1,2},{2,3},{3,4},{4,5},{5,6},{6,7},{8,9},{9,10},{10,11},{11... | collective-permute-start | bytes 1179656 | tf_op jit(solution)/shard_map/ppermute | solution.py:413
  15.2 1.9 %collective-permute-start.3 = (f32[6,16,8,128]{3,2,1,0:T(8,128)}, f32[6,16,8,128]{3,2,1,0:T(8,128)S(1)}, u32[]{:S(2)}, u32[]{:S(2)}) collective-permute-start(f32[6,16,8,128]{3,2,1,0:T(8,128)} %get-tuple-element.16), channel_id=1, source_target_pairs={{1,0},{2,1},{3,2},{4,3},{5,4},{6,5},{7,6},{9,8},{10,9},{11,10},{12... | collective-permute-start | bytes 1179656 | tf_op jit(solution)/shard_map/ppermute | solution.py:413
  17.2 5.7 %collective-permute-start.4 = (f32[24,128]{1,0:T(8,128)}, f32[24,128]{1,0:T(8,128)S(1)}, u32[]{:S(2)}, u32[]{:S(2)}) collective-permute-start(f32[24,128]{1,0:T(8,128)} %get-tuple-element.17), channel_id=1, source_target_pairs={{0,9},{1,10},{2,11},{3,12},{4,13},{5,14},{6,15},{8,17},{9,18},{10,... | collective-permute-start | bytes 36872 | tf_op jit(solution)/shard_map/ppermute | solution.py:413
  22.9 1.0 %collective-permute-done.4.c_ll = f32[24,128]{1,0:T(8,128)S(1)} collective-permute-done((f32[24,128]{1,0:T(8,128)}, f32[24,128]{1,0:T(8,128)S(1)}, u32[]{:S(2)}, u32[]{:S(2)}) %collective-permute-start.4) | collective-permute-done | bytes 12320 | tf_op jit(solution)/shard_map/ppermute | solution.py:413
  23.9 2.9 %collective-permute-start.5 = (f32[24,128]{1,0:T(8,128)}, f32[24,128]{1,0:T(8,128)S(1)}, u32[]{:S(2)}, u32[]{:S(2)}) collective-permute-start(f32[24,128]{1,0:T(8,128)} %get-tuple-element.18), channel_id=1, source_target_pairs={{1,8},{2,9},{3,10},{4,11},{5,12},{6,13},{7,14},{9,16},{10,17},{11,... | collective-permute-start | bytes 36872 | tf_op jit(solution)/shard_map/ppermute | solution.py:413
  26.8 1.0 %collective-permute-done.5.c_lh = f32[24,128]{1,0:T(8,128)S(1)} collective-permute-done((f32[24,128]{1,0:T(8,128)}, f32[24,128]{1,0:T(8,128)S(1)}, u32[]{:S(2)}, u32[]{:S(2)}) %collective-permute-start.5) | collective-permute-done | bytes 12320 | tf_op jit(solution)/shard_map/ppermute | solution.py:413
  27.8 1.3 %collective-permute-start.6 = (f32[24,128]{1,0:T(8,128)}, f32[24,128]{1,0:T(8,128)S(1)}, u32[]{:S(2)}, u32[]{:S(2)}) collective-permute-start(f32[24,128]{1,0:T(8,128)} %get-tuple-element.19), channel_id=1, source_target_pairs={{8,1},{9,2},{10,3},{11,4},{12,5},{13,6},{14,7},{16,9},{17,10},{18,... | collective-permute-start | bytes 36872 | tf_op jit(solution)/shard_map/ppermute | solution.py:413
  29.1 3.9 %collective-permute-done.6.c_hl = f32[24,128]{1,0:T(8,128)S(1)} collective-permute-done((f32[24,128]{1,0:T(8,128)}, f32[24,128]{1,0:T(8,128)S(1)}, u32[]{:S(2)}, u32[]{:S(2)}) %collective-permute-start.6) | collective-permute-done | bytes 12320 | tf_op jit(solution)/shard_map/ppermute | solution.py:413
  33.1 1.3 %collective-permute-start.7 = (f32[24,128]{1,0:T(8,128)}, f32[24,128]{1,0:T(8,128)S(1)}, u32[]{:S(2)}, u32[]{:S(2)}) collective-permute-start(f32[24,128]{1,0:T(8,128)} %get-tuple-element.20), channel_id=1, source_target_pairs={{9,0},{10,1},{11,2},{12,3},{13,4},{14,5},{15,6},{17,8},{18,9},{19,... | collective-permute-start | bytes 36872 | tf_op jit(solution)/shard_map/ppermute | solution.py:413
  34.3 8.3 %collective-permute-done.7.c_hh = f32[24,128]{1,0:T(8,128)S(1)} collective-permute-done((f32[24,128]{1,0:T(8,128)}, f32[24,128]{1,0:T(8,128)S(1)}, u32[]{:S(2)}, u32[]{:S(2)}) %collective-permute-start.7) | collective-permute-done | bytes 12320 | tf_op jit(solution)/shard_map/ppermute | solution.py:413
  42.7 0.0 copy-start
  42.7 0.0 collective-permute-done.1.xh
  42.7 0.5 copy-done.7
  43.2 0.2 copy-done.2
  43.4 0.1 copy-done.3
  43.5 0.2 copy-done
  43.7 0.8 copy-done.1
  44.6 18.7 %powers.1 = (f32[8,16,64,128]{3,2,1,0:T(8,128)}, f32[256,128]{1,0:T(8,128)}) custom-call(f32[2,16,64,128]{3,2,1,0:T(8,128)} %rhs.7, f32[3,16,64,128]{3,2,1,0:T(8,128)} %vel.5, f32[16,64,128]{2,1,0:T(8,128)} %diag.5, f32[20,64,128]{2,1,0:T(8,128)} %copy-done, f32[20,64,128]{2,1,0:T(8,128)} %copy-done.1, f32[6,16,8,128]{3,2,1,0:T(8,128)} %copy-done.2, ...), custom_call_target="tpu_custom_call" | custom-call | tf_op jit(solution)/shard_map/powers/pallas_call | solution.py:431
  63.3 30.8 %all_to_all.11 = f32[256,1,128]{2,1,0:T(1,128)} all-to-all(f32[256,1,128]{2,1,0:T(1,128)} %bitcast.5), channel_id=1, replica_groups=mesh['gx'=32,'gy'=8] {'gx','gy'}, dimensions={0} | all-to-all | bytes 262144 | tf_op jit(solution)/shard_map/all_to_all | solution.py:449
  94.1 7.4 %combine.1 = (f32[10,16,64,128]{3,2,1,0:T(8,128)}, f32[10,10]{1,0:T(8,128)}, f32[2,16,64,128]{3,2,1,0:T(8,128)}) custom-call(f32[256,128]{1,0:T(8,128)} %bitcast.4, f32[2,16,64,128]{3,2,1,0:T(8,128)} %rhs.7, f32[8,16,64,128]{3,2,1,0:T(8,128)} %get-tuple-element.22.basis), custom_call_target="tpu_custom_call" | custom-call | tf_op jit(solution)/shard_map/combine/pallas_call | solution.py:451
  (13 shorter events, 0.0 us)
Async XLA Ops:
  3.2 39.5 %collective-permute-start = (f32[20,64,128]{2,1,0:T(8,128)}, f32[20,64,128]{2,1,0:T(8,128)S(1)}, u32[]{:S(2)}, u32[]{:S(2)}) collective-permute-start(f32[20,64,128]{2,1,0:T(8,128)} %get-tuple-element.13), channel_id=1, source_target_pairs={{0,8},{1,9},{2,10},{3,11},{4,12},{5,13},{6,14},{7,15},{8,16},{9,17... | collective-permute-start | bytes 1966088 | tf_op jit(solution)/shard_map/ppermute | solution.py:413
  7.6 35.1 %collective-permute-start.1 = (f32[20,64,128]{2,1,0:T(8,128)}, f32[20,64,128]{2,1,0:T(8,128)S(1)}, u32[]{:S(2)}, u32[]{:S(2)}) collective-permute-start(f32[20,64,128]{2,1,0:T(8,128)} %get-tuple-element.14), channel_id=1, source_target_pairs={{8,0},{9,1},{10,2},{11,3},{12,4},{13,5},{14,6},{15,7},{16,8},{17,9... | collective-permute-start | bytes 1966088 | tf_op jit(solution)/shard_map/ppermute | solution.py:413
  11.2 31.5 %collective-permute-start.2 = (f32[6,16,8,128]{3,2,1,0:T(8,128)}, f32[6,16,8,128]{3,2,1,0:T(8,128)S(1)}, u32[]{:S(2)}, u32[]{:S(2)}) collective-permute-start(f32[6,16,8,128]{3,2,1,0:T(8,128)} %get-tuple-element.15), channel_id=1, source_target_pairs={{0,1},{1,2},{2,3},{3,4},{4,5},{5,6},{6,7},{8,9},{9,10},{10,11},{11... | collective-permute-start | bytes 1179656 | tf_op jit(solution)/shard_map/ppermute | solution.py:413
  15.2 27.4 %collective-permute-start.3 = (f32[6,16,8,128]{3,2,1,0:T(8,128)}, f32[6,16,8,128]{3,2,1,0:T(8,128)S(1)}, u32[]{:S(2)}, u32[]{:S(2)}) collective-permute-start(f32[6,16,8,128]{3,2,1,0:T(8,128)} %get-tuple-element.16), channel_id=1, source_target_pairs={{1,0},{2,1},{3,2},{4,3},{5,4},{6,5},{7,6},{9,8},{10,9},{11,10},{12... | collective-permute-start | bytes 1179656 | tf_op jit(solution)/shard_map/ppermute | solution.py:413
  17.2 6.7 %collective-permute-start.4 = (f32[24,128]{1,0:T(8,128)}, f32[24,128]{1,0:T(8,128)S(1)}, u32[]{:S(2)}, u32[]{:S(2)}) collective-permute-start(f32[24,128]{1,0:T(8,128)} %get-tuple-element.17), channel_id=1, source_target_pairs={{0,9},{1,10},{2,11},{3,12},{4,13},{5,14},{6,15},{8,17},{9,18},{10,... | collective-permute-start | bytes 36872 | tf_op jit(solution)/shard_map/ppermute | solution.py:413
  23.9 18.8 %copy-start.4 = (f32[24,128]{1,0:T(8,128)}, f32[24,128]{1,0:T(8,128)S(1)}, u32[]{:S(2)}) copy-start(f32[24,128]{1,0:T(8,128)S(1)} %collective-permute-done.4.c_ll) | copy-start | bytes 36868
  23.9 3.9 %collective-permute-start.5 = (f32[24,128]{1,0:T(8,128)}, f32[24,128]{1,0:T(8,128)S(1)}, u32[]{:S(2)}, u32[]{:S(2)}) collective-permute-start(f32[24,128]{1,0:T(8,128)} %get-tuple-element.18), channel_id=1, source_target_pairs={{1,8},{2,9},{3,10},{4,11},{5,12},{6,13},{7,14},{9,16},{10,17},{11,... | collective-permute-start | bytes 36872 | tf_op jit(solution)/shard_map/ppermute | solution.py:413
  27.8 14.9 %copy-start.5 = (f32[24,128]{1,0:T(8,128)}, f32[24,128]{1,0:T(8,128)S(1)}, u32[]{:S(2)}) copy-start(f32[24,128]{1,0:T(8,128)S(1)} %collective-permute-done.5.c_lh) | copy-start | bytes 36868
  27.8 5.2 %collective-permute-start.6 = (f32[24,128]{1,0:T(8,128)}, f32[24,128]{1,0:T(8,128)S(1)}, u32[]{:S(2)}, u32[]{:S(2)}) collective-permute-start(f32[24,128]{1,0:T(8,128)} %get-tuple-element.19), channel_id=1, source_target_pairs={{8,1},{9,2},{10,3},{11,4},{12,5},{13,6},{14,7},{16,9},{17,10},{18,... | collective-permute-start | bytes 36872 | tf_op jit(solution)/shard_map/ppermute | solution.py:413
  33.0 9.7 %copy-start.6 = (f32[24,128]{1,0:T(8,128)}, f32[24,128]{1,0:T(8,128)S(1)}, u32[]{:S(2)}) copy-start(f32[24,128]{1,0:T(8,128)S(1)} %collective-permute-done.6.c_hl) | copy-start | bytes 36868
  33.1 9.6 %collective-permute-start.7 = (f32[24,128]{1,0:T(8,128)}, f32[24,128]{1,0:T(8,128)S(1)}, u32[]{:S(2)}, u32[]{:S(2)}) collective-permute-start(f32[24,128]{1,0:T(8,128)} %get-tuple-element.20), channel_id=1, source_target_pairs={{9,0},{10,1},{11,2},{12,3},{13,4},{14,5},{15,6},{17,8},{18,9},{19,... | collective-permute-start | bytes 36872 | tf_op jit(solution)/shard_map/ppermute | solution.py:413
  42.6 0.6 copy-start.7
  42.6 0.8 copy-start.2
  42.7 0.9 copy-start.3
  42.7 1.1 %copy-start = (f32[20,64,128]{2,1,0:T(8,128)}, f32[20,64,128]{2,1,0:T(8,128)S(1)}, u32[]{:S(2)}) copy-start(f32[20,64,128]{2,1,0:T(8,128)S(1)} %collective-permute-done.xl) | copy-start | bytes 1966084
  43.7 0.8 copy-start.1

commit v2 on v1

v2 whole, which is shorter than its diff:
```python
import functools
import math

import jax
import jax.numpy as jnp
from jax import lax
from jax.experimental import pallas as pl
from jax.experimental.pallas import tpu as pltpu
from jax.sharding import PartitionSpec as P

S = 4
RHS = 2
COLS = 10
YP = 16

F32 = jnp.float32
FIELD_CORNER = [(dx, dy) for dx in (1, 2, 3) for dy in (1, 2, 3) if dx + dy <= 4]
COEF_CORNER = [(dx, dy) for dx in (1, 2) for dy in (1, 2) if dx + dy <= 3]
CORNER_ROWS = RHS * len(FIELD_CORNER) + 4 * len(COEF_CORNER)


def slot(i, k):
    return (8 * k if k < 8 else 64 + 16 * (k - 8)) + i


def run_copies(copies):
    for copy in copies:
        copy.start()
    for copy in copies:
        copy.wait()


def pack_x_kernel(X, rhs, vel, diag, low, high, sems):
    copies = []
    for out, at4, at3 in ((high, X - 4, X - 3), (low, 0, 0)):
        for f in range(RHS):
            copies.append((rhs.at[f, pl.ds(at4, 4)], out.at[pl.ds(4 * f, 4)]))
        for c in range(3):
            copies.append((vel.at[c, pl.ds(at3, 3)], out.at[pl.ds(8 + 3 * c, 3)]))
        copies.append((diag.at[pl.ds(at3, 3)], out.at[pl.ds(17, 3)]))
    run_copies([pltpu.make_async_copy(s, d, sems.at[i]) for i, (s, d) in enumerate(copies)])


def pack_y_kernel(Y, rhs, vel, diag, low, high, sems):
    copies = []
    for out, at in ((high, Y - 8), (low, 0)):
        copies.append((rhs.at[:, :, pl.ds(at, 8)], out.at[pl.ds(0, 2)]))
        copies.append((vel.at[:, :, pl.ds(at, 8)], out.at[pl.ds(2, 3)]))
        copies.append((diag.at[:, pl.ds(at, 8)], out.at[5]))
    run_copies([pltpu.make_async_copy(s, d, sems.at[i]) for i, (s, d) in enumerate(copies)])


def load_kernel(X, Y, rhs, vel, diag, V, U, sems):
    own_x, own_y = pl.ds(4, X), pl.ds(YP, Y)
    copies = [
        (rhs, V.at[0, :, own_x, own_y]),
        (vel, U.at[pl.ds(0, 3), own_x, own_y]),
        (diag, U.at[3, own_x, own_y]),
    ]
    run_copies([pltpu.make_async_copy(s, d, sems.at[i]) for i, (s, d) in enumerate(copies)])


def corner_cells(X, Y, low, own):
    cells = []
    for y_low in (True, False):
        for f in range(6):
            for dx, dy in FIELD_CORNER if f < 2 else COEF_CORNER:
                if own:
                    x = 3 + dx if low else X + 4 - dx
                else:
                    x = 4 - dx if low else X + 3 + dx
                cells.append((f, x, YP - dy if y_low else YP + Y - 1 + dy))
    return cells


def place_y_kernel(X, Y, yl, yh, V_in, U_in, V, U, low, high):
    for got, at in ((yl, YP - 8), (yh, YP + Y)):
        for x in range(X):
            for f in range(2):
                V[0, f, 4 + x, at : at + 8, :] = got[f, x]
            for c in range(4):
                U[c, 4 + x, at : at + 8, :] = got[2 + c, x]
    for out, is_low in ((low, True), (high, False)):
        for row, (f, x, y) in enumerate(corner_cells(X, Y, is_low, True)):
            out[row : row + 1, :] = (
                V[0, f, x, y : y + 1, :] if f < 2 else U[f - 2, x, y : y + 1, :]
            )


def total(x):
    return jnp.sum(jnp.sum(x, axis=0, keepdims=True), axis=1, keepdims=True)


def fold8(x):
    rows = x.shape[0]
    parts = [x[8 * i : 8 * i + 8] for i in range(rows // 8)]
    while len(parts) > 1:
        parts = [a + b for a, b in zip(parts[::2], parts[1::2])] + (
            [parts[-1]] if len(parts) % 2 else []
        )
    return parts[0]


def coefficient_rows(X, Y, U, A, rows):
    gx, gy = lax.axis_index("gx"), lax.axis_index("gy")
    nx, ny = lax.axis_size("gx"), lax.axis_size("gy")
    WIDE = Y + 16
    inner = pl.ds(YP - 8, WIDE)
    yi = lax.broadcasted_iota(jnp.int32, (WIDE, 128), 0)
    zi = lax.broadcasted_iota(jnp.int32, (WIDE, 128), 1)
    y_in = ((yi >= 8) | (gy > 0)) & ((yi < Y + 8) | (gy < ny - 1))

    def one(x):
        x_in = ((x >= 4) | (gx > 0)) & ((x < X + 4) | (gx < nx - 1))
        g = jnp.where(y_in & x_in, 1.0 / (6.0 + U[3, x, inner, :]), 0.0)
        for c in range(3):
            ug = U[c, x, inner, :] * g
            plus, minus = g + ug, g - ug
            if c == 2:
                plus = jnp.where(zi == 0, 0.0, plus)
                minus = jnp.where(zi == 127, 0.0, minus)
            A[2 * c, x, inner, :] = plus
            A[2 * c + 1, x, inner, :] = minus

    for_rows(rows, one, 2)


def for_rows(rows, body, unroll):
    def run(i, carry):
        for first, last in rows:
            body(first + i)
        return carry

    lax.fori_loop(0, rows[0][1] - rows[0][0], run, 0, unroll=unroll)


def power_rows(Y, V, V4, A, k, rows, unroll):
    begin, size = (YP, Y) if k == S else (YP - 8, Y + 16)
    here = pl.ds(begin, size)

    def one(x):
        a = [A[c, x, here, :] for c in range(6)]
        for f in range(RHS):
            centre = V[k - 1, f, x, here, :]
            value = a[4] * pltpu.roll(centre, 1, 1) + a[5] * pltpu.roll(centre, 127, 1)
            value += a[0] * V[k - 1, f, x - 1, here, :] + a[1] * V[k - 1, f, x + 1, here, :]
            value += a[2] * V[k - 1, f, x, pl.ds(begin - 1, size), :]
            value += a[3] * V[k - 1, f, x, pl.ds(begin + 1, size), :]
            if k == S:
                V4[f, x - 4] = value
            else:
                V[k, f, x, here, :] = value

    for_rows(rows, one, unroll)


def basis_rows(V, V4, k, x, at, size):
    if k >= RHS * S:
        return V4[k - RHS * S, x, pl.ds(at, size), :]
    return V[k // RHS, k % RHS, x + 4, pl.ds(YP + at, size), :]


def local_factor(Y, V, V4, Q, rows):
    CH = 32
    zero = jnp.zeros((8, 128), F32)

    def first_dots(i, accs):
        accs = list(accs)
        for first, _ in rows:
            x = first + i
            for at in range(0, Y, CH):
                q = basis_rows(V, V4, 0, x, at, CH)
                for k in range(COLS):
                    accs[k] = accs[k] + fold8(q * basis_rows(V, V4, k, x, at, CH))
        return tuple(accs)

    count = rows[0][1] - rows[0][0]
    accs = lax.fori_loop(0, count, first_dots, (zero,) * COLS)
    lane = lax.broadcasted_iota(jnp.int32, (1, 128), 1)
    line = jnp.zeros((1, 128), F32)
    for j in range(COLS):
        dots = [total(a) for a in accs]
        live = dots[0] > 0.0
        length = jnp.sqrt(jnp.where(live, dots[0], 1.0))
        inv = jnp.where(live, 1.0 / length, 0.0)
        for k in range(j, COLS):
            line = jnp.where(lane == slot(j, k), dots[k - j] * inv, line)
        if j == COLS - 1:
            return line
        inv2 = inv * inv
        alphas = [jnp.broadcast_to(d * inv2, (8, 128)) for d in dots[1:]]

        def get(k, x, at, size, j=j):
            if j == 0 or k == 0:
                return basis_rows(V, V4, k, x, at, size)
            return Q[k - 1, x, pl.ds(at, size), :]

        def sweep(i, accs, j=j, get=get, alphas=alphas):
            accs = list(accs)
            for first, _ in rows:
                x = first + i
                for at in range(0, Y, CH):
                    q = get(j, x, at, CH)
                    after = None
                    for k in range(j + 1, COLS):
                        alpha = jnp.concatenate([alphas[k - j - 1]] * (CH // 8), axis=0)
                        value = get(k, x, at, CH) - alpha * q
                        Q[k - 1, x, pl.ds(at, CH), :] = value
                        if k == j + 1:
                            after = value
                        accs[k - j - 1] = accs[k - j - 1] + fold8(after * value)
            return tuple(accs)

        accs = lax.fori_loop(0, count, sweep, (zero,) * (COLS - 1 - j))


def inner_kernel(X, Y, V_in, U, V, V4, A, line, Q):
    coefficient_rows(X, Y, U, A, [(4, X + 4)])
    for k in range(1, S + 1):
        power_rows(Y, V, V4, A, k, [(4 + k, X + 4 - k)], 4)
    line[...] = local_factor(Y, V, V4, Q, [(4, X // 2), (X // 2, X - 4)])


def outer_kernel(X, Y, xl, xh, cl, ch, inner_line, V_in, V4_in, A_in, U_in, V, V4, A, U, packed, Q):
    own_y = slice(YP, YP + Y)
    for got, at4, at3 in ((xl, 0, 1), (xh, X + 4, X + 4)):
        for i in range(4):
            for f in range(RHS):
                V[0, f, at4 + i, own_y, :] = got[4 * f + i]
        for i in range(3):
            for c in range(4):
                U[c, at3 + i, own_y, :] = got[8 + 3 * c + i]
    for got, is_low in ((cl, True), (ch, False)):
        for row, (f, x, y) in enumerate(corner_cells(X, Y, is_low, False)):
            if f < 2:
                V[0, f, x, y : y + 1, :] = got[row : row + 1, :]
            else:
                U[f - 2, x, y : y + 1, :] = got[row : row + 1, :]
    coefficient_rows(X, Y, U, A, [(1, 4), (X + 4, X + 7)])
    for k in range(1, S + 1):
        power_rows(Y, V, V4, A, k, [(k, k + 4), (X + 4 - k, X + 8 - k)], 2)
    line = local_factor(Y, V, V4, Q, [(0, 4), (X - 4, X)])
    row = lax.broadcasted_iota(jnp.int32, (8, 128), 0)
    both = jnp.where(row % 2 == 0, inner_line[...], line)
    packed[...] = jnp.concatenate([both] * (packed.shape[0] // 8), axis=0)


def fold_lanes(x):
    parts = [x[:, i : i + 128] for i in range(0, x.shape[1], 128)]
    return functools.reduce(lambda a, b: a + b, parts)


def merged_factor(gathered):
    g = gathered.T
    cols = []
    for k in range(COLS):
        if k < 8:
            cols.append([g[8 * k : 8 * k + 8]])
        else:
            at = 64 + 16 * (k - 8)
            cols.append([g[at : at + 8], g[at + 8 : at + 16]])
    R = {}
    for j in range(COLS):
        dots = []
        for k in range(j, COLS):
            p = fold_lanes(cols[j][0] * cols[k][0])
            if j >= 8:
                p = p + fold_lanes(cols[j][1] * cols[k][1])
            dots.append(total(p))
        inv = 1.0 / jnp.sqrt(dots[0])
        for k in range(j, COLS):
            R[j, k] = dots[k - j] * inv
        inv2 = inv * inv
        for k in range(j + 1, COLS):
            alpha = dots[k - j] * inv2
            for part in range(len(cols[j])):
                cols[k][part] = cols[k][part] - alpha * cols[j][part]
    return R


def inverse(R):
    T = {}
    recip = [1.0 / R[j, j] for j in range(COLS)]
    for j in range(COLS):
        T[j, j] = recip[j]
        for i in range(j):
            s = T[i, i] * R[i, j]
            for k in range(i + 1, j):
                s = s + T[i, k] * R[k, j]
            T[i, j] = -s * recip[j]
    return T


def least_squares(R):
    n = RHS * S
    cols = []
    for c in range(n):
        col = []
        for i in range(c + RHS + 1):
            minus = R[i, c + RHS]
            col.append(R[i, c] - minus if i <= c else -minus)
        cols.append(col)
    upper, target = {}, {}
    recips = []

    def dot(a, b):
        terms = [x * y for x, y in zip(a, b)]
        while len(terms) > 1:
            terms = [x + y for x, y in zip(terms[::2], terms[1::2])] + (
                [terms[-1]] if len(terms) % 2 else []
            )
        return terms[0]

    for j in range(n):
        inv = 1.0 / jnp.sqrt(dot(cols[j], cols[j]))
        recips.append(inv)
        q = [v * inv for v in cols[j]]
        for c in range(j + 1, n):
            w = dot(q, cols[c])
            upper[j, c] = w
            for i in range(len(q)):
                cols[c][i] = cols[c][i] - w * q[i]
        for e in range(RHS):
            target[j, e] = dot(q, [R[i, e] for i in range(e + 1)])
    coef = {}
    for e in range(RHS):
        for j in reversed(range(n)):
            value = target[j, e]
            for later in range(j + 1, n):
                value = value - upper[j, later] * coef[later, e]
            coef[j, e] = value * recips[j]
    return coef


def final_kernel(
    X, Y, scale, gathered, V, V4, ortho, triangle, update, O, W, out_sems
):
    R = merged_factor(gathered[...])
    row = lax.broadcasted_iota(jnp.int32, (16, 128), 0)
    lane = lax.broadcasted_iota(jnp.int32, (16, 128), 1)
    tri = jnp.zeros((16, 128), F32)
    for (i, j), value in R.items():
        tri = jnp.where((row == i) & (lane == j), value * (1.0 / scale), tri)
    triangle[...] = tri[:COLS, :COLS]
    T = inverse(R)
    weights = {}
    for n, ((i, j), value) in enumerate(T.items()):
        weights[i, j] = n
        W[n] = jnp.broadcast_to(value * scale, (8, 128))
    coef = least_squares(R)
    base = len(weights)
    for n, ((k, e), value) in enumerate(coef.items()):
        weights[k, COLS + e] = base + n
        W[base + n] = jnp.broadcast_to(value, (8, 128))

    CH = 32
    XB = 2
    outs = []
    for block in range(X // XB):

        def rows(i, carry, block=block):
            x = block * XB + i
            for at in range(0, Y, CH):
                b = [basis_rows(V, V4, k, x, at, CH) for k in range(COLS)]
                for j in range(COLS + RHS):
                    value = None
                    for k in range(j + 1 if j < COLS else RHS * S):
                        w = jnp.concatenate([W[weights[k, j]]] * (CH // 8), axis=0)
                        value = w * b[k] if value is None else value + w * b[k]
                    O[j, x, pl.ds(at, CH), :] = value
            return carry

        lax.fori_loop(0, XB, rows, 0)
        here = pl.ds(block * XB, XB)
        for copy in (
            pltpu.make_async_copy(
                O.at[pl.ds(0, COLS), here], ortho.at[:, here], out_sems.at[2 * block]
            ),
            pltpu.make_async_copy(
                O.at[pl.ds(COLS, RHS), here], update.at[:, here], out_sems.at[2 * block + 1]
            ),
        ):
            copy.start()
            outs.append(copy)
    for copy in outs:
        copy.wait()


ANY = pl.BlockSpec(memory_space=pl.ANY)
VMEM = pl.BlockSpec(memory_space=pltpu.VMEM)
MIB = 1024 * 1024
PIN, BLOCK, FAR = range(3)


def call(kernel, name, inputs, outputs, scratch=(), aliases={}, limit=4):
    pin = lambda a: pltpu.with_memory_space_constraint(a, pltpu.VMEM)
    spec = lambda place: ANY if place == FAR else VMEM
    return pl.pallas_call(
        kernel,
        out_shape=tuple(
            pltpu.VMEM(o, F32) if place == PIN else jax.ShapeDtypeStruct(o, F32)
            for o, place in outputs
        ),
        in_specs=[spec(place) for _, place in inputs],
        out_specs=tuple(spec(place) for _, place in outputs),
        scratch_shapes=list(scratch),
        input_output_aliases=aliases,
        compiler_params=pltpu.CompilerParams(vmem_limit_bytes=limit * MIB),
        name=name,
    )(*(pin(a) if place == PIN else a for a, place in inputs))


def body(right_sides, diagonal, velocity):
    _, X, Y, Z = right_sides.shape
    nx, ny = lax.axis_size("gx"), lax.axis_size("gy")
    devices = nx * ny
    scale = math.sqrt(X * Y * Z * devices)
    XE, YE = X + 8, Y + 2 * YP
    inputs = [(right_sides, FAR), (velocity, FAR), (diagonal, FAR)]
    dma = pltpu.SemaphoreType.DMA

    def shift(value, axis, by):
        size = lax.axis_size(axis)
        return lax.ppermute(
            value, axis, [(i, i + by) for i in range(size) if 0 <= i + by < size]
        )

    slab = ((20, Y, Z), PIN)
    x_low, x_high = call(
        functools.partial(pack_x_kernel, X), "pack_x", inputs, [slab, slab], [dma((12,))]
    )
    xl, xh = shift(x_high, "gx", 1), shift(x_low, "gx", -1)
    slab = ((6, X, 8, Z), PIN)
    y_low, y_high = call(
        functools.partial(pack_y_kernel, Y), "pack_y", inputs, [slab, slab], [dma((6,))]
    )
    yl, yh = shift(y_high, "gy", 1), shift(y_low, "gy", -1)
    v_shape, u_shape = ((S, RHS, XE, YE, Z), PIN), ((4, XE, YE, Z), PIN)
    V, U = call(
        functools.partial(load_kernel, X, Y), "load", inputs, [v_shape, u_shape], [dma((3,))]
    )
    strip = ((2 * CORNER_ROWS, Z), PIN)
    V, U, c_low, c_high = call(
        functools.partial(place_y_kernel, X, Y),
        "place_y",
        [(yl, PIN), (yh, PIN), (V, PIN), (U, PIN)],
        [v_shape, u_shape, strip, strip],
        aliases={2: 0, 3: 1},
    )
    cl, ch = shift(c_high, "gx", 1), shift(c_low, "gx", -1)
    v4_shape, a_shape = ((RHS, X, Y, Z), PIN), ((6, XE, YE, Z), PIN)
    work = pltpu.VMEM((COLS - 1, X, Y, Z), F32)
    V, V4, A, line = call(
        functools.partial(inner_kernel, X, Y),
        "inner",
        [(V, PIN), (U, PIN)],
        [v_shape, v4_shape, a_shape, ((1, 128), PIN)],
        [work],
        aliases={0: 0},
        limit=8,
    )
    V, V4, A, U, packed = call(
        functools.partial(outer_kernel, X, Y),
        "outer",
        [(a, PIN) for a in (xl, xh, cl, ch, line, V, V4, A, U)],
        [v_shape, v4_shape, a_shape, u_shape, ((2 * devices, 128), BLOCK)],
        [work],
        aliases={5: 0, 6: 1, 7: 2, 8: 3},
        limit=8,
    )
    gathered = lax.all_to_all(packed, ("gx", "gy"), 0, 0, tiled=True)
    out = [((COLS, X, Y, Z), FAR), ((COLS, COLS), BLOCK), ((RHS, X, Y, Z), FAR)]
    ortho, triangle, update = call(
        functools.partial(final_kernel, X, Y, scale),
        "combine",
        [(gathered, BLOCK), (V, PIN), (V4, PIN)],
        out,
        [
            pltpu.VMEM((COLS + RHS, X, Y, Z), F32),
            pltpu.VMEM((71, 8, 128), F32),
            dma((X,)),
        ],
        limit=10,
    )
    return ortho, triangle, update


def solution(mesh):
    return jax.shard_map(
        body,
        mesh=mesh,
        in_specs=(P(None, "gx", "gy", None), P("gx", "gy", None), P(None, "gx", "gy", None)),
        out_specs=(P(None, "gx", "gy", None), P(), P(None, "gx", "gy", None)),
        check_vma=False,
    )
```

time: 102 us -> 81.3 us (0.80)
  Pallas kernels: 30.9 us -> 19.9 us
  waiting for transfers between devices: 14.3 us -> 7.19 us
  starting transfers between devices: 22.8 us -> 17.2 us
  local copies, waits for them, and re-layouts: 1.87 us -> 3.67 us
  blocking collectives: 30.8 us -> 32.2 us
    pallas_call x4 -> x7, Pallas kernels: 30.9 us -> 19.9 us  [call(): pl.pallas_call(kernel, out_shape=tuple((pltpu.VMEM(o, F32) if place == PI...]
    ppermute x8 -> x6, waiting for transfers between devices: 14.3 us -> 7.19 us  [shift(): lax.ppermute(value, axis, [(i, i + by) for i in range(size) if 0 <= i + b...]
    ppermute x8 -> x6, starting transfers between devices: 22.8 us -> 17.2 us  [shift(): lax.ppermute(value, axis, [(i, i + by) for i in range(size) if 0 <= i + b...]
    unnamed x16 -> x6, local copies, waits for them, and re-layouts: 1.87 us -> 3.67 us
    all_to_all x1, blocking collectives: 30.8 us -> 32.2 us  [body(): gathered = lax.all_to_all(packed, ('gx', 'gy'), 0, 0, tiled=True)]
  transfers between devices with their start and end apart: 8 -> 6, of which waited for: 4 -> 2; matrix products, arithmetic and copies ran while one was open for 0% -> 0% of each run, Pallas kernels for 2% -> 9%
where the time goes in v2:
time: 81.3 us; the launch traced here: 80.9 us
  blocking collectives  32.2 us (40%)
  Pallas kernels  19.9 us (24%)
  starting transfers between devices  17.2 us (21%)
  waiting for transfers between devices  7.19 us (9%)
  local copies, waits for them, and re-layouts  3.67 us (5%)
    all_to_all x1, blocking collectives, body(): gathered = lax.all_to_all(packed, ('gx', 'gy'), 0, 0, tiled=True)  32.2 us
    pallas_call x7, Pallas kernels, call(): pl.pallas_call(kernel, out_shape=tuple((pltpu.VMEM(o, F32) if place == PI...  19.9 us
    ppermute x6, starting transfers between devices, shift(): lax.ppermute(value, axis, [(i, i + by) for i in range(size) if 0 <= i + b...  17.2 us
    ppermute x6, waiting for transfers between devices, shift(): lax.ppermute(value, axis, [(i, i + by) for i in range(size) if 0 <= i + b...  7.19 us
    unnamed x6, local copies, waits for them, and re-layouts  3.67 us
  transfers between devices with their start and end apart: 6, of which 2 were waited for; matrix products, arithmetic and copies ran while one was open for 0% of the time, Pallas kernels for 9%

profile of v2, /device:TPU:1, one launch (start us, length us, event | category | flops | bytes accessed | tf_op | source)
XLA Modules:
  0.0 80.9 jit_solution(8196654219080773955)
XLA Ops:
  0.6 0.0 copy-start
  0.6 1.4 %copy-done = f32[3,16,64,128]{3,2,1,0:T(8,128)S(1)} copy-done((f32[3,16,64,128]{3,2,1,0:T(8,128)S(1)}, f32[3,16,64,128]{3,2,1,0:T(8,128)}, u32[]{:S(2)}) %copy-start) | copy-done | bytes 1572888
  2.0 1.2 %copy-done.1 = f32[2,16,64,128]{3,2,1,0:T(8,128)S(1)} copy-done((f32[2,16,64,128]{3,2,1,0:T(8,128)S(1)}, f32[2,16,64,128]{3,2,1,0:T(8,128)}, u32[]{:S(2)}) %copy-start.1) | copy-done | bytes 1048600
  3.3 1.0 %copy-done.2 = f32[16,64,128]{2,1,0:T(8,128)S(1)} copy-done((f32[16,64,128]{2,1,0:T(8,128)S(1)}, f32[16,64,128]{2,1,0:T(8,128)}, u32[]{:S(2)}) %copy-start.2) | copy-done | bytes 524312
  4.3 1.8 %pack_x.1 = (f32[20,64,128]{2,1,0:T(8,128)S(1)}, f32[20,64,128]{2,1,0:T(8,128)S(1)}) custom-call(f32[2,16,64,128]{3,2,1,0:T(8,128)S(1)} %copy-done.1, f32[3,16,64,128]{3,2,1,0:T(8,128)S(1)} %copy-done, f32[16,64,128]{2,1,0:T(8,128)S(1)} %copy-done.2), custom_call_target="tpu_custom_call" | custom-call | tf_op jit(solution)/shard_map/pack_x/pallas_call | solution.py:398
  6.1 4.4 %collective-permute-start = (f32[20,64,128]{2,1,0:T(8,128)S(1)}, f32[20,64,128]{2,1,0:T(8,128)S(1)}, u32[]{:S(2)}, u32[]{:S(2)}) collective-permute-start(f32[20,64,128]{2,1,0:T(8,128)S(1)} %get-tuple-element.20), channel_id=1, source_target_pairs={{0,8},{8,16},{16,24},{24,32},{32,40},{40,48},{48,56},{56,64},{64,7... | collective-permute-start | bytes 1966088 | tf_op jit(solution)/shard_map/ppermute | solution.py:424
  10.5 1.3 %collective-permute-start.1 = (f32[20,64,128]{2,1,0:T(8,128)S(1)}, f32[20,64,128]{2,1,0:T(8,128)S(1)}, u32[]{:S(2)}, u32[]{:S(2)}) collective-permute-start(f32[20,64,128]{2,1,0:T(8,128)S(1)} %get-tuple-element.21), channel_id=1, source_target_pairs={{8,0},{16,8},{24,16},{32,24},{40,32},{48,40},{56,48},{64,56},{72,6... | collective-permute-start | bytes 1966088 | tf_op jit(solution)/shard_map/ppermute | solution.py:424
  11.8 0.2 pack_y.1
  12.0 4.0 %collective-permute-start.2 = (f32[6,16,8,128]{3,2,1,0:T(8,128)S(1)}, f32[6,16,8,128]{3,2,1,0:T(8,128)S(1)}, u32[]{:S(2)}, u32[]{:S(2)}) collective-permute-start(f32[6,16,8,128]{3,2,1,0:T(8,128)S(1)} %get-tuple-element.22), channel_id=1, source_target_pairs={{0,1},{1,2},{2,3},{3,4},{4,5},{5,6},{6,7},{8,9},{9,10},{10,11},{11... | collective-permute-start | bytes 1179656 | tf_op jit(solution)/shard_map/ppermute | solution.py:424
  16.1 1.9 %collective-permute-start.3 = (f32[6,16,8,128]{3,2,1,0:T(8,128)S(1)}, f32[6,16,8,128]{3,2,1,0:T(8,128)S(1)}, u32[]{:S(2)}, u32[]{:S(2)}) collective-permute-start(f32[6,16,8,128]{3,2,1,0:T(8,128)S(1)} %get-tuple-element.23), channel_id=1, source_target_pairs={{1,0},{2,1},{3,2},{4,3},{5,4},{6,5},{7,6},{9,8},{10,9},{11,10},{12... | collective-permute-start | bytes 1179656 | tf_op jit(solution)/shard_map/ppermute | solution.py:424
  18.0 0.3 load.1
  18.3 2.5 %collective-permute-done.2.yl = f32[6,16,8,128]{3,2,1,0:T(8,128)S(1)} collective-permute-done((f32[6,16,8,128]{3,2,1,0:T(8,128)S(1)}, f32[6,16,8,128]{3,2,1,0:T(8,128)S(1)}, u32[]{:S(2)}, u32[]{:S(2)}) %collective-permute-start.2) | collective-permute-done | bytes 393248 | tf_op jit(solution)/shard_map/ppermute | solution.py:424
  20.8 4.7 %collective-permute-done.3.yh = f32[6,16,8,128]{3,2,1,0:T(8,128)S(1)} collective-permute-done((f32[6,16,8,128]{3,2,1,0:T(8,128)S(1)}, f32[6,16,8,128]{3,2,1,0:T(8,128)S(1)}, u32[]{:S(2)}, u32[]{:S(2)}) %collective-permute-start.3) | collective-permute-done | bytes 393248 | tf_op jit(solution)/shard_map/ppermute | solution.py:424
  25.4 0.1 place_y.1
  25.6 4.3 %collective-permute-start.4 = (f32[48,128]{1,0:T(8,128)S(1)}, f32[48,128]{1,0:T(8,128)S(1)}, u32[]{:S(2)}, u32[]{:S(2)}) collective-permute-start(f32[48,128]{1,0:T(8,128)S(1)} %get-tuple-element.26), channel_id=1, source_target_pairs={{0,8},{8,16},{16,24},{24,32},{32,40},{40,48},{48,56},{56,64},{64,7... | collective-permute-start | bytes 73736 | tf_op jit(solution)/shard_map/ppermute | solution.py:424
  29.8 1.3 %collective-permute-start.5 = (f32[48,128]{1,0:T(8,128)S(1)}, f32[48,128]{1,0:T(8,128)S(1)}, u32[]{:S(2)}, u32[]{:S(2)}) collective-permute-start(f32[48,128]{1,0:T(8,128)S(1)} %get-tuple-element.27), channel_id=1, source_target_pairs={{8,0},{16,8},{24,16},{32,24},{40,32},{48,40},{56,48},{64,56},{72,6... | collective-permute-start | bytes 73736 | tf_op jit(solution)/shard_map/ppermute | solution.py:424
  31.1 6.7 %inner.1 = (f32[4,2,24,96,128]{4,3,2,1,0:T(8,128)S(1)}, f32[2,16,64,128]{3,2,1,0:T(8,128)S(1)}, f32[6,24,96,128]{3,2,1,0:T(8,128)S(1)}, f32[1,128]{1,0:T(1,128)S(1)}) custom-call(f32[4,2,24,96,128]{4,3,2,1,0:T(8,128)S(1)} %get-tuple-element.28.V_in, f32[4,24,96,128]{3,2,1,0:T(8,128)S(1)} %get-tuple-element.29.U.U_in), custom_call_target="tpu_custom_call", output_to_operand_aliasing={{0}: (0, {})} | custom-call | tf_op jit(solution)/shard_map/inner/pallas_call | solution.py:398
  37.8 0.0 collective-permute-done.4.cl
  37.8 0.0 collective-permute-done.5.ch
  37.8 0.0 collective-permute-done.xl
  37.8 0.0 collective-permute-done.1.xh
  37.9 5.4 %outer.1 = (f32[4,2,24,96,128]{4,3,2,1,0:T(8,128)S(1)}, f32[2,16,64,128]{3,2,1,0:T(8,128)S(1)}, f32[6,24,96,128]{3,2,1,0:T(8,128)S(1)}, f32[4,24,96,128]{3,2,1,0:T(8,128)S(1)}, f32[512,128]{1,0:T(8,128)S(1)}) custom-call(f32[20,64,128]{2,1,0:T(8,128)S(1)} %collective-permute-done.xl, ...), custom_call_target="tpu_custom_call", output_to_operand_aliasing={{0}: (5, {}), {1}: (6, {}), {2}: (7, {}), {3}: (8, {})} | custom-call | tf_op jit(solution)/shard_map/outer/pallas_call | solution.py:398
  43.3 32.2 %all_to_all.11 = f32[256,2,128]{2,1,0:T(2,128)S(1)} all-to-all(f32[256,2,128]{2,1,0:T(2,128)S(1)} %bitcast.3), channel_id=1, replica_groups=mesh['gx'=32,'gy'=8] {'gx','gy'}, dimensions={0} | all-to-all | bytes 524288 | tf_op jit(solution)/shard_map/all_to_all | solution.py:471
  75.5 5.4 %combine.1 = (f32[10,16,64,128]{3,2,1,0:T(8,128)}, f32[10,10]{1,0:T(8,128)}, f32[2,16,64,128]{3,2,1,0:T(8,128)}) custom-call(f32[512,128]{1,0:T(8,128)S(1)} %bitcast.2, f32[4,2,24,96,128]{4,3,2,1,0:T(8,128)S(1)} %get-tuple-element.35.V, f32[2,16,64,128]{3,2,1,0:T(8,128)S(1)} %get-tuple-element.36.V4), custom_call_target="tpu_custom_call" | custom-call | tf_op jit(solution)/shard_map/combine/pallas_call | solution.py:398
  (2 shorter events, 0.0 us)
Async XLA Ops:
  0.6 1.4 %copy-start = (f32[3,16,64,128]{3,2,1,0:T(8,128)S(1)}, f32[3,16,64,128]{3,2,1,0:T(8,128)}, u32[]{:S(2)}) copy-start(f32[3,16,64,128]{3,2,1,0:T(8,128)} %vel.5) | copy-start | bytes 4718596
  2.0 1.2 %copy-start.1 = (f32[2,16,64,128]{3,2,1,0:T(8,128)S(1)}, f32[2,16,64,128]{3,2,1,0:T(8,128)}, u32[]{:S(2)}) copy-start(f32[2,16,64,128]{3,2,1,0:T(8,128)} %rhs.5) | copy-start | bytes 3145732
  3.3 1.0 %copy-start.2 = (f32[16,64,128]{2,1,0:T(8,128)S(1)}, f32[16,64,128]{2,1,0:T(8,128)}, u32[]{:S(2)}) copy-start(f32[16,64,128]{2,1,0:T(8,128)} %diag.5) | copy-start | bytes 1572868
  6.1 31.7 %collective-permute-start = (f32[20,64,128]{2,1,0:T(8,128)S(1)}, f32[20,64,128]{2,1,0:T(8,128)S(1)}, u32[]{:S(2)}, u32[]{:S(2)}) collective-permute-start(f32[20,64,128]{2,1,0:T(8,128)S(1)} %get-tuple-element.20), channel_id=1, source_target_pairs={{0,8},{8,16},{16,24},{24,32},{32,40},{40,48},{48,56},{56,64},{64,7... | collective-permute-start | bytes 1966088 | tf_op jit(solution)/shard_map/ppermute | solution.py:424
  10.5 27.3 %collective-permute-start.1 = (f32[20,64,128]{2,1,0:T(8,128)S(1)}, f32[20,64,128]{2,1,0:T(8,128)S(1)}, u32[]{:S(2)}, u32[]{:S(2)}) collective-permute-start(f32[20,64,128]{2,1,0:T(8,128)S(1)} %get-tuple-element.21), channel_id=1, source_target_pairs={{8,0},{16,8},{24,16},{32,24},{40,32},{48,40},{56,48},{64,56},{72,6... | collective-permute-start | bytes 1966088 | tf_op jit(solution)/shard_map/ppermute | solution.py:424
  12.0 8.8 %collective-permute-start.2 = (f32[6,16,8,128]{3,2,1,0:T(8,128)S(1)}, f32[6,16,8,128]{3,2,1,0:T(8,128)S(1)}, u32[]{:S(2)}, u32[]{:S(2)}) collective-permute-start(f32[6,16,8,128]{3,2,1,0:T(8,128)S(1)} %get-tuple-element.22), channel_id=1, source_target_pairs={{0,1},{1,2},{2,3},{3,4},{4,5},{5,6},{6,7},{8,9},{9,10},{10,11},{11... | collective-permute-start | bytes 1179656 | tf_op jit(solution)/shard_map/ppermute | solution.py:424
  16.1 9.4 %collective-permute-start.3 = (f32[6,16,8,128]{3,2,1,0:T(8,128)S(1)}, f32[6,16,8,128]{3,2,1,0:T(8,128)S(1)}, u32[]{:S(2)}, u32[]{:S(2)}) collective-permute-start(f32[6,16,8,128]{3,2,1,0:T(8,128)S(1)} %get-tuple-element.23), channel_id=1, source_target_pairs={{1,0},{2,1},{3,2},{4,3},{5,4},{6,5},{7,6},{9,8},{10,9},{11,10},{12... | collective-permute-start | bytes 1179656 | tf_op jit(solution)/shard_map/ppermute | solution.py:424
  25.6 12.3 %collective-permute-start.4 = (f32[48,128]{1,0:T(8,128)S(1)}, f32[48,128]{1,0:T(8,128)S(1)}, u32[]{:S(2)}, u32[]{:S(2)}) collective-permute-start(f32[48,128]{1,0:T(8,128)S(1)} %get-tuple-element.26), channel_id=1, source_target_pairs={{0,8},{8,16},{16,24},{24,32},{32,40},{40,48},{48,56},{56,64},{64,7... | collective-permute-start | bytes 73736 | tf_op jit(solution)/shard_map/ppermute | solution.py:424
  29.8 8.0 %collective-permute-start.5 = (f32[48,128]{1,0:T(8,128)S(1)}, f32[48,128]{1,0:T(8,128)S(1)}, u32[]{:S(2)}, u32[]{:S(2)}) collective-permute-start(f32[48,128]{1,0:T(8,128)S(1)} %get-tuple-element.27), channel_id=1, source_target_pairs={{8,0},{16,8},{24,16},{32,24},{40,32},{48,40},{56,48},{64,56},{72,6... | collective-permute-start | bytes 73736 | tf_op jit(solution)/shard_map/ppermute | solution.py:424

commit v3 on v2

--- a/solution.py
+++ b/solution.py
@@ -30,9 +30,15 @@
         copy.wait()
 
 
-def pack_x_kernel(X, rhs, vel, diag, low, high, sems):
+def toward_high(axis, pairing):
+    return lax.axis_index(axis) % 2 == pairing
+
+
+def pack_x_kernel(X, rhs, vel, diag, first, second, sems):
     copies = []
-    for out, at4, at3 in ((high, X - 4, X - 3), (low, 0, 0)):
+    for pairing, out in enumerate((first, second)):
+        high = toward_high("gx", pairing)
+        at4, at3 = jnp.where(high, X - 4, 0), jnp.where(high, X - 3, 0)
         for f in range(RHS):
             copies.append((rhs.at[f, pl.ds(at4, 4)], out.at[pl.ds(4 * f, 4)]))
         for c in range(3):
@@ -41,12 +47,13 @@
     run_copies([pltpu.make_async_copy(s, d, sems.at[i]) for i, (s, d) in enumerate(copies)])
 
 
-def pack_y_kernel(Y, rhs, vel, diag, low, high, sems):
+def pack_y_kernel(Y, rhs, vel, diag, first, second, sems):
     copies = []
-    for out, at in ((high, Y - 8), (low, 0)):
-        copies.append((rhs.at[:, :, pl.ds(at, 8)], out.at[pl.ds(0, 2)]))
-        copies.append((vel.at[:, :, pl.ds(at, 8)], out.at[pl.ds(2, 3)]))
-        copies.append((diag.at[:, pl.ds(at, 8)], out.at[5]))
+    for pairing, out in enumerate((first, second)):
+        at = pl.ds(pl.multiple_of(jnp.where(toward_high("gy", pairing), Y - 8, 0), 8), 8)
+        copies.append((rhs.at[:, :, at], out.at[pl.ds(0, 2)]))
+        copies.append((vel.at[:, :, at], out.at[pl.ds(2, 3)]))
+        copies.append((diag.at[:, at], out.at[5]))
     run_copies([pltpu.make_async_copy(s, d, sems.at[i]) for i, (s, d) in enumerate(copies)])
 
 
@@ -60,28 +67,31 @@
     run_copies([pltpu.make_async_copy(s, d, sems.at[i]) for i, (s, d) in enumerate(copies)])
 
 
-def corner_cells(X, Y, low, own):
+def corner_cells(X, Y, high, own):
     cells = []
     for y_low in (True, False):
         for f in range(6):
             for dx, dy in FIELD_CORNER if f < 2 else COEF_CORNER:
                 if own:
-                    x = 3 + dx if low else X + 4 - dx
+                    x = jnp.where(high, X + 4 - dx, 3 + dx)
                 else:
-                    x = 4 - dx if low else X + 3 + dx
+                    x = jnp.where(high, X + 3 + dx, 4 - dx)
                 cells.append((f, x, YP - dy if y_low else YP + Y - 1 + dy))
     return cells
 
 
-def place_y_kernel(X, Y, yl, yh, V_in, U_in, V, U, low, high):
-    for got, at in ((yl, YP - 8), (yh, YP + Y)):
+def place_y_kernel(X, Y, y0, y1, V_in, U_in, V, U, first, second):
+    for pairing, got in enumerate((y0, y1)):
+        at = jnp.where(toward_high("gy", pairing), YP + Y, YP - 8)
+        here = pl.ds(pl.multiple_of(at, 8), 8)
         for x in range(X):
             for f in range(2):
-                V[0, f, 4 + x, at : at + 8, :] = got[f, x]
+                V[0, f, 4 + x, here, :] = got[f, x]
             for c in range(4):
-                U[c, 4 + x, at : at + 8, :] = got[2 + c, x]
-    for out, is_low in ((low, True), (high, False)):
-        for row, (f, x, y) in enumerate(corner_cells(X, Y, is_low, True)):
+                U[c, 4 + x, here, :] = got[2 + c, x]
+    for pairing, out in enumerate((first, second)):
+        cells = corner_cells(X, Y, toward_high("gx", pairing), True)
+        for row, (f, x, y) in enumerate(cells):
             out[row : row + 1, :] = (
                 V[0, f, x, y : y + 1, :] if f < 2 else U[f - 2, x, y : y + 1, :]
             )
@@ -221,21 +231,22 @@
     line[...] = local_factor(Y, V, V4, Q, [(4, X // 2), (X // 2, X - 4)])
 
 
-def outer_kernel(X, Y, xl, xh, cl, ch, inner_line, V_in, V4_in, A_in, U_in, V, V4, A, U, packed, Q):
+def outer_kernel(X, Y, x0, x1, c0, c1, inner_line, V_in, V4_in, A_in, U_in, V, V4, A, U, packed, Q):
     own_y = slice(YP, YP + Y)
-    for got, at4, at3 in ((xl, 0, 1), (xh, X + 4, X + 4)):
+    for pairing, (got, corner) in enumerate(((x0, c0), (x1, c1))):
+        high = toward_high("gx", pairing)
+        at4, at3 = jnp.where(high, X + 4, 0), jnp.where(high, X + 4, 1)
         for i in range(4):
             for f in range(RHS):
                 V[0, f, at4 + i, own_y, :] = got[4 * f + i]
         for i in range(3):
             for c in range(4):
                 U[c, at3 + i, own_y, :] = got[8 + 3 * c + i]
-    for got, is_low in ((cl, True), (ch, False)):
-        for row, (f, x, y) in enumerate(corner_cells(X, Y, is_low, False)):
+        for row, (f, x, y) in enumerate(corner_cells(X, Y, high, False)):
             if f < 2:
-                V[0, f, x, y : y + 1, :] = got[row : row + 1, :]
+                V[0, f, x, y : y + 1, :] = corner[row : row + 1, :]
             else:
-                U[f - 2, x, y : y + 1, :] = got[row : row + 1, :]
+                U[f - 2, x, y : y + 1, :] = corner[row : row + 1, :]
     coefficient_rows(X, Y, U, A, [(1, 4), (X + 4, X + 7)])
     for k in range(1, S + 1):
         power_rows(Y, V, V4, A, k, [(k, k + 4), (X + 4 - k, X + 8 - k)], 2)
@@ -416,38 +427,40 @@
     devices = nx * ny
     scale = math.sqrt(X * Y * Z * devices)
     XE, YE = X + 8, Y + 2 * YP
-    inputs = [(right_sides, FAR), (velocity, FAR), (diagonal, FAR)]
+    inputs = [
+        (pltpu.with_memory_space_constraint(a, pltpu.HBM), FAR)
+        for a in (right_sides, velocity, diagonal)
+    ]
     dma = pltpu.SemaphoreType.DMA
 
-    def shift(value, axis, by):
+    def swap(value, axis, pairing):
         size = lax.axis_size(axis)
-        return lax.ppermute(
-            value, axis, [(i, i + by) for i in range(size) if 0 <= i + by < size]
-        )
+        pairs = [(i, i + 1) for i in range(pairing, size - 1, 2)]
+        return lax.ppermute(value, axis, pairs + [(j, i) for i, j in pairs])
 
     slab = ((20, Y, Z), PIN)
-    x_low, x_high = call(
+    x0, x1 = call(
         functools.partial(pack_x_kernel, X), "pack_x", inputs, [slab, slab], [dma((12,))]
     )
-    xl, xh = shift(x_high, "gx", 1), shift(x_low, "gx", -1)
+    x0, x1 = swap(x0, "gx", 0), swap(x1, "gx", 1)
     slab = ((6, X, 8, Z), PIN)
-    y_low, y_high = call(
+    y0, y1 = call(
         functools.partial(pack_y_kernel, Y), "pack_y", inputs, [slab, slab], [dma((6,))]
     )
-    yl, yh = shift(y_high, "gy", 1), shift(y_low, "gy", -1)
+    y1, y0 = swap(y1, "gy", 1), swap(y0, "gy", 0)
     v_shape, u_shape = ((S, RHS, XE, YE, Z), PIN), ((4, XE, YE, Z), PIN)
     V, U = call(
         functools.partial(load_kernel, X, Y), "load", inputs, [v_shape, u_shape], [dma((3,))]
     )
     strip = ((2 * CORNER_ROWS, Z), PIN)
-    V, U, c_low, c_high = call(
+    V, U, c0, c1 = call(
         functools.partial(place_y_kernel, X, Y),
         "place_y",
-        [(yl, PIN), (yh, PIN), (V, PIN), (U, PIN)],
+        [(y0, PIN), (y1, PIN), (V, PIN), (U, PIN)],
         [v_shape, u_shape, strip, strip],
         aliases={2: 0, 3: 1},
     )
-    cl, ch = shift(c_high, "gx", 1), shift(c_low, "gx", -1)
+    c0, c1 = swap(c0, "gx", 0), swap(c1, "gx", 1)
     v4_shape, a_shape = ((RHS, X, Y, Z), PIN), ((6, XE, YE, Z), PIN)
     work = pltpu.VMEM((COLS - 1, X, Y, Z), F32)
     V, V4, A, line = call(
@@ -462,7 +475,7 @@
     V, V4, A, U, packed = call(
         functools.partial(outer_kernel, X, Y),
         "outer",
-        [(a, PIN) for a in (xl, xh, cl, ch, line, V, V4, A, U)],
+        [(a, PIN) for a in (x0, x1, c0, c1, line, V, V4, A, U)],
         [v_shape, v4_shape, a_shape, u_shape, ((2 * devices, 128), BLOCK)],
         [work],
         aliases={5: 0, 6: 1, 7: 2, 8: 3},

time: 81.3 us -> 69.9 us (0.86)
  starting transfers between devices: 17.2 us -> 12.9 us
  local copies, waits for them, and re-layouts: 3.67 us -> 0 us
  blocking collectives: 32.2 us -> 29.4 us
  waiting for transfers between devices: 7.19 us -> 4.4 us
  Pallas kernels: 19.9 us -> 22.2 us
    ppermute x6, starting transfers between devices: 17.2 us -> 12.9 us  [swap(): return lax.ppermute(value, axis, pairs + [(j, i) for i, j in pairs])]
    unnamed x6 -> x0, local copies, waits for them, and re-layouts: 3.67 us -> none
    ppermute x6, waiting for transfers between devices: 7.19 us -> 4.4 us  [swap(): return lax.ppermute(value, axis, pairs + [(j, i) for i, j in pairs])]
    all_to_all x1, blocking collectives: 32.2 us -> 29.4 us  [body(): gathered = lax.all_to_all(packed, ('gx', 'gy'), 0, 0, tiled=True)]
    pallas_call x7, Pallas kernels: 19.9 us -> 22.2 us  [call(): pl.pallas_call(kernel, out_shape=tuple((pltpu.VMEM(o, F32) if place == PI...]
  transfers between devices with their start and end apart: 6 -> 6, of which waited for: 2 -> 1; matrix products, arithmetic and copies ran while one was open for 0% -> 0% of each run, Pallas kernels for 9% -> 14%
where the time goes in v3:
time: 69.9 us; the launch traced here: 69.7 us
  blocking collectives  29.4 us (42%)
  Pallas kernels  22.2 us (32%)
  starting transfers between devices  12.9 us (18%)
  waiting for transfers between devices  4.4 us (6%)
  between operations  0.73 us (1%)
    all_to_all x1, blocking collectives, body(): gathered = lax.all_to_all(packed, ('gx', 'gy'), 0, 0, tiled=True)  29.4 us
    pallas_call x7, Pallas kernels, call(): pl.pallas_call(kernel, out_shape=tuple((pltpu.VMEM(o, F32) if place == PI...  22.2 us
    ppermute x6, starting transfers between devices, swap(): return lax.ppermute(value, axis, pairs + [(j, i) for i, j in pairs])  12.9 us
    ppermute x6, waiting for transfers between devices, swap(): return lax.ppermute(value, axis, pairs + [(j, i) for i, j in pairs])  4.4 us
  transfers between devices with their start and end apart: 6, of which 1 were waited for; matrix products, arithmetic and copies ran while one was open for 0% of the time, Pallas kernels for 14%

profile of v3, /device:TPU:1, one launch (start us, length us, event | category | flops | bytes accessed | tf_op | source)
XLA Modules:
  0.0 69.7 jit_solution(5632166959854567300)
XLA Ops:
  0.6 1.5 %pack_x.1 = (f32[20,64,128]{2,1,0:T(8,128)S(1)}, f32[20,64,128]{2,1,0:T(8,128)S(1)}) custom-call(f32[2,16,64,128]{3,2,1,0:T(8,128)} %rhs.5, f32[3,16,64,128]{3,2,1,0:T(8,128)} %vel.5, f32[16,64,128]{2,1,0:T(8,128)} %diag.5), custom_call_target="tpu_custom_call" | custom-call | tf_op jit(solution)/shard_map/pack_x/pallas_call | solution.py:409
  2.1 2.6 %collective-permute-start = (f32[20,64,128]{2,1,0:T(8,128)S(1)}, f32[20,64,128]{2,1,0:T(8,128)S(1)}, u32[]{:S(2)}, u32[]{:S(2)}) collective-permute-start(f32[20,64,128]{2,1,0:T(8,128)S(1)} %get-tuple-element.20), channel_id=1, source_target_pairs={{0,8},{16,24},{32,40},{48,56},{64,72},{80,88},{96,104},{112,120},{... | collective-permute-start | bytes 1966088 | tf_op jit(solution)/shard_map/ppermute | solution.py:439
  4.7 0.7 collective-permute-start.1
  5.4 1.3 %pack_y.1 = (f32[6,16,8,128]{3,2,1,0:T(8,128)S(1)}, f32[6,16,8,128]{3,2,1,0:T(8,128)S(1)}) custom-call(f32[2,16,64,128]{3,2,1,0:T(8,128)} %rhs.5, f32[3,16,64,128]{3,2,1,0:T(8,128)} %vel.5, f32[16,64,128]{2,1,0:T(8,128)} %diag.5), custom_call_target="tpu_custom_call" | custom-call | tf_op jit(solution)/shard_map/pack_y/pallas_call | solution.py:409
  6.6 1.0 %collective-permute-start.2 = (f32[6,16,8,128]{3,2,1,0:T(8,128)S(1)}, f32[6,16,8,128]{3,2,1,0:T(8,128)S(1)}, u32[]{:S(2)}, u32[]{:S(2)}) collective-permute-start(f32[6,16,8,128]{3,2,1,0:T(8,128)S(1)} %get-tuple-element.22), channel_id=1, source_target_pairs={{0,1},{2,3},{4,5},{6,7},{1,0},{3,2},{5,4},{7,6},{8,9},{10,11},{12,... | collective-permute-start | bytes 1179656 | tf_op jit(solution)/shard_map/ppermute | solution.py:439
  7.7 3.1 %collective-permute-start.3 = (f32[6,16,8,128]{3,2,1,0:T(8,128)S(1)}, f32[6,16,8,128]{3,2,1,0:T(8,128)S(1)}, u32[]{:S(2)}, u32[]{:S(2)}) collective-permute-start(f32[6,16,8,128]{3,2,1,0:T(8,128)S(1)} %get-tuple-element.23), channel_id=1, source_target_pairs={{1,2},{3,4},{5,6},{2,1},{4,3},{6,5},{9,10},{11,12},{13,14},{10,9},... | collective-permute-start | bytes 1179656 | tf_op jit(solution)/shard_map/ppermute | solution.py:439
  10.8 1.9 %load.1 = (f32[4,2,24,96,128]{4,3,2,1,0:T(8,128)S(1)}, f32[4,24,96,128]{3,2,1,0:T(8,128)S(1)}) custom-call(f32[2,16,64,128]{3,2,1,0:T(8,128)} %rhs.5, f32[3,16,64,128]{3,2,1,0:T(8,128)} %vel.5, f32[16,64,128]{2,1,0:T(8,128)} %diag.5), custom_call_target="tpu_custom_call" | custom-call | tf_op jit(solution)/shard_map/load/pallas_call | solution.py:409
  12.7 0.0 collective-permute-done.2.y0
  12.7 4.4 %collective-permute-done.3.y1 = f32[6,16,8,128]{3,2,1,0:T(8,128)S(1)} collective-permute-done((f32[6,16,8,128]{3,2,1,0:T(8,128)S(1)}, f32[6,16,8,128]{3,2,1,0:T(8,128)S(1)}, u32[]{:S(2)}, u32[]{:S(2)}) %collective-permute-start.3) | collective-permute-done | bytes 393248 | tf_op jit(solution)/shard_map/ppermute | solution.py:439
  17.1 0.1 place_y.1
  17.2 4.8 %collective-permute-start.4 = (f32[48,128]{1,0:T(8,128)S(1)}, f32[48,128]{1,0:T(8,128)S(1)}, u32[]{:S(2)}, u32[]{:S(2)}) collective-permute-start(f32[48,128]{1,0:T(8,128)S(1)} %get-tuple-element.26), channel_id=1, source_target_pairs={{0,8},{16,24},{32,40},{48,56},{64,72},{80,88},{96,104},{112,120},{... | collective-permute-start | bytes 73736 | tf_op jit(solution)/shard_map/ppermute | solution.py:439
  22.0 0.7 collective-permute-start.5
  22.7 6.7 %inner.1 = (f32[4,2,24,96,128]{4,3,2,1,0:T(8,128)S(1)}, f32[2,16,64,128]{3,2,1,0:T(8,128)S(1)}, f32[6,24,96,128]{3,2,1,0:T(8,128)S(1)}, f32[1,128]{1,0:T(1,128)S(1)}) custom-call(f32[4,2,24,96,128]{4,3,2,1,0:T(8,128)S(1)} %get-tuple-element.28.V_in, f32[4,24,96,128]{3,2,1,0:T(8,128)S(1)} %get-tuple-element.29.U.U_in), custom_call_target="tpu_custom_call", output_to_operand_aliasing={{0}: (0, {})} | custom-call | tf_op jit(solution)/shard_map/inner/pallas_call | solution.py:409
  29.4 0.0 collective-permute-done.4.c0
  29.4 0.0 collective-permute-done.5.c1
  29.4 0.0 collective-permute-done.x0
  29.4 0.0 collective-permute-done.1.x1
  29.4 5.4 %outer.1 = (f32[4,2,24,96,128]{4,3,2,1,0:T(8,128)S(1)}, f32[2,16,64,128]{3,2,1,0:T(8,128)S(1)}, f32[6,24,96,128]{3,2,1,0:T(8,128)S(1)}, f32[4,24,96,128]{3,2,1,0:T(8,128)S(1)}, f32[512,128]{1,0:T(8,128)S(1)}) custom-call(f32[20,64,128]{2,1,0:T(8,128)S(1)} %collective-permute-done.x0, ...), custom_call_target="tpu_custom_call", output_to_operand_aliasing={{0}: (5, {}), {1}: (6, {}), {2}: (7, {}), {3}: (8, {})} | custom-call | tf_op jit(solution)/shard_map/outer/pallas_call | solution.py:409
  34.9 29.4 %all_to_all.11 = f32[256,2,128]{2,1,0:T(2,128)S(1)} all-to-all(f32[256,2,128]{2,1,0:T(2,128)S(1)} %bitcast.3), channel_id=1, replica_groups=mesh['gx'=32,'gy'=8] {'gx','gy'}, dimensions={0} | all-to-all | bytes 524288 | tf_op jit(solution)/shard_map/all_to_all | solution.py:484
  64.2 5.4 %combine.1 = (f32[10,16,64,128]{3,2,1,0:T(8,128)}, f32[10,10]{1,0:T(8,128)}, f32[2,16,64,128]{3,2,1,0:T(8,128)}) custom-call(f32[512,128]{1,0:T(8,128)S(1)} %bitcast.2, f32[4,2,24,96,128]{4,3,2,1,0:T(8,128)S(1)} %get-tuple-element.35.V, f32[2,16,64,128]{3,2,1,0:T(8,128)S(1)} %get-tuple-element.36.V4), custom_call_target="tpu_custom_call" | custom-call | tf_op jit(solution)/shard_map/combine/pallas_call | solution.py:409
Async XLA Ops:
  2.1 27.3 %collective-permute-start = (f32[20,64,128]{2,1,0:T(8,128)S(1)}, f32[20,64,128]{2,1,0:T(8,128)S(1)}, u32[]{:S(2)}, u32[]{:S(2)}) collective-permute-start(f32[20,64,128]{2,1,0:T(8,128)S(1)} %get-tuple-element.20), channel_id=1, source_target_pairs={{0,8},{16,24},{32,40},{48,56},{64,72},{80,88},{96,104},{112,120},{... | collective-permute-start | bytes 1966088 | tf_op jit(solution)/shard_map/ppermute | solution.py:439
  4.7 24.7 %collective-permute-start.1 = (f32[20,64,128]{2,1,0:T(8,128)S(1)}, f32[20,64,128]{2,1,0:T(8,128)S(1)}, u32[]{:S(2)}, u32[]{:S(2)}) collective-permute-start(f32[20,64,128]{2,1,0:T(8,128)S(1)} %get-tuple-element.21), channel_id=1, source_target_pairs={{8,16},{24,32},{40,48},{56,64},{72,80},{88,96},{104,112},{120,128}... | collective-permute-start | bytes 1966088 | tf_op jit(solution)/shard_map/ppermute | solution.py:439
  6.6 6.0 %collective-permute-start.2 = (f32[6,16,8,128]{3,2,1,0:T(8,128)S(1)}, f32[6,16,8,128]{3,2,1,0:T(8,128)S(1)}, u32[]{:S(2)}, u32[]{:S(2)}) collective-permute-start(f32[6,16,8,128]{3,2,1,0:T(8,128)S(1)} %get-tuple-element.22), channel_id=1, source_target_pairs={{0,1},{2,3},{4,5},{6,7},{1,0},{3,2},{5,4},{7,6},{8,9},{10,11},{12,... | collective-permute-start | bytes 1179656 | tf_op jit(solution)/shard_map/ppermute | solution.py:439
  7.7 9.4 %collective-permute-start.3 = (f32[6,16,8,128]{3,2,1,0:T(8,128)S(1)}, f32[6,16,8,128]{3,2,1,0:T(8,128)S(1)}, u32[]{:S(2)}, u32[]{:S(2)}) collective-permute-start(f32[6,16,8,128]{3,2,1,0:T(8,128)S(1)} %get-tuple-element.23), channel_id=1, source_target_pairs={{1,2},{3,4},{5,6},{2,1},{4,3},{6,5},{9,10},{11,12},{13,14},{10,9},... | collective-permute-start | bytes 1179656 | tf_op jit(solution)/shard_map/ppermute | solution.py:439
  17.2 12.2 %collective-permute-start.4 = (f32[48,128]{1,0:T(8,128)S(1)}, f32[48,128]{1,0:T(8,128)S(1)}, u32[]{:S(2)}, u32[]{:S(2)}) collective-permute-start(f32[48,128]{1,0:T(8,128)S(1)} %get-tuple-element.26), channel_id=1, source_target_pairs={{0,8},{16,24},{32,40},{48,56},{64,72},{80,88},{96,104},{112,120},{... | collective-permute-start | bytes 73736 | tf_op jit(solution)/shard_map/ppermute | solution.py:439
  22.0 7.3 %collective-permute-start.5 = (f32[48,128]{1,0:T(8,128)S(1)}, f32[48,128]{1,0:T(8,128)S(1)}, u32[]{:S(2)}, u32[]{:S(2)}) collective-permute-start(f32[48,128]{1,0:T(8,128)S(1)} %get-tuple-element.27), channel_id=1, source_target_pairs={{8,16},{24,32},{40,48},{56,64},{72,80},{88,96},{104,112},{120,128}... | collective-permute-start | bytes 73736 | tf_op jit(solution)/shard_map/ppermute | solution.py:439

commit v4 on v3

--- a/solution.py
+++ b/solution.py
@@ -23,20 +23,18 @@
     return (8 * k if k < 8 else 64 + 16 * (k - 8)) + i
 
 
-def run_copies(copies):
-    for copy in copies:
-        copy.start()
-    for copy in copies:
-        copy.wait()
-
-
 def toward_high(axis, pairing):
     return lax.axis_index(axis) % 2 == pairing
 
 
-def pack_x_kernel(X, rhs, vel, diag, first, second, sems):
-    copies = []
-    for pairing, out in enumerate((first, second)):
+def pack_kernel(X, Y, rhs, vel, diag, x0, x1, y0, y1, V, U, sems):
+    own_x, own_y = pl.ds(4, X), pl.ds(YP, Y)
+    copies = [
+        (rhs, V.at[0, :, own_x, own_y]),
+        (vel, U.at[pl.ds(0, 3), own_x, own_y]),
+        (diag, U.at[3, own_x, own_y]),
+    ]
+    for pairing, out in enumerate((x0, x1)):
         high = toward_high("gx", pairing)
         at4, at3 = jnp.where(high, X - 4, 0), jnp.where(high, X - 3, 0)
         for f in range(RHS):
@@ -44,27 +42,21 @@
         for c in range(3):
             copies.append((vel.at[c, pl.ds(at3, 3)], out.at[pl.ds(8 + 3 * c, 3)]))
         copies.append((diag.at[pl.ds(at3, 3)], out.at[pl.ds(17, 3)]))
-    run_copies([pltpu.make_async_copy(s, d, sems.at[i]) for i, (s, d) in enumerate(copies)])
-
-
-def pack_y_kernel(Y, rhs, vel, diag, first, second, sems):
-    copies = []
-    for pairing, out in enumerate((first, second)):
-        at = pl.ds(pl.multiple_of(jnp.where(toward_high("gy", pairing), Y - 8, 0), 8), 8)
-        copies.append((rhs.at[:, :, at], out.at[pl.ds(0, 2)]))
-        copies.append((vel.at[:, :, at], out.at[pl.ds(2, 3)]))
-        copies.append((diag.at[:, at], out.at[5]))
-    run_copies([pltpu.make_async_copy(s, d, sems.at[i]) for i, (s, d) in enumerate(copies)])
-
-
-def load_kernel(X, Y, rhs, vel, diag, V, U, sems):
-    own_x, own_y = pl.ds(4, X), pl.ds(YP, Y)
-    copies = [
-        (rhs, V.at[0, :, own_x, own_y]),
-        (vel, U.at[pl.ds(0, 3), own_x, own_y]),
-        (diag, U.at[3, own_x, own_y]),
-    ]
-    run_copies([pltpu.make_async_copy(s, d, sems.at[i]) for i, (s, d) in enumerate(copies)])
+    copies = [pltpu.make_async_copy(s, d, sems.at[i]) for i, (s, d) in enumerate(copies)]
+    for copy in copies:
+        copy.start()
+    for copy in copies[:3]:
+        copy.wait()
+    first_high = toward_high("gy", 0)
+    for f in range(6):
+        for x in range(X):
+            field = V.at[0, f, 4 + x] if f < 2 else U.at[f - 2, 4 + x]
+            low, high = field[YP : YP + 4, :], field[YP + Y - 4 : YP + Y, :]
+            at = 4 * (f * X + x)
+            y0[at : at + 4, :] = jnp.where(first_high, high, low)
+            y1[at : at + 4, :] = jnp.where(first_high, low, high)
+    for copy in copies[3:]:
+        copy.wait()
 
 
 def corner_cells(X, Y, high, own):
@@ -81,14 +73,14 @@
 
 
 def place_y_kernel(X, Y, y0, y1, V_in, U_in, V, U, first, second):
-    for pairing, got in enumerate((y0, y1)):
-        at = jnp.where(toward_high("gy", pairing), YP + Y, YP - 8)
-        here = pl.ds(pl.multiple_of(at, 8), 8)
+    first_high = toward_high("gy", 0)
+    for f in range(6):
         for x in range(X):
-            for f in range(2):
-                V[0, f, 4 + x, here, :] = got[f, x]
-            for c in range(4):
-                U[c, 4 + x, here, :] = got[2 + c, x]
+            at = 4 * (f * X + x)
+            a, b = y0[at : at + 4, :], y1[at : at + 4, :]
+            field = V.at[0, f, 4 + x] if f < 2 else U.at[f - 2, 4 + x]
+            field[YP - 4 : YP, :] = jnp.where(first_high, b, a)
+            field[YP + Y : YP + Y + 4, :] = jnp.where(first_high, a, b)
     for pairing, out in enumerate((first, second)):
         cells = corner_cells(X, Y, toward_high("gx", pairing), True)
         for row, (f, x, y) in enumerate(cells):
@@ -185,7 +177,7 @@
         return tuple(accs)
 
     count = rows[0][1] - rows[0][0]
-    accs = lax.fori_loop(0, count, first_dots, (zero,) * COLS)
+    accs = lax.fori_loop(0, count, first_dots, (zero,) * COLS, unroll=4)
     lane = lax.broadcasted_iota(jnp.int32, (1, 128), 1)
     line = jnp.zeros((1, 128), F32)
     for j in range(COLS):
@@ -197,8 +189,8 @@
             line = jnp.where(lane == slot(j, k), dots[k - j] * inv, line)
         if j == COLS - 1:
             return line
-        inv2 = inv * inv
-        alphas = [jnp.broadcast_to(d * inv2, (8, 128)) for d in dots[1:]]
+        recip = 1.0 / jnp.where(live, dots[0], 1.0)
+        alphas = [jnp.broadcast_to(d * recip, (8, 128)) for d in dots[1:]]
 
         def get(k, x, at, size, j=j):
             if j == 0 or k == 0:
@@ -221,7 +213,7 @@
                         accs[k - j - 1] = accs[k - j - 1] + fold8(after * value)
             return tuple(accs)
 
-        accs = lax.fori_loop(0, count, sweep, (zero,) * (COLS - 1 - j))
+        accs = lax.fori_loop(0, count, sweep, (zero,) * (COLS - 1 - j), unroll=4)
 
 
 def inner_kernel(X, Y, V_in, U, V, V4, A, line, Q):
@@ -438,20 +430,17 @@
         pairs = [(i, i + 1) for i in range(pairing, size - 1, 2)]
         return lax.ppermute(value, axis, pairs + [(j, i) for i, j in pairs])
 
-    slab = ((20, Y, Z), PIN)
-    x0, x1 = call(
-        functools.partial(pack_x_kernel, X), "pack_x", inputs, [slab, slab], [dma((12,))]
+    v_shape, u_shape = ((S, RHS, XE, YE, Z), PIN), ((4, XE, YE, Z), PIN)
+    x_slab, y_slab = ((20, Y, Z), PIN), ((24 * X, Z), PIN)
+    x0, x1, y0, y1, V, U = call(
+        functools.partial(pack_kernel, X, Y),
+        "pack",
+        inputs,
+        [x_slab, x_slab, y_slab, y_slab, v_shape, u_shape],
+        [dma((15,))],
     )
     x0, x1 = swap(x0, "gx", 0), swap(x1, "gx", 1)
-    slab = ((6, X, 8, Z), PIN)
-    y0, y1 = call(
-        functools.partial(pack_y_kernel, Y), "pack_y", inputs, [slab, slab], [dma((6,))]
-    )
     y1, y0 = swap(y1, "gy", 1), swap(y0, "gy", 0)
-    v_shape, u_shape = ((S, RHS, XE, YE, Z), PIN), ((4, XE, YE, Z), PIN)
-    V, U = call(
-        functools.partial(load_kernel, X, Y), "load", inputs, [v_shape, u_shape], [dma((3,))]
-    )
     strip = ((2 * CORNER_ROWS, Z), PIN)
     V, U, c0, c1 = call(
         functools.partial(place_y_kernel, X, Y),

time: 69.9 us -> 66 us (0.944)
  Pallas kernels: 22.2 us -> 18.6 us
    pallas_call x7 -> x5, Pallas kernels: 22.2 us -> 18.6 us  [call(): pl.pallas_call(kernel, out_shape=tuple((pltpu.VMEM(o, F32) if place == PI...]
  transfers between devices with their start and end apart: 6 -> 6, of which waited for: 1 -> 1; matrix products, arithmetic and copies ran while one was open for 0% -> 0% of each run, Pallas kernels for 14% -> 9%
where the time goes in v4:
time: 66 us; the launch traced here: 65.8 us
  blocking collectives  29.4 us (45%)
  Pallas kernels  18.6 us (28%)
  starting transfers between devices  12.9 us (20%)
  waiting for transfers between devices  4.16 us (6%)
  between operations  0.72 us (1%)
    all_to_all x1, blocking collectives, body(): gathered = lax.all_to_all(packed, ('gx', 'gy'), 0, 0, tiled=True)  29.4 us
    pallas_call x5, Pallas kernels, call(): pl.pallas_call(kernel, out_shape=tuple((pltpu.VMEM(o, F32) if place == PI...  18.6 us
    ppermute x6, starting transfers between devices, swap(): return lax.ppermute(value, axis, pairs + [(j, i) for i, j in pairs])  12.9 us
    ppermute x6, waiting for transfers between devices, swap(): return lax.ppermute(value, axis, pairs + [(j, i) for i, j in pairs])  4.16 us
  transfers between devices with their start and end apart: 6, of which 1 were waited for; matrix products, arithmetic and copies ran while one was open for 0% of the time, Pallas kernels for 9%

profile of v4, /device:TPU:1, one launch (start us, length us, event | category | flops | bytes accessed | tf_op | source)
XLA Modules:
  0.0 65.8 jit_solution(1973135103677989516)
XLA Ops:
  0.6 2.3 %pack.1 = (f32[20,64,128]{2,1,0:T(8,128)S(1)}, f32[20,64,128]{2,1,0:T(8,128)S(1)}, f32[384,128]{1,0:T(8,128)S(1)}, f32[384,128]{1,0:T(8,128)S(1)}, f32[4,2,24,96...) custom-call(f32[2,16,64,128]{3,2,1,0:T(8,128)} %rhs.1, f32[3,16,64,128]{3,2,1,0:T(8,128)} %vel.1, f32[16,64,128]{2,1,0:T(8,128)} %diag.1), custom_call_target="tpu_custom_call" | custom-call | tf_op jit(solution)/shard_map/pack/pallas_call | solution.py:401
  3.0 2.6 %collective-permute-start = (f32[20,64,128]{2,1,0:T(8,128)S(1)}, f32[20,64,128]{2,1,0:T(8,128)S(1)}, u32[]{:S(2)}, u32[]{:S(2)}) collective-permute-start(f32[20,64,128]{2,1,0:T(8,128)S(1)} %get-tuple-element.20), channel_id=1, source_target_pairs={{0,8},{16,24},{32,40},{48,56},{64,72},{80,88},{96,104},{112,120},{... | collective-permute-start | bytes 1966088 | tf_op jit(solution)/shard_map/ppermute | solution.py:431
  5.5 0.7 %collective-permute-start.1 = (f32[20,64,128]{2,1,0:T(8,128)S(1)}, f32[20,64,128]{2,1,0:T(8,128)S(1)}, u32[]{:S(2)}, u32[]{:S(2)}) collective-permute-start(f32[20,64,128]{2,1,0:T(8,128)S(1)} %get-tuple-element.21), channel_id=1, source_target_pairs={{8,16},{24,32},{40,48},{56,64},{72,80},{88,96},{104,112},{120,128}... | collective-permute-start | bytes 1966088 | tf_op jit(solution)/shard_map/ppermute | solution.py:431
  6.2 1.0 %collective-permute-start.2 = (f32[384,128]{1,0:T(8,128)S(1)}, f32[384,128]{1,0:T(8,128)S(1)}, u32[]{:S(2)}, u32[]{:S(2)}) collective-permute-start(f32[384,128]{1,0:T(8,128)S(1)} %get-tuple-element.22), channel_id=1, source_target_pairs={{0,1},{2,3},{4,5},{6,7},{1,0},{3,2},{5,4},{7,6},{8,9},{10,11},{12,... | collective-permute-start | bytes 589832 | tf_op jit(solution)/shard_map/ppermute | solution.py:431
  7.3 3.1 %collective-permute-start.3 = (f32[384,128]{1,0:T(8,128)S(1)}, f32[384,128]{1,0:T(8,128)S(1)}, u32[]{:S(2)}, u32[]{:S(2)}) collective-permute-start(f32[384,128]{1,0:T(8,128)S(1)} %get-tuple-element.23), channel_id=1, source_target_pairs={{1,2},{3,4},{5,6},{2,1},{4,3},{6,5},{9,10},{11,12},{13,14},{10,9},... | collective-permute-start | bytes 589832 | tf_op jit(solution)/shard_map/ppermute | solution.py:431
  10.4 0.0 collective-permute-done.2.y0
  10.4 4.2 %collective-permute-done.3.y1 = f32[384,128]{1,0:T(8,128)S(1)} collective-permute-done((f32[384,128]{1,0:T(8,128)S(1)}, f32[384,128]{1,0:T(8,128)S(1)}, u32[]{:S(2)}, u32[]{:S(2)}) %collective-permute-start.3) | collective-permute-done | bytes 196640 | tf_op jit(solution)/shard_map/ppermute | solution.py:431
  14.5 0.1 place_y.1
  14.7 4.8 %collective-permute-start.4 = (f32[48,128]{1,0:T(8,128)S(1)}, f32[48,128]{1,0:T(8,128)S(1)}, u32[]{:S(2)}, u32[]{:S(2)}) collective-permute-start(f32[48,128]{1,0:T(8,128)S(1)} %get-tuple-element.26), channel_id=1, source_target_pairs={{0,8},{16,24},{32,40},{48,56},{64,72},{80,88},{96,104},{112,120},{... | collective-permute-start | bytes 73736 | tf_op jit(solution)/shard_map/ppermute | solution.py:431
  19.5 0.7 collective-permute-start.5
  20.2 6.0 %inner.1 = (f32[4,2,24,96,128]{4,3,2,1,0:T(8,128)S(1)}, f32[2,16,64,128]{3,2,1,0:T(8,128)S(1)}, f32[6,24,96,128]{3,2,1,0:T(8,128)S(1)}, f32[1,128]{1,0:T(1,128)S(1)}) custom-call(f32[4,2,24,96,128]{4,3,2,1,0:T(8,128)S(1)} %get-tuple-element.28.V_in, f32[4,24,96,128]{3,2,1,0:T(8,128)S(1)} %get-tuple-element.29.U.U_in), custom_call_target="tpu_custom_call", output_to_operand_aliasing={{0}: (0, {})} | custom-call | tf_op jit(solution)/shard_map/inner/pallas_call | solution.py:401
  26.2 0.0 collective-permute-done.4.c0
  26.2 0.0 collective-permute-done.5.c1
  26.2 0.0 collective-permute-done.x0
  26.2 0.0 collective-permute-done.1.x1
  26.2 4.7 %outer.1 = (f32[4,2,24,96,128]{4,3,2,1,0:T(8,128)S(1)}, f32[2,16,64,128]{3,2,1,0:T(8,128)S(1)}, f32[6,24,96,128]{3,2,1,0:T(8,128)S(1)}, f32[4,24,96,128]{3,2,1,0:T(8,128)S(1)}, f32[512,128]{1,0:T(8,128)S(1)}) custom-call(f32[20,64,128]{2,1,0:T(8,128)S(1)} %collective-permute-done.x0, ...), custom_call_target="tpu_custom_call", output_to_operand_aliasing={{0}: (5, {}), {1}: (6, {}), {2}: (7, {}), {3}: (8, {})} | custom-call | tf_op jit(solution)/shard_map/outer/pallas_call | solution.py:401
  31.0 29.4 %all_to_all.11 = f32[256,2,128]{2,1,0:T(2,128)S(1)} all-to-all(f32[256,2,128]{2,1,0:T(2,128)S(1)} %bitcast.3), channel_id=1, replica_groups=mesh['gx'=32,'gy'=8] {'gx','gy'}, dimensions={0} | all-to-all | bytes 524288 | tf_op jit(solution)/shard_map/all_to_all | solution.py:473
  60.4 5.4 %combine.1 = (f32[10,16,64,128]{3,2,1,0:T(8,128)}, f32[10,10]{1,0:T(8,128)}, f32[2,16,64,128]{3,2,1,0:T(8,128)}) custom-call(f32[512,128]{1,0:T(8,128)S(1)} %bitcast.2, f32[4,2,24,96,128]{4,3,2,1,0:T(8,128)S(1)} %get-tuple-element.35.V, f32[2,16,64,128]{3,2,1,0:T(8,128)S(1)} %get-tuple-element.36.V4), custom_call_target="tpu_custom_call" | custom-call | tf_op jit(solution)/shard_map/combine/pallas_call | solution.py:401
Async XLA Ops:
  3.0 23.2 %collective-permute-start = (f32[20,64,128]{2,1,0:T(8,128)S(1)}, f32[20,64,128]{2,1,0:T(8,128)S(1)}, u32[]{:S(2)}, u32[]{:S(2)}) collective-permute-start(f32[20,64,128]{2,1,0:T(8,128)S(1)} %get-tuple-element.20), channel_id=1, source_target_pairs={{0,8},{16,24},{32,40},{48,56},{64,72},{80,88},{96,104},{112,120},{... | collective-permute-start | bytes 1966088 | tf_op jit(solution)/shard_map/ppermute | solution.py:431
  5.5 20.7 %collective-permute-start.1 = (f32[20,64,128]{2,1,0:T(8,128)S(1)}, f32[20,64,128]{2,1,0:T(8,128)S(1)}, u32[]{:S(2)}, u32[]{:S(2)}) collective-permute-start(f32[20,64,128]{2,1,0:T(8,128)S(1)} %get-tuple-element.21), channel_id=1, source_target_pairs={{8,16},{24,32},{40,48},{56,64},{72,80},{88,96},{104,112},{120,128}... | collective-permute-start | bytes 1966088 | tf_op jit(solution)/shard_map/ppermute | solution.py:431
  6.2 4.2 %collective-permute-start.2 = (f32[384,128]{1,0:T(8,128)S(1)}, f32[384,128]{1,0:T(8,128)S(1)}, u32[]{:S(2)}, u32[]{:S(2)}) collective-permute-start(f32[384,128]{1,0:T(8,128)S(1)} %get-tuple-element.22), channel_id=1, source_target_pairs={{0,1},{2,3},{4,5},{6,7},{1,0},{3,2},{5,4},{7,6},{8,9},{10,11},{12,... | collective-permute-start | bytes 589832 | tf_op jit(solution)/shard_map/ppermute | solution.py:431
  7.3 7.3 %collective-permute-start.3 = (f32[384,128]{1,0:T(8,128)S(1)}, f32[384,128]{1,0:T(8,128)S(1)}, u32[]{:S(2)}, u32[]{:S(2)}) collective-permute-start(f32[384,128]{1,0:T(8,128)S(1)} %get-tuple-element.23), channel_id=1, source_target_pairs={{1,2},{3,4},{5,6},{2,1},{4,3},{6,5},{9,10},{11,12},{13,14},{10,9},... | collective-permute-start | bytes 589832 | tf_op jit(solution)/shard_map/ppermute | solution.py:431
  14.7 11.5 %collective-permute-start.4 = (f32[48,128]{1,0:T(8,128)S(1)}, f32[48,128]{1,0:T(8,128)S(1)}, u32[]{:S(2)}, u32[]{:S(2)}) collective-permute-start(f32[48,128]{1,0:T(8,128)S(1)} %get-tuple-element.26), channel_id=1, source_target_pairs={{0,8},{16,24},{32,40},{48,56},{64,72},{80,88},{96,104},{112,120},{... | collective-permute-start | bytes 73736 | tf_op jit(solution)/shard_map/ppermute | solution.py:431
  19.5 6.7 %collective-permute-start.5 = (f32[48,128]{1,0:T(8,128)S(1)}, f32[48,128]{1,0:T(8,128)S(1)}, u32[]{:S(2)}, u32[]{:S(2)}) collective-permute-start(f32[48,128]{1,0:T(8,128)S(1)} %get-tuple-element.27), channel_id=1, source_target_pairs={{8,16},{24,32},{40,48},{56,64},{72,80},{88,96},{104,112},{120,128}... | collective-permute-start | bytes 73736 | tf_op jit(solution)/shard_map/ppermute | solution.py:431

commit v5 on v4

--- a/solution.py
+++ b/solution.py
@@ -19,8 +19,32 @@
 CORNER_ROWS = RHS * len(FIELD_CORNER) + 4 * len(COEF_CORNER)
 
 
-def slot(i, k):
-    return (8 * k if k < 8 else 64 + 16 * (k - 8)) + i
+def slot(leaf, i, k):
+    if i >= 8:
+        return 104 + 3 * leaf + (k - 8) + (i - 8)
+    if k >= 8:
+        return 72 + 16 * leaf + 8 * (k - 8) + i
+    if k == 7:
+        return 56 + 8 * leaf + i
+    return 8 * (6 - k) + 7 - k + i if leaf else 8 * k + i
+
+
+def unpack(g, leaf):
+    row = lax.broadcasted_iota(jnp.int32, (8, g.shape[1]), 0)
+
+    def rows(first, count):
+        group = g[8 * (first // 8) : 8 * (first // 8) + 8]
+        if first % 8:
+            group = pltpu.roll(group, 8 - first % 8, 0)
+        return group if count == 8 else jnp.where(row < count, group, 0.0)
+
+    cols = []
+    for k in range(COLS):
+        parts = [rows(slot(leaf, 0, k), min(k + 1, 8))]
+        if k >= 8:
+            parts.append(rows(slot(leaf, 8, k), k - 7))
+        cols.append(parts)
+    return cols
 
 
 def toward_high(axis, pairing):
@@ -34,19 +58,20 @@
         (vel, U.at[pl.ds(0, 3), own_x, own_y]),
         (diag, U.at[3, own_x, own_y]),
     ]
-    for pairing, out in enumerate((x0, x1)):
-        high = toward_high("gx", pairing)
-        at4, at3 = jnp.where(high, X - 4, 0), jnp.where(high, X - 3, 0)
-        for f in range(RHS):
-            copies.append((rhs.at[f, pl.ds(at4, 4)], out.at[pl.ds(4 * f, 4)]))
-        for c in range(3):
-            copies.append((vel.at[c, pl.ds(at3, 3)], out.at[pl.ds(8 + 3 * c, 3)]))
-        copies.append((diag.at[pl.ds(at3, 3)], out.at[pl.ds(17, 3)]))
     copies = [pltpu.make_async_copy(s, d, sems.at[i]) for i, (s, d) in enumerate(copies)]
     for copy in copies:
         copy.start()
-    for copy in copies[:3]:
+    for copy in copies:
         copy.wait()
+    for pairing, out in enumerate((x0, x1)):
+        high = toward_high("gx", pairing)
+        at4, at3 = jnp.where(high, X, 4), jnp.where(high, X + 1, 4)
+        for i in range(4):
+            for f in range(RHS):
+                out[4 * f + i] = V[0, f, at4 + i, YP : YP + Y, :]
+        for i in range(3):
+            for c in range(4):
+                out[8 + 3 * c + i] = U[c, at3 + i, YP : YP + Y, :]
     first_high = toward_high("gy", 0)
     for f in range(6):
         for x in range(X):
@@ -55,8 +80,6 @@
             at = 4 * (f * X + x)
             y0[at : at + 4, :] = jnp.where(first_high, high, low)
             y1[at : at + 4, :] = jnp.where(first_high, low, high)
-    for copy in copies[3:]:
-        copy.wait()
 
 
 def corner_cells(X, Y, high, own):
@@ -103,26 +126,25 @@
     return parts[0]
 
 
-def coefficient_rows(X, Y, U, A, rows):
+def coefficient_rows(X, Y, U, A, rows, begin, size):
     gx, gy = lax.axis_index("gx"), lax.axis_index("gy")
     nx, ny = lax.axis_size("gx"), lax.axis_size("gy")
-    WIDE = Y + 16
-    inner = pl.ds(YP - 8, WIDE)
-    yi = lax.broadcasted_iota(jnp.int32, (WIDE, 128), 0)
-    zi = lax.broadcasted_iota(jnp.int32, (WIDE, 128), 1)
-    y_in = ((yi >= 8) | (gy > 0)) & ((yi < Y + 8) | (gy < ny - 1))
+    here = pl.ds(begin, size)
+    yi = begin + lax.broadcasted_iota(jnp.int32, (size, 128), 0)
+    zi = lax.broadcasted_iota(jnp.int32, (size, 128), 1)
+    y_in = ((yi >= YP) | (gy > 0)) & ((yi < Y + YP) | (gy < ny - 1))
 
     def one(x):
         x_in = ((x >= 4) | (gx > 0)) & ((x < X + 4) | (gx < nx - 1))
-        g = jnp.where(y_in & x_in, 1.0 / (6.0 + U[3, x, inner, :]), 0.0)
+        g = jnp.where(y_in & x_in, 1.0 / (6.0 + U[3, x, here, :]), 0.0)
         for c in range(3):
-            ug = U[c, x, inner, :] * g
+            ug = U[c, x, here, :] * g
             plus, minus = g + ug, g - ug
             if c == 2:
                 plus = jnp.where(zi == 0, 0.0, plus)
                 minus = jnp.where(zi == 127, 0.0, minus)
-            A[2 * c, x, inner, :] = plus
-            A[2 * c + 1, x, inner, :] = minus
+            A[2 * c, x, here, :] = plus
+            A[2 * c + 1, x, here, :] = minus
 
     for_rows(rows, one, 2)
 
@@ -136,22 +158,21 @@
     lax.fori_loop(0, rows[0][1] - rows[0][0], run, 0, unroll=unroll)
 
 
-def power_rows(Y, V, V4, A, k, rows, unroll):
-    begin, size = (YP, Y) if k == S else (YP - 8, Y + 16)
-    here = pl.ds(begin, size)
-
+def power_rows(V, V4, A, k, rows, pieces, unroll):
     def one(x):
-        a = [A[c, x, here, :] for c in range(6)]
-        for f in range(RHS):
-            centre = V[k - 1, f, x, here, :]
-            value = a[4] * pltpu.roll(centre, 1, 1) + a[5] * pltpu.roll(centre, 127, 1)
-            value += a[0] * V[k - 1, f, x - 1, here, :] + a[1] * V[k - 1, f, x + 1, here, :]
-            value += a[2] * V[k - 1, f, x, pl.ds(begin - 1, size), :]
-            value += a[3] * V[k - 1, f, x, pl.ds(begin + 1, size), :]
-            if k == S:
-                V4[f, x - 4] = value
-            else:
-                V[k, f, x, here, :] = value
+        for begin, size in pieces:
+            here = pl.ds(begin, size)
+            a = [A[c, x, here, :] for c in range(6)]
+            for f in range(RHS):
+                centre = V[k - 1, f, x, here, :]
+                value = a[4] * pltpu.roll(centre, 1, 1) + a[5] * pltpu.roll(centre, 127, 1)
+                value += a[0] * V[k - 1, f, x - 1, here, :] + a[1] * V[k - 1, f, x + 1, here, :]
+                value += a[2] * V[k - 1, f, x, pl.ds(begin - 1, size), :]
+                value += a[3] * V[k - 1, f, x, pl.ds(begin + 1, size), :]
+                if k == S:
+                    V4[f, x - 4, pl.ds(begin - YP, size), :] = value
+                else:
+                    V[k, f, x, here, :] = value
 
     for_rows(rows, one, unroll)
 
@@ -162,21 +183,18 @@
     return V[k // RHS, k % RHS, x + 4, pl.ds(YP + at, size), :]
 
 
-def local_factor(Y, V, V4, Q, rows):
-    CH = 32
+def local_factor(V, V4, Q, leaf, count, pieces):
     zero = jnp.zeros((8, 128), F32)
 
     def first_dots(i, accs):
         accs = list(accs)
-        for first, _ in rows:
-            x = first + i
-            for at in range(0, Y, CH):
-                q = basis_rows(V, V4, 0, x, at, CH)
-                for k in range(COLS):
-                    accs[k] = accs[k] + fold8(q * basis_rows(V, V4, k, x, at, CH))
+        for row, at, size in pieces:
+            x = row + i
+            q = basis_rows(V, V4, 0, x, at, size)
+            for k in range(COLS):
+                accs[k] = accs[k] + fold8(q * basis_rows(V, V4, k, x, at, size))
         return tuple(accs)
 
-    count = rows[0][1] - rows[0][0]
     accs = lax.fori_loop(0, count, first_dots, (zero,) * COLS, unroll=4)
     lane = lax.broadcasted_iota(jnp.int32, (1, 128), 1)
     line = jnp.zeros((1, 128), F32)
@@ -186,7 +204,7 @@
         length = jnp.sqrt(jnp.where(live, dots[0], 1.0))
         inv = jnp.where(live, 1.0 / length, 0.0)
         for k in range(j, COLS):
-            line = jnp.where(lane == slot(j, k), dots[k - j] * inv, line)
+            line = jnp.where(lane == slot(leaf, j, k), dots[k - j] * inv, line)
         if j == COLS - 1:
             return line
         recip = 1.0 / jnp.where(live, dots[0], 1.0)
@@ -199,28 +217,38 @@
 
         def sweep(i, accs, j=j, get=get, alphas=alphas):
             accs = list(accs)
-            for first, _ in rows:
-                x = first + i
-                for at in range(0, Y, CH):
-                    q = get(j, x, at, CH)
-                    after = None
-                    for k in range(j + 1, COLS):
-                        alpha = jnp.concatenate([alphas[k - j - 1]] * (CH // 8), axis=0)
-                        value = get(k, x, at, CH) - alpha * q
-                        Q[k - 1, x, pl.ds(at, CH), :] = value
-                        if k == j + 1:
-                            after = value
-                        accs[k - j - 1] = accs[k - j - 1] + fold8(after * value)
+            for row, at, size in pieces:
+                x = row + i
+                q = get(j, x, at, size)
+                after = None
+                for k in range(j + 1, COLS):
+                    alpha = jnp.concatenate([alphas[k - j - 1]] * (size // 8), axis=0)
+                    value = get(k, x, at, size) - alpha * q
+                    Q[k - 1, x, pl.ds(at, size), :] = value
+                    if k == j + 1:
+                        after = value
+                    accs[k - j - 1] = accs[k - j - 1] + fold8(after * value)
             return tuple(accs)
 
         accs = lax.fori_loop(0, count, sweep, (zero,) * (COLS - 1 - j), unroll=4)
 
 
 def inner_kernel(X, Y, V_in, U, V, V4, A, line, Q):
-    coefficient_rows(X, Y, U, A, [(4, X + 4)])
+    coefficient_rows(X, Y, U, A, [(4, X + 4)], YP, Y)
     for k in range(1, S + 1):
-        power_rows(Y, V, V4, A, k, [(4 + k, X + 4 - k)], 4)
-    line[...] = local_factor(Y, V, V4, Q, [(4, X // 2), (X // 2, X - 4)])
+        power_rows(V, V4, A, k, [(4 + k, X + 4 - k)], [(YP, Y)], 4)
+    half = (Y - 16) // 2
+    pieces = [(row, at, half) for row in (4, X // 2) for at in (8, 8 + half)]
+    line[...] = local_factor(V, V4, Q, 0, X // 2 - 4, pieces)
+
+
+def edge_kernel(X, Y, U, V_in, V4_in, A_in, V, V4, A):
+    for begin in (YP - 8, YP + Y):
+        coefficient_rows(X, Y, U, A, [(4, X + 4)], begin, 8)
+    for k in range(1, S):
+        pieces = [(YP - 8, 16), (YP + Y - 8, 16)]
+        power_rows(V, V4, A, k, [(4 + k, X + 4 - k)], pieces, 4)
+    power_rows(V, V4, A, S, [(4 + S, X + 4 - S)], [(YP, 8), (YP + Y - 8, 8)], 4)
 
 
 def outer_kernel(X, Y, x0, x1, c0, c1, inner_line, V_in, V4_in, A_in, U_in, V, V4, A, U, packed, Q):
@@ -239,13 +267,14 @@
                 V[0, f, x, y : y + 1, :] = corner[row : row + 1, :]
             else:
                 U[f - 2, x, y : y + 1, :] = corner[row : row + 1, :]
-    coefficient_rows(X, Y, U, A, [(1, 4), (X + 4, X + 7)])
+    coefficient_rows(X, Y, U, A, [(1, 4), (X + 4, X + 7)], YP - 8, Y + 16)
     for k in range(1, S + 1):
-        power_rows(Y, V, V4, A, k, [(k, k + 4), (X + 4 - k, X + 8 - k)], 2)
-    line = local_factor(Y, V, V4, Q, [(0, 4), (X - 4, X)])
-    row = lax.broadcasted_iota(jnp.int32, (8, 128), 0)
-    both = jnp.where(row % 2 == 0, inner_line[...], line)
-    packed[...] = jnp.concatenate([both] * (packed.shape[0] // 8), axis=0)
+        piece = (YP - 8, Y + 16) if k < S else (YP, Y)
+        power_rows(V, V4, A, k, [(k, k + 4), (X + 4 - k, X + 8 - k)], [piece], 2)
+    pieces = [(row, at, Y // 2) for row in (0, X - 4) for at in (0, Y // 2)]
+    pieces += [(row, at, 8) for row in (4, X // 2) for at in (0, Y - 8)]
+    line = local_factor(V, V4, Q, 1, 4, pieces)
+    packed[...] = jnp.broadcast_to(inner_line[...] + line, packed.shape)
 
 
 def fold_lanes(x):
@@ -255,13 +284,10 @@
 
 def merged_factor(gathered):
     g = gathered.T
-    cols = []
-    for k in range(COLS):
-        if k < 8:
-            cols.append([g[8 * k : 8 * k + 8]])
-        else:
-            at = 64 + 16 * (k - 8)
-            cols.append([g[at : at + 8], g[at + 8 : at + 16]])
+    cols = [
+        [jnp.concatenate(parts, axis=1) for parts in zip(*pair)]
+        for pair in zip(unpack(g, 0), unpack(g, 1))
+    ]
     R = {}
     for j in range(COLS):
         dots = []
@@ -273,9 +299,9 @@
         inv = 1.0 / jnp.sqrt(dots[0])
         for k in range(j, COLS):
             R[j, k] = dots[k - j] * inv
-        inv2 = inv * inv
+        recip = 1.0 / dots[0]
         for k in range(j + 1, COLS):
-            alpha = dots[k - j] * inv2
+            alpha = dots[k - j] * recip
             for part in range(len(cols[j])):
                 cols[k][part] = cols[k][part] - alpha * cols[j][part]
     return R
@@ -437,19 +463,10 @@
         "pack",
         inputs,
         [x_slab, x_slab, y_slab, y_slab, v_shape, u_shape],
-        [dma((15,))],
+        [dma((3,))],
     )
     x0, x1 = swap(x0, "gx", 0), swap(x1, "gx", 1)
     y1, y0 = swap(y1, "gy", 1), swap(y0, "gy", 0)
-    strip = ((2 * CORNER_ROWS, Z), PIN)
-    V, U, c0, c1 = call(
-        functools.partial(place_y_kernel, X, Y),
-        "place_y",
-        [(y0, PIN), (y1, PIN), (V, PIN), (U, PIN)],
-        [v_shape, u_shape, strip, strip],
-        aliases={2: 0, 3: 1},
-    )
-    c0, c1 = swap(c0, "gx", 0), swap(c1, "gx", 1)
     v4_shape, a_shape = ((RHS, X, Y, Z), PIN), ((6, XE, YE, Z), PIN)
     work = pltpu.VMEM((COLS - 1, X, Y, Z), F32)
     V, V4, A, line = call(
@@ -461,11 +478,27 @@
         aliases={0: 0},
         limit=8,
     )
+    strip = ((2 * CORNER_ROWS, Z), PIN)
+    V, U, c0, c1 = call(
+        functools.partial(place_y_kernel, X, Y),
+        "place_y",
+        [(y0, PIN), (y1, PIN), (V, PIN), (U, PIN)],
+        [v_shape, u_shape, strip, strip],
+        aliases={2: 0, 3: 1},
+    )
+    c0, c1 = swap(c0, "gx", 0), swap(c1, "gx", 1)
+    V, V4, A = call(
+        functools.partial(edge_kernel, X, Y),
+        "edge",
+        [(a, PIN) for a in (U, V, V4, A)],
+        [v_shape, v4_shape, a_shape],
+        aliases={1: 0, 2: 1, 3: 2},
+    )
     V, V4, A, U, packed = call(
         functools.partial(outer_kernel, X, Y),
         "outer",
         [(a, PIN) for a in (x0, x1, c0, c1, line, V, V4, A, U)],
-        [v_shape, v4_shape, a_shape, u_shape, ((2 * devices, 128), BLOCK)],
+        [v_shape, v4_shape, a_shape, u_shape, ((devices, 128), BLOCK)],
         [work],
         aliases={5: 0, 6: 1, 7: 2, 8: 3},
         limit=8,

time: 66 us -> 62.5 us (0.947)
  waiting for transfers between devices: 4.16 us -> 0.02 us
  Pallas kernels: 18.6 us -> 19.3 us
    ppermute x6, waiting for transfers between devices: 4.16 us -> 0.02 us  [swap(): return lax.ppermute(value, axis, pairs + [(j, i) for i, j in pairs])]
    pallas_call x5 -> x6, Pallas kernels: 18.6 us -> 19.3 us  [call(): pl.pallas_call(kernel, out_shape=tuple((pltpu.VMEM(o, F32) if place == PI...]
  transfers between devices with their start and end apart: 6 -> 6, of which waited for: 1 -> 0; matrix products, arithmetic and copies ran while one was open for 0% -> 0% of each run, Pallas kernels for 9% -> 11%
where the time goes in v5:
time: 62.5 us; the launch traced here: 62.3 us
  blocking collectives  29.4 us (47%)
  Pallas kernels  19.3 us (31%)
  starting transfers between devices  12.9 us (21%)
  between operations  0.73 us (1%)
    all_to_all x1, blocking collectives, body(): gathered = lax.all_to_all(packed, ('gx', 'gy'), 0, 0, tiled=True)  29.4 us
    pallas_call x6, Pallas kernels, call(): pl.pallas_call(kernel, out_shape=tuple((pltpu.VMEM(o, F32) if place == PI...  19.3 us
    ppermute x6, starting transfers between devices, swap(): return lax.ppermute(value, axis, pairs + [(j, i) for i, j in pairs])  12.9 us
  transfers between devices with their start and end apart: 6, of which 0 were waited for; matrix products, arithmetic and copies ran while one was open for 0% of the time, Pallas kernels for 11%

profile of v5, /device:TPU:1, one launch (start us, length us, event | category | flops | bytes accessed | tf_op | source)
XLA Modules:
  0.0 62.3 jit_solution(7192252597741498064)
XLA Ops:
  0.6 2.0 %pack.1 = (f32[20,64,128]{2,1,0:T(8,128)S(1)}, f32[20,64,128]{2,1,0:T(8,128)S(1)}, f32[384,128]{1,0:T(8,128)S(1)}, f32[384,128]{1,0:T(8,128)S(1)}, f32[4,2,24,96...) custom-call(f32[2,16,64,128]{3,2,1,0:T(8,128)} %rhs.1, f32[3,16,64,128]{3,2,1,0:T(8,128)} %vel.1, f32[16,64,128]{2,1,0:T(8,128)} %diag.1), custom_call_target="tpu_custom_call" | custom-call | tf_op jit(solution)/shard_map/pack/pallas_call | solution.py:427
  2.7 2.6 %collective-permute-start = (f32[20,64,128]{2,1,0:T(8,128)S(1)}, f32[20,64,128]{2,1,0:T(8,128)S(1)}, u32[]{:S(2)}, u32[]{:S(2)}) collective-permute-start(f32[20,64,128]{2,1,0:T(8,128)S(1)} %get-tuple-element.23), channel_id=1, source_target_pairs={{0,8},{16,24},{32,40},{48,56},{64,72},{80,88},{96,104},{112,120},{... | collective-permute-start | bytes 1966088 | tf_op jit(solution)/shard_map/ppermute | solution.py:457
  5.2 0.7 %collective-permute-start.1 = (f32[20,64,128]{2,1,0:T(8,128)S(1)}, f32[20,64,128]{2,1,0:T(8,128)S(1)}, u32[]{:S(2)}, u32[]{:S(2)}) collective-permute-start(f32[20,64,128]{2,1,0:T(8,128)S(1)} %get-tuple-element.24), channel_id=1, source_target_pairs={{8,16},{24,32},{40,48},{56,64},{72,80},{88,96},{104,112},{120,128}... | collective-permute-start | bytes 1966088 | tf_op jit(solution)/shard_map/ppermute | solution.py:457
  5.9 1.0 %collective-permute-start.2 = (f32[384,128]{1,0:T(8,128)S(1)}, f32[384,128]{1,0:T(8,128)S(1)}, u32[]{:S(2)}, u32[]{:S(2)}) collective-permute-start(f32[384,128]{1,0:T(8,128)S(1)} %get-tuple-element.25), channel_id=1, source_target_pairs={{0,1},{2,3},{4,5},{6,7},{1,0},{3,2},{5,4},{7,6},{8,9},{10,11},{12,... | collective-permute-start | bytes 589832 | tf_op jit(solution)/shard_map/ppermute | solution.py:457
  6.9 3.1 %collective-permute-start.3 = (f32[384,128]{1,0:T(8,128)S(1)}, f32[384,128]{1,0:T(8,128)S(1)}, u32[]{:S(2)}, u32[]{:S(2)}) collective-permute-start(f32[384,128]{1,0:T(8,128)S(1)} %get-tuple-element.26), channel_id=1, source_target_pairs={{1,2},{3,4},{5,6},{2,1},{4,3},{6,5},{9,10},{11,12},{13,14},{10,9},... | collective-permute-start | bytes 589832 | tf_op jit(solution)/shard_map/ppermute | solution.py:457
  10.1 4.8 %inner.1 = (f32[4,2,24,96,128]{4,3,2,1,0:T(8,128)S(1)}, f32[2,16,64,128]{3,2,1,0:T(8,128)S(1)}, f32[6,24,96,128]{3,2,1,0:T(8,128)S(1)}, f32[1,128]{1,0:T(1,128)S(1)}) custom-call(f32[4,2,24,96,128]{4,3,2,1,0:T(8,128)S(1)} %get-tuple-element.27.V_in, f32[4,24,96,128]{3,2,1,0:T(8,128)S(1)} %get-tuple-element.28.U.U_in), custom_call_target="tpu_custom_call", output_to_operand_aliasing={{0}: (0, {})} | custom-call | tf_op jit(solution)/shard_map/inner/pallas_call | solution.py:427
  14.8 0.0 collective-permute-done.2.y0
  14.9 0.0 collective-permute-done.3.y1
  14.9 0.1 place_y.1
  15.0 4.8 %collective-permute-start.4 = (f32[48,128]{1,0:T(8,128)S(1)}, f32[48,128]{1,0:T(8,128)S(1)}, u32[]{:S(2)}, u32[]{:S(2)}) collective-permute-start(f32[48,128]{1,0:T(8,128)S(1)} %get-tuple-element.30), channel_id=1, source_target_pairs={{0,8},{16,24},{32,40},{48,56},{64,72},{80,88},{96,104},{112,120},{... | collective-permute-start | bytes 73736 | tf_op jit(solution)/shard_map/ppermute | solution.py:457
  19.8 0.7 %collective-permute-start.5 = (f32[48,128]{1,0:T(8,128)S(1)}, f32[48,128]{1,0:T(8,128)S(1)}, u32[]{:S(2)}, u32[]{:S(2)}) collective-permute-start(f32[48,128]{1,0:T(8,128)S(1)} %get-tuple-element.31), channel_id=1, source_target_pairs={{8,16},{24,32},{40,48},{56,64},{72,80},{88,96},{104,112},{120,128}... | collective-permute-start | bytes 73736 | tf_op jit(solution)/shard_map/ppermute | solution.py:457
  20.5 2.0 %edge.1 = (f32[4,2,24,96,128]{4,3,2,1,0:T(8,128)S(1)}, f32[2,16,64,128]{3,2,1,0:T(8,128)S(1)}, f32[6,24,96,128]{3,2,1,0:T(8,128)S(1)}) custom-call(f32[4,24,96,128]{3,2,1,0:T(8,128)S(1)} %get-tuple-element.33.U.U_in, f32[4,2,24,96,128]{4,3,2,1,0:T(8,128)S(1)} %get-tuple-element.34.V_in, ...), custom_call_target="tpu_custom_call", output_to_operand_aliasing={{0}: (1, {}), {1}: (2, {}), {2}: (3, {})} | custom-call | tf_op jit(solution)/shard_map/edge/pallas_call | solution.py:427
  22.5 0.0 collective-permute-done.4.c0
  22.5 0.0 collective-permute-done.5.c1
  22.5 0.0 collective-permute-done.x0
  22.5 0.0 collective-permute-done.1.x1
  22.5 5.1 %outer.1 = (f32[4,2,24,96,128]{4,3,2,1,0:T(8,128)S(1)}, f32[2,16,64,128]{3,2,1,0:T(8,128)S(1)}, f32[6,24,96,128]{3,2,1,0:T(8,128)S(1)}, f32[4,24,96,128]{3,2,1,0:T(8,128)S(1)}, f32[256,128]{1,0:T(8,128)S(1)}) custom-call(f32[20,64,128]{2,1,0:T(8,128)S(1)} %collective-permute-done.x0, ...), custom_call_target="tpu_custom_call", output_to_operand_aliasing={{0}: (5, {}), {1}: (6, {}), {2}: (7, {}), {3}: (8, {})} | custom-call | tf_op jit(solution)/shard_map/outer/pallas_call | solution.py:427
  27.6 29.4 %all_to_all.11 = f32[256,1,128]{2,1,0:T(1,128)S(1)} all-to-all(f32[256,1,128]{2,1,0:T(1,128)S(1)} %bitcast.5), channel_id=1, replica_groups=mesh['gx'=32,'gy'=8] {'gx','gy'}, dimensions={0} | all-to-all | bytes 262144 | tf_op jit(solution)/shard_map/all_to_all | solution.py:506
  57.0 5.3 %combine.1 = (f32[10,16,64,128]{3,2,1,0:T(8,128)}, f32[10,10]{1,0:T(8,128)}, f32[2,16,64,128]{3,2,1,0:T(8,128)}) custom-call(f32[256,128]{1,0:T(8,128)S(1)} %bitcast.4, f32[4,2,24,96,128]{4,3,2,1,0:T(8,128)S(1)} %get-tuple-element.41.V, f32[2,16,64,128]{3,2,1,0:T(8,128)S(1)} %get-tuple-element.42.V4), custom_call_target="tpu_custom_call" | custom-call | tf_op jit(solution)/shard_map/combine/pallas_call | solution.py:427
Async XLA Ops:
  2.7 19.8 %collective-permute-start = (f32[20,64,128]{2,1,0:T(8,128)S(1)}, f32[20,64,128]{2,1,0:T(8,128)S(1)}, u32[]{:S(2)}, u32[]{:S(2)}) collective-permute-start(f32[20,64,128]{2,1,0:T(8,128)S(1)} %get-tuple-element.23), channel_id=1, source_target_pairs={{0,8},{16,24},{32,40},{48,56},{64,72},{80,88},{96,104},{112,120},{... | collective-permute-start | bytes 1966088 | tf_op jit(solution)/shard_map/ppermute | solution.py:457
  5.2 17.3 %collective-permute-start.1 = (f32[20,64,128]{2,1,0:T(8,128)S(1)}, f32[20,64,128]{2,1,0:T(8,128)S(1)}, u32[]{:S(2)}, u32[]{:S(2)}) collective-permute-start(f32[20,64,128]{2,1,0:T(8,128)S(1)} %get-tuple-element.24), channel_id=1, source_target_pairs={{8,16},{24,32},{40,48},{56,64},{72,80},{88,96},{104,112},{120,128}... | collective-permute-start | bytes 1966088 | tf_op jit(solution)/shard_map/ppermute | solution.py:457
  5.9 8.9 %collective-permute-start.2 = (f32[384,128]{1,0:T(8,128)S(1)}, f32[384,128]{1,0:T(8,128)S(1)}, u32[]{:S(2)}, u32[]{:S(2)}) collective-permute-start(f32[384,128]{1,0:T(8,128)S(1)} %get-tuple-element.25), channel_id=1, source_target_pairs={{0,1},{2,3},{4,5},{6,7},{1,0},{3,2},{5,4},{7,6},{8,9},{10,11},{12,... | collective-permute-start | bytes 589832 | tf_op jit(solution)/shard_map/ppermute | solution.py:457
  6.9 7.9 %collective-permute-start.3 = (f32[384,128]{1,0:T(8,128)S(1)}, f32[384,128]{1,0:T(8,128)S(1)}, u32[]{:S(2)}, u32[]{:S(2)}) collective-permute-start(f32[384,128]{1,0:T(8,128)S(1)} %get-tuple-element.26), channel_id=1, source_target_pairs={{1,2},{3,4},{5,6},{2,1},{4,3},{6,5},{9,10},{11,12},{13,14},{10,9},... | collective-permute-start | bytes 589832 | tf_op jit(solution)/shard_map/ppermute | solution.py:457
  15.0 7.5 %collective-permute-start.4 = (f32[48,128]{1,0:T(8,128)S(1)}, f32[48,128]{1,0:T(8,128)S(1)}, u32[]{:S(2)}, u32[]{:S(2)}) collective-permute-start(f32[48,128]{1,0:T(8,128)S(1)} %get-tuple-element.30), channel_id=1, source_target_pairs={{0,8},{16,24},{32,40},{48,56},{64,72},{80,88},{96,104},{112,120},{... | collective-permute-start | bytes 73736 | tf_op jit(solution)/shard_map/ppermute | solution.py:457
  19.8 2.6 %collective-permute-start.5 = (f32[48,128]{1,0:T(8,128)S(1)}, f32[48,128]{1,0:T(8,128)S(1)}, u32[]{:S(2)}, u32[]{:S(2)}) collective-permute-start(f32[48,128]{1,0:T(8,128)S(1)} %get-tuple-element.31), channel_id=1, source_target_pairs={{8,16},{24,32},{40,48},{56,64},{72,80},{88,96},{104,112},{120,128}... | collective-permute-start | bytes 73736 | tf_op jit(solution)/shard_map/ppermute | solution.py:457

commit v6 on v5

--- a/solution.py
+++ b/solution.py
@@ -11,6 +11,7 @@
 S = 4
 RHS = 2
 COLS = 10
+UNROLL = 4
 YP = 16
 
 F32 = jnp.float32
@@ -19,32 +20,8 @@
 CORNER_ROWS = RHS * len(FIELD_CORNER) + 4 * len(COEF_CORNER)
 
 
-def slot(leaf, i, k):
-    if i >= 8:
-        return 104 + 3 * leaf + (k - 8) + (i - 8)
-    if k >= 8:
-        return 72 + 16 * leaf + 8 * (k - 8) + i
-    if k == 7:
-        return 56 + 8 * leaf + i
-    return 8 * (6 - k) + 7 - k + i if leaf else 8 * k + i
-
-
-def unpack(g, leaf):
-    row = lax.broadcasted_iota(jnp.int32, (8, g.shape[1]), 0)
-
-    def rows(first, count):
-        group = g[8 * (first // 8) : 8 * (first // 8) + 8]
-        if first % 8:
-            group = pltpu.roll(group, 8 - first % 8, 0)
-        return group if count == 8 else jnp.where(row < count, group, 0.0)
-
-    cols = []
-    for k in range(COLS):
-        parts = [rows(slot(leaf, 0, k), min(k + 1, 8))]
-        if k >= 8:
-            parts.append(rows(slot(leaf, 8, k), k - 7))
-        cols.append(parts)
-    return cols
+def slot(i, k):
+    return (8 * k if k < 8 else 64 + 16 * (k - 8)) + i
 
 
 def toward_high(axis, pairing):
@@ -183,8 +160,12 @@
     return V[k // RHS, k % RHS, x + 4, pl.ds(YP + at, size), :]
 
 
-def local_factor(V, V4, Q, leaf, count, pieces):
+def local_factor(V, V4, Q, count, pieces, before=None, packed=False):
     zero = jnp.zeros((8, 128), F32)
+    top = [zero] * COLS
+    if before is not None:
+        first_row = lax.broadcasted_iota(jnp.int32, (8, 128), 0) == 0
+        top = [jnp.where(first_row, before[k : k + 1, :], 0.0) for k in range(COLS)]
 
     def first_dots(i, accs):
         accs = list(accs)
@@ -195,20 +176,24 @@
                 accs[k] = accs[k] + fold8(q * basis_rows(V, V4, k, x, at, size))
         return tuple(accs)
 
-    accs = lax.fori_loop(0, count, first_dots, (zero,) * COLS, unroll=4)
+    start = tuple(top[0] * t for t in top)
+    accs = lax.fori_loop(0, count, first_dots, start, unroll=UNROLL)
     lane = lax.broadcasted_iota(jnp.int32, (1, 128), 1)
-    line = jnp.zeros((1, 128), F32)
+    lines = [jnp.zeros((1, 128), F32)] * (1 if packed else COLS)
     for j in range(COLS):
         dots = [total(a) for a in accs]
         live = dots[0] > 0.0
         length = jnp.sqrt(jnp.where(live, dots[0], 1.0))
         inv = jnp.where(live, 1.0 / length, 0.0)
         for k in range(j, COLS):
-            line = jnp.where(lane == slot(leaf, j, k), dots[k - j] * inv, line)
+            line, at = (0, slot(j, k)) if packed else (k, j)
+            lines[line] = jnp.where(lane == at, dots[k - j] * inv, lines[line])
         if j == COLS - 1:
-            return line
+            return lines
         recip = 1.0 / jnp.where(live, dots[0], 1.0)
         alphas = [jnp.broadcast_to(d * recip, (8, 128)) for d in dots[1:]]
+        for k in range(j + 1, COLS):
+            top[k] = top[k] - alphas[k - j - 1] * top[j]
 
         def get(k, x, at, size, j=j):
             if j == 0 or k == 0:
@@ -230,51 +215,75 @@
                     accs[k - j - 1] = accs[k - j - 1] + fold8(after * value)
             return tuple(accs)
 
-        accs = lax.fori_loop(0, count, sweep, (zero,) * (COLS - 1 - j), unroll=4)
-
-
-def inner_kernel(X, Y, V_in, U, V, V4, A, line, Q):
+        start = tuple(top[j + 1] * t for t in top[j + 1 :])
+        accs = lax.fori_loop(0, count, sweep, start, unroll=UNROLL)
+
+
+def store_factor(out, lines):
+    for k, line in enumerate(lines):
+        out[k : k + 1, :] = line
+
+
+def inner_kernel(X, Y, V_in, U, V, V4, A, factor, Q):
     coefficient_rows(X, Y, U, A, [(4, X + 4)], YP, Y)
     for k in range(1, S + 1):
         power_rows(V, V4, A, k, [(4 + k, X + 4 - k)], [(YP, Y)], 4)
     half = (Y - 16) // 2
     pieces = [(row, at, half) for row in (4, X // 2) for at in (8, 8 + half)]
-    line[...] = local_factor(V, V4, Q, 0, X // 2 - 4, pieces)
+    store_factor(factor, local_factor(V, V4, Q, X // 2 - 4, pieces))
+
+
+def beside_y(Y, k):
+    if k == S:
+        return [(YP, 8), (YP + Y - 8, 8)]
+    return [(YP - 8, 16), (YP + Y - 8, 16)]
 
 
 def edge_kernel(X, Y, U, V_in, V4_in, A_in, V, V4, A):
     for begin in (YP - 8, YP + Y):
         coefficient_rows(X, Y, U, A, [(4, X + 4)], begin, 8)
-    for k in range(1, S):
-        pieces = [(YP - 8, 16), (YP + Y - 8, 16)]
-        power_rows(V, V4, A, k, [(4 + k, X + 4 - k)], pieces, 4)
-    power_rows(V, V4, A, S, [(4 + S, X + 4 - S)], [(YP, 8), (YP + Y - 8, 8)], 4)
-
-
-def outer_kernel(X, Y, x0, x1, c0, c1, inner_line, V_in, V4_in, A_in, U_in, V, V4, A, U, packed, Q):
-    own_y = slice(YP, YP + Y)
-    for pairing, (got, corner) in enumerate(((x0, c0), (x1, c1))):
+    for k in range(1, S + 1):
+        power_rows(V, V4, A, k, [(4 + k, X + 4 - k)], beside_y(Y, k), 7)
+
+
+def near_x(X, k):
+    return [(k, k + 4), (X + 4 - k, X + 8 - k)]
+
+
+def face_kernel(X, Y, x0, x1, before, V_in, V4_in, A_in, U_in, V, V4, A, U, factor, Q):
+    for pairing, got in enumerate((x0, x1)):
         high = toward_high("gx", pairing)
         at4, at3 = jnp.where(high, X + 4, 0), jnp.where(high, X + 4, 1)
         for i in range(4):
             for f in range(RHS):
-                V[0, f, at4 + i, own_y, :] = got[4 * f + i]
+                V[0, f, at4 + i, YP : YP + Y, :] = got[4 * f + i]
         for i in range(3):
             for c in range(4):
-                U[c, at3 + i, own_y, :] = got[8 + 3 * c + i]
-        for row, (f, x, y) in enumerate(corner_cells(X, Y, high, False)):
+                U[c, at3 + i, YP : YP + Y, :] = got[8 + 3 * c + i]
+    coefficient_rows(X, Y, U, A, [(1, 4), (X + 4, X + 7)], YP, Y)
+    for k in range(1, S + 1):
+        power_rows(V, V4, A, k, near_x(X, k), [(YP, Y)], 2)
+    half = (Y - 16) // 2
+    pieces = [(row, at, half) for row in (0, X - 4) for at in (8, 8 + half)]
+    pieces += [(row, at, 8) for row in (4, X // 2) for at in (0, Y - 8)]
+    store_factor(factor, local_factor(V, V4, Q, 4, pieces, before))
+
+
+def corner_kernel(X, Y, c0, c1, before, V_in, V4_in, A_in, U_in, V, V4, A, U, packed, Q):
+    for pairing, corner in enumerate((c0, c1)):
+        cells = corner_cells(X, Y, toward_high("gx", pairing), False)
+        for row, (f, x, y) in enumerate(cells):
             if f < 2:
                 V[0, f, x, y : y + 1, :] = corner[row : row + 1, :]
             else:
                 U[f - 2, x, y : y + 1, :] = corner[row : row + 1, :]
-    coefficient_rows(X, Y, U, A, [(1, 4), (X + 4, X + 7)], YP - 8, Y + 16)
+    for begin in (YP - 8, YP + Y):
+        coefficient_rows(X, Y, U, A, [(1, 4), (X + 4, X + 7)], begin, 8)
     for k in range(1, S + 1):
-        piece = (YP - 8, Y + 16) if k < S else (YP, Y)
-        power_rows(V, V4, A, k, [(k, k + 4), (X + 4 - k, X + 8 - k)], [piece], 2)
-    pieces = [(row, at, Y // 2) for row in (0, X - 4) for at in (0, Y // 2)]
-    pieces += [(row, at, 8) for row in (4, X // 2) for at in (0, Y - 8)]
-    line = local_factor(V, V4, Q, 1, 4, pieces)
-    packed[...] = jnp.broadcast_to(inner_line[...] + line, packed.shape)
+        power_rows(V, V4, A, k, near_x(X, k), beside_y(Y, k), 4)
+    pieces = [(row, at, 8) for row in (0, X - 4) for at in (0, Y - 8)]
+    (line,) = local_factor(V, V4, Q, 4, pieces, before, packed=True)
+    packed[...] = jnp.broadcast_to(line, packed.shape)
 
 
 def fold_lanes(x):
@@ -284,10 +293,10 @@
 
 def merged_factor(gathered):
     g = gathered.T
-    cols = [
-        [jnp.concatenate(parts, axis=1) for parts in zip(*pair)]
-        for pair in zip(unpack(g, 0), unpack(g, 1))
-    ]
+    cols = []
+    for k in range(COLS):
+        at = slot(0, k)
+        cols.append([g[i : i + 8] for i in range(at, at + k + 1, 8)])
     R = {}
     for j in range(COLS):
         dots = []
@@ -469,11 +478,12 @@
     y1, y0 = swap(y1, "gy", 1), swap(y0, "gy", 0)
     v4_shape, a_shape = ((RHS, X, Y, Z), PIN), ((6, XE, YE, Z), PIN)
     work = pltpu.VMEM((COLS - 1, X, Y, Z), F32)
-    V, V4, A, line = call(
+    factor_shape = ((16, Z), PIN)
+    V, V4, A, factor = call(
         functools.partial(inner_kernel, X, Y),
         "inner",
         [(V, PIN), (U, PIN)],
-        [v_shape, v4_shape, a_shape, ((1, 128), PIN)],
+        [v_shape, v4_shape, a_shape, factor_shape],
         [work],
         aliases={0: 0},
         limit=8,
@@ -494,13 +504,23 @@
         [v_shape, v4_shape, a_shape],
         aliases={1: 0, 2: 1, 3: 2},
     )
+    state = [v_shape, v4_shape, a_shape, u_shape]
+    V, V4, A, U, factor = call(
+        functools.partial(face_kernel, X, Y),
+        "face",
+        [(a, PIN) for a in (x0, x1, factor, V, V4, A, U)],
+        state + [factor_shape],
+        [work],
+        aliases={3: 0, 4: 1, 5: 2, 6: 3},
+        limit=8,
+    )
     V, V4, A, U, packed = call(
-        functools.partial(outer_kernel, X, Y),
-        "outer",
-        [(a, PIN) for a in (x0, x1, c0, c1, line, V, V4, A, U)],
-        [v_shape, v4_shape, a_shape, u_shape, ((devices, 128), BLOCK)],
+        functools.partial(corner_kernel, X, Y),
+        "corner",
+        [(a, PIN) for a in (c0, c1, factor, V, V4, A, U)],
+        state + [((devices, 128), BLOCK)],
         [work],
-        aliases={5: 0, 6: 1, 7: 2, 8: 3},
+        aliases={3: 0, 4: 1, 5: 2, 6: 3},
         limit=8,
     )
     gathered = lax.all_to_all(packed, ("gx", "gy"), 0, 0, tiled=True)

time: 62.5 us -> 62.8 us (level)
    pallas_call x6 -> x7, Pallas kernels: 19.3 us -> 19.6 us  [call(): pl.pallas_call(kernel, out_shape=tuple((pltpu.VMEM(o, F32) if place == PI...]
  transfers between devices with their start and end apart: 6 -> 6, of which waited for: 0 -> 0; matrix products, arithmetic and copies ran while one was open for 0% -> 0% of each run, Pallas kernels for 11% -> 17%
where the time goes in v6:
time: 62.8 us; the launch traced here: 62.6 us
  blocking collectives  29.4 us (47%)
  Pallas kernels  19.6 us (31%)
  starting transfers between devices  12.9 us (21%)
  between operations  0.73 us (1%)
    all_to_all x1, blocking collectives, body(): gathered = lax.all_to_all(packed, ('gx', 'gy'), 0, 0, tiled=True)  29.4 us
    pallas_call x7, Pallas kernels, call(): pl.pallas_call(kernel, out_shape=tuple((pltpu.VMEM(o, F32) if place == PI...  19.6 us
    ppermute x6, starting transfers between devices, swap(): return lax.ppermute(value, axis, pairs + [(j, i) for i, j in pairs])  12.9 us
  transfers between devices with their start and end apart: 6, of which 0 were waited for; matrix products, arithmetic and copies ran while one was open for 0% of the time, Pallas kernels for 17%

profile of v6, /device:TPU:1, one launch (start us, length us, event | category | flops | bytes accessed | tf_op | source)
XLA Modules:
  0.0 62.6 jit_solution(11991012498591096009)
XLA Ops:
  0.6 2.0 %pack.1 = (f32[20,64,128]{2,1,0:T(8,128)S(1)}, f32[20,64,128]{2,1,0:T(8,128)S(1)}, f32[384,128]{1,0:T(8,128)S(1)}, f32[384,128]{1,0:T(8,128)S(1)}, f32[4,2,24,96...) custom-call(f32[2,16,64,128]{3,2,1,0:T(8,128)} %rhs.1, f32[3,16,64,128]{3,2,1,0:T(8,128)} %vel.1, f32[16,64,128]{2,1,0:T(8,128)} %diag.1), custom_call_target="tpu_custom_call" | custom-call | tf_op jit(solution)/shard_map/pack/pallas_call | solution.py:436
  2.7 2.6 %collective-permute-start.4 = (f32[20,64,128]{2,1,0:T(8,128)S(1)}, f32[20,64,128]{2,1,0:T(8,128)S(1)}, u32[]{:S(2)}, u32[]{:S(2)}) collective-permute-start(f32[20,64,128]{2,1,0:T(8,128)S(1)} %get-tuple-element.35), channel_id=1, source_target_pairs={{0,8},{16,24},{32,40},{48,56},{64,72},{80,88},{96,104},{112,120},{... | collective-permute-start | bytes 1966088 | tf_op jit(solution)/shard_map/ppermute | solution.py:466
  5.2 0.7 %collective-permute-start.5 = (f32[20,64,128]{2,1,0:T(8,128)S(1)}, f32[20,64,128]{2,1,0:T(8,128)S(1)}, u32[]{:S(2)}, u32[]{:S(2)}) collective-permute-start(f32[20,64,128]{2,1,0:T(8,128)S(1)} %get-tuple-element.36), channel_id=1, source_target_pairs={{8,16},{24,32},{40,48},{56,64},{72,80},{88,96},{104,112},{120,128}... | collective-permute-start | bytes 1966088 | tf_op jit(solution)/shard_map/ppermute | solution.py:466
  5.9 1.0 %collective-permute-start = (f32[384,128]{1,0:T(8,128)S(1)}, f32[384,128]{1,0:T(8,128)S(1)}, u32[]{:S(2)}, u32[]{:S(2)}) collective-permute-start(f32[384,128]{1,0:T(8,128)S(1)} %get-tuple-element.28), channel_id=1, source_target_pairs={{0,1},{2,3},{4,5},{6,7},{1,0},{3,2},{5,4},{7,6},{8,9},{10,11},{12,... | collective-permute-start | bytes 589832 | tf_op jit(solution)/shard_map/ppermute | solution.py:466
  6.9 3.1 %collective-permute-start.1 = (f32[384,128]{1,0:T(8,128)S(1)}, f32[384,128]{1,0:T(8,128)S(1)}, u32[]{:S(2)}, u32[]{:S(2)}) collective-permute-start(f32[384,128]{1,0:T(8,128)S(1)} %get-tuple-element.29), channel_id=1, source_target_pairs={{1,2},{3,4},{5,6},{2,1},{4,3},{6,5},{9,10},{11,12},{13,14},{10,9},... | collective-permute-start | bytes 589832 | tf_op jit(solution)/shard_map/ppermute | solution.py:466
  10.1 4.6 %inner.1 = (f32[4,2,24,96,128]{4,3,2,1,0:T(8,128)S(1)}, f32[2,16,64,128]{3,2,1,0:T(8,128)S(1)}, f32[6,24,96,128]{3,2,1,0:T(8,128)S(1)}, f32[16,128]{1,0:T(8,128)S(1)}) custom-call(f32[4,2,24,96,128]{4,3,2,1,0:T(8,128)S(1)} %get-tuple-element.30.V_in, f32[4,24,96,128]{3,2,1,0:T(8,128)S(1)} %get-tuple-element.31.U.U_in), custom_call_target="tpu_custom_call", output_to_operand_aliasing={{0}: (0, {})} | custom-call | tf_op jit(solution)/shard_map/inner/pallas_call | solution.py:436
  14.7 0.0 collective-permute-done.y0
  14.7 0.0 collective-permute-done.1.y1
  14.7 0.1 place_y.1
  14.8 4.8 %collective-permute-start.2 = (f32[48,128]{1,0:T(8,128)S(1)}, f32[48,128]{1,0:T(8,128)S(1)}, u32[]{:S(2)}, u32[]{:S(2)}) collective-permute-start(f32[48,128]{1,0:T(8,128)S(1)} %get-tuple-element.33), channel_id=1, source_target_pairs={{0,8},{16,24},{32,40},{48,56},{64,72},{80,88},{96,104},{112,120},{... | collective-permute-start | bytes 73736 | tf_op jit(solution)/shard_map/ppermute | solution.py:466
  19.7 0.7 %collective-permute-start.3 = (f32[48,128]{1,0:T(8,128)S(1)}, f32[48,128]{1,0:T(8,128)S(1)}, u32[]{:S(2)}, u32[]{:S(2)}) collective-permute-start(f32[48,128]{1,0:T(8,128)S(1)} %get-tuple-element.34), channel_id=1, source_target_pairs={{8,16},{24,32},{40,48},{56,64},{72,80},{88,96},{104,112},{120,128}... | collective-permute-start | bytes 73736 | tf_op jit(solution)/shard_map/ppermute | solution.py:466
  20.3 1.9 %edge.1 = (f32[4,2,24,96,128]{4,3,2,1,0:T(8,128)S(1)}, f32[2,16,64,128]{3,2,1,0:T(8,128)S(1)}, f32[6,24,96,128]{3,2,1,0:T(8,128)S(1)}) custom-call(f32[4,24,96,128]{3,2,1,0:T(8,128)S(1)} %get-tuple-element.38.U.U_in, f32[4,2,24,96,128]{4,3,2,1,0:T(8,128)S(1)} %get-tuple-element.39.V_in, ...), custom_call_target="tpu_custom_call", output_to_operand_aliasing={{0}: (1, {}), {1}: (2, {}), {2}: (3, {})} | custom-call | tf_op jit(solution)/shard_map/edge/pallas_call | solution.py:436
  22.2 0.0 collective-permute-done.4.x0
  22.2 0.0 collective-permute-done.5.x1
  22.2 4.1 %face.1 = (f32[4,2,24,96,128]{4,3,2,1,0:T(8,128)S(1)}, f32[2,16,64,128]{3,2,1,0:T(8,128)S(1)}, f32[6,24,96,128]{3,2,1,0:T(8,128)S(1)}, f32[4,24,96,128]{3,2,1,0:T(8,128)S(1)}, f32[16,128]{1,0:T(8,128)S(1)}) custom-call(f32[20,64,128]{2,1,0:T(8,128)S(1)} %collective-permute-done.4.x0, ...), custom_call_target="tpu_custom_call", output_to_operand_aliasing={{0}: (3, {}), {1}: (4, {}), {2}: (5, {}), {3}: (6, {})} | custom-call | tf_op jit(solution)/shard_map/face/pallas_call | solution.py:436
  26.4 0.0 collective-permute-done.2.c0
  26.4 0.0 collective-permute-done.3.c1
  26.4 1.8 %corner.1 = (f32[4,2,24,96,128]{4,3,2,1,0:T(8,128)S(1)}, f32[2,16,64,128]{3,2,1,0:T(8,128)S(1)}, f32[6,24,96,128]{3,2,1,0:T(8,128)S(1)}, f32[4,24,96,128]{3,2,1,0:T(8,128)S(1)}, f32[256,128]{1,0:T(8,128)S(1)}) custom-call(f32[48,128]{1,0:T(8,128)S(1)} %collective-permute-done.2.c0, ...), custom_call_target="tpu_custom_call", output_to_operand_aliasing={{0}: (3, {}), {1}: (4, {}), {2}: (5, {}), {3}: (6, {})} | custom-call | tf_op jit(solution)/shard_map/corner/pallas_call | solution.py:436
  28.2 29.4 %all_to_all.11 = f32[256,1,128]{2,1,0:T(1,128)S(1)} all-to-all(f32[256,1,128]{2,1,0:T(1,128)S(1)} %bitcast.5), channel_id=1, replica_groups=mesh['gx'=32,'gy'=8] {'gx','gy'}, dimensions={0} | all-to-all | bytes 262144 | tf_op jit(solution)/shard_map/all_to_all | solution.py:526
  57.6 5.1 %combine.1 = (f32[10,16,64,128]{3,2,1,0:T(8,128)}, f32[10,10]{1,0:T(8,128)}, f32[2,16,64,128]{3,2,1,0:T(8,128)}) custom-call(f32[256,128]{1,0:T(8,128)S(1)} %bitcast.4, f32[4,2,24,96,128]{4,3,2,1,0:T(8,128)S(1)} %get-tuple-element.51.V, f32[2,16,64,128]{3,2,1,0:T(8,128)S(1)} %get-tuple-element.52.V4), custom_call_target="tpu_custom_call" | custom-call | tf_op jit(solution)/shard_map/combine/pallas_call | solution.py:436
Async XLA Ops:
  2.7 19.6 %collective-permute-start.4 = (f32[20,64,128]{2,1,0:T(8,128)S(1)}, f32[20,64,128]{2,1,0:T(8,128)S(1)}, u32[]{:S(2)}, u32[]{:S(2)}) collective-permute-start(f32[20,64,128]{2,1,0:T(8,128)S(1)} %get-tuple-element.35), channel_id=1, source_target_pairs={{0,8},{16,24},{32,40},{48,56},{64,72},{80,88},{96,104},{112,120},{... | collective-permute-start | bytes 1966088 | tf_op jit(solution)/shard_map/ppermute | solution.py:466
  5.2 17.0 %collective-permute-start.5 = (f32[20,64,128]{2,1,0:T(8,128)S(1)}, f32[20,64,128]{2,1,0:T(8,128)S(1)}, u32[]{:S(2)}, u32[]{:S(2)}) collective-permute-start(f32[20,64,128]{2,1,0:T(8,128)S(1)} %get-tuple-element.36), channel_id=1, source_target_pairs={{8,16},{24,32},{40,48},{56,64},{72,80},{88,96},{104,112},{120,128}... | collective-permute-start | bytes 1966088 | tf_op jit(solution)/shard_map/ppermute | solution.py:466
  5.9 8.8 %collective-permute-start = (f32[384,128]{1,0:T(8,128)S(1)}, f32[384,128]{1,0:T(8,128)S(1)}, u32[]{:S(2)}, u32[]{:S(2)}) collective-permute-start(f32[384,128]{1,0:T(8,128)S(1)} %get-tuple-element.28), channel_id=1, source_target_pairs={{0,1},{2,3},{4,5},{6,7},{1,0},{3,2},{5,4},{7,6},{8,9},{10,11},{12,... | collective-permute-start | bytes 589832 | tf_op jit(solution)/shard_map/ppermute | solution.py:466
  6.9 7.7 %collective-permute-start.1 = (f32[384,128]{1,0:T(8,128)S(1)}, f32[384,128]{1,0:T(8,128)S(1)}, u32[]{:S(2)}, u32[]{:S(2)}) collective-permute-start(f32[384,128]{1,0:T(8,128)S(1)} %get-tuple-element.29), channel_id=1, source_target_pairs={{1,2},{3,4},{5,6},{2,1},{4,3},{6,5},{9,10},{11,12},{13,14},{10,9},... | collective-permute-start | bytes 589832 | tf_op jit(solution)/shard_map/ppermute | solution.py:466
  14.8 11.6 %collective-permute-start.2 = (f32[48,128]{1,0:T(8,128)S(1)}, f32[48,128]{1,0:T(8,128)S(1)}, u32[]{:S(2)}, u32[]{:S(2)}) collective-permute-start(f32[48,128]{1,0:T(8,128)S(1)} %get-tuple-element.33), channel_id=1, source_target_pairs={{0,8},{16,24},{32,40},{48,56},{64,72},{80,88},{96,104},{112,120},{... | collective-permute-start | bytes 73736 | tf_op jit(solution)/shard_map/ppermute | solution.py:466
  19.7 6.7 %collective-permute-start.3 = (f32[48,128]{1,0:T(8,128)S(1)}, f32[48,128]{1,0:T(8,128)S(1)}, u32[]{:S(2)}, u32[]{:S(2)}) collective-permute-start(f32[48,128]{1,0:T(8,128)S(1)} %get-tuple-element.34), channel_id=1, source_target_pairs={{8,16},{24,32},{40,48},{56,64},{72,80},{88,96},{104,112},{120,128}... | collective-permute-start | bytes 73736 | tf_op jit(solution)/shard_map/ppermute | solution.py:466

commit v7 on v6

--- a/solution.py
+++ b/solution.py
@@ -42,13 +42,13 @@
         copy.wait()
     for pairing, out in enumerate((x0, x1)):
         high = toward_high("gx", pairing)
-        at4, at3 = jnp.where(high, X, 4), jnp.where(high, X + 1, 4)
-        for i in range(4):
+        at3, at2 = jnp.where(high, X + 1, 4), jnp.where(high, X + 2, 4)
+        for i in range(3):
             for f in range(RHS):
-                out[4 * f + i] = V[0, f, at4 + i, YP : YP + Y, :]
-        for i in range(3):
+                out[3 * f + i] = V[0, f, at3 + i, YP : YP + Y, :]
+        for i in range(2):
             for c in range(4):
-                out[8 + 3 * c + i] = U[c, at3 + i, YP : YP + Y, :]
+                out[6 + 2 * c + i] = U[c, at2 + i, YP : YP + Y, :]
     first_high = toward_high("gy", 0)
     for f in range(6):
         for x in range(X):
@@ -72,7 +72,7 @@
     return cells
 
 
-def place_y_kernel(X, Y, y0, y1, V_in, U_in, V, U, first, second):
+def place_y_kernel(X, Y, y0, y1, A, V_in, U_in, V, U, first, second):
     first_high = toward_high("gy", 0)
     for f in range(6):
         for x in range(X):
@@ -81,10 +81,13 @@
             field = V.at[0, f, 4 + x] if f < 2 else U.at[f - 2, 4 + x]
             field[YP - 4 : YP, :] = jnp.where(first_high, b, a)
             field[YP + Y : YP + Y + 4, :] = jnp.where(first_high, a, b)
+    power_rows(V, None, A, 1, [(6, 7), (X + 1, X + 2)], [(YP, 8), (YP + Y - 8, 8)], 1)
     for pairing, out in enumerate((first, second)):
-        cells = corner_cells(X, Y, toward_high("gx", pairing), True)
-        for row, (f, x, y) in enumerate(cells):
-            out[row : row + 1, :] = (
+        high = toward_high("gx", pairing)
+        for f in range(RHS):
+            out[f * Y : (f + 1) * Y, :] = V[1, f, jnp.where(high, X + 1, 6), YP : YP + Y, :]
+        for row, (f, x, y) in enumerate(corner_cells(X, Y, high, True)):
+            out[RHS * Y + row : RHS * Y + row + 1, :] = (
                 V[0, f, x, y : y + 1, :] if f < 2 else U[f - 2, x, y : y + 1, :]
             )
 
@@ -160,14 +163,20 @@
     return V[k // RHS, k % RHS, x + 4, pl.ds(YP + at, size), :]
 
 
-def local_factor(V, V4, Q, count, pieces, before=None, packed=False):
+def local_factor(V, V4, Q, groups, before=None, packed=False):
+    def over_groups(body, accs):
+        for count, pieces in groups:
+            run = functools.partial(body, pieces)
+            accs = lax.fori_loop(0, count, run, accs, unroll=min(count, UNROLL))
+        return accs
+
     zero = jnp.zeros((8, 128), F32)
     top = [zero] * COLS
     if before is not None:
         first_row = lax.broadcasted_iota(jnp.int32, (8, 128), 0) == 0
         top = [jnp.where(first_row, before[k : k + 1, :], 0.0) for k in range(COLS)]
 
-    def first_dots(i, accs):
+    def first_dots(pieces, i, accs):
         accs = list(accs)
         for row, at, size in pieces:
             x = row + i
@@ -177,12 +186,12 @@
         return tuple(accs)
 
     start = tuple(top[0] * t for t in top)
-    accs = lax.fori_loop(0, count, first_dots, start, unroll=UNROLL)
+    accs = over_groups(first_dots, start)
     lane = lax.broadcasted_iota(jnp.int32, (1, 128), 1)
     lines = [jnp.zeros((1, 128), F32)] * (1 if packed else COLS)
     for j in range(COLS):
         dots = [total(a) for a in accs]
-        live = dots[0] > 0.0
+        live = dots[0] >= 1e-37
         length = jnp.sqrt(jnp.where(live, dots[0], 1.0))
         inv = jnp.where(live, 1.0 / length, 0.0)
         for k in range(j, COLS):
@@ -200,7 +209,7 @@
                 return basis_rows(V, V4, k, x, at, size)
             return Q[k - 1, x, pl.ds(at, size), :]
 
-        def sweep(i, accs, j=j, get=get, alphas=alphas):
+        def sweep(pieces, i, accs, j=j, get=get, alphas=alphas):
             accs = list(accs)
             for row, at, size in pieces:
                 x = row + i
@@ -216,7 +225,7 @@
             return tuple(accs)
 
         start = tuple(top[j + 1] * t for t in top[j + 1 :])
-        accs = lax.fori_loop(0, count, sweep, start, unroll=UNROLL)
+        accs = over_groups(sweep, start)
 
 
 def store_factor(out, lines):
@@ -230,7 +239,7 @@
         power_rows(V, V4, A, k, [(4 + k, X + 4 - k)], [(YP, Y)], 4)
     half = (Y - 16) // 2
     pieces = [(row, at, half) for row in (4, X // 2) for at in (8, 8 + half)]
-    store_factor(factor, local_factor(V, V4, Q, X // 2 - 4, pieces))
+    store_factor(factor, local_factor(V, V4, Q, [(X // 2 - 4, pieces)]))
 
 
 def beside_y(Y, k):
@@ -247,42 +256,53 @@
 
 
 def near_x(X, k):
-    return [(k, k + 4), (X + 4 - k, X + 8 - k)]
+    return [(k + 1, k + 4), (X + 4 - k, X + 7 - k)]
+
+
+def nearest_x(X, k):
+    return [(k, k + 1), (X + 7 - k, X + 8 - k)]
 
 
 def face_kernel(X, Y, x0, x1, before, V_in, V4_in, A_in, U_in, V, V4, A, U, factor, Q):
     for pairing, got in enumerate((x0, x1)):
         high = toward_high("gx", pairing)
-        at4, at3 = jnp.where(high, X + 4, 0), jnp.where(high, X + 4, 1)
-        for i in range(4):
+        at3, at2 = jnp.where(high, X + 4, 1), jnp.where(high, X + 4, 2)
+        for i in range(3):
             for f in range(RHS):
-                V[0, f, at4 + i, YP : YP + Y, :] = got[4 * f + i]
-        for i in range(3):
+                V[0, f, at3 + i, YP : YP + Y, :] = got[3 * f + i]
+        for i in range(2):
             for c in range(4):
-                U[c, at3 + i, YP : YP + Y, :] = got[8 + 3 * c + i]
-    coefficient_rows(X, Y, U, A, [(1, 4), (X + 4, X + 7)], YP, Y)
+                U[c, at2 + i, YP : YP + Y, :] = got[6 + 2 * c + i]
+    coefficient_rows(X, Y, U, A, [(2, 4), (X + 4, X + 6)], YP, Y)
     for k in range(1, S + 1):
-        power_rows(V, V4, A, k, near_x(X, k), [(YP, Y)], 2)
+        power_rows(V, V4, A, k, near_x(X, k), [(YP, Y)], 3)
     half = (Y - 16) // 2
-    pieces = [(row, at, half) for row in (0, X - 4) for at in (8, 8 + half)]
-    pieces += [(row, at, 8) for row in (4, X // 2) for at in (0, Y - 8)]
-    store_factor(factor, local_factor(V, V4, Q, 4, pieces, before))
+    faces = [(row, at, half) for row in (1, X - 4) for at in (8, 8 + half)]
+    sides = [(row, at, 8) for row in (4, X // 2) for at in (0, Y - 8)]
+    groups = [(3, faces), (X // 2 - 4, sides)]
+    store_factor(factor, local_factor(V, V4, Q, groups, before))
 
 
 def corner_kernel(X, Y, c0, c1, before, V_in, V4_in, A_in, U_in, V, V4, A, U, packed, Q):
-    for pairing, corner in enumerate((c0, c1)):
-        cells = corner_cells(X, Y, toward_high("gx", pairing), False)
-        for row, (f, x, y) in enumerate(cells):
+    for pairing, got in enumerate((c0, c1)):
+        high = toward_high("gx", pairing)
+        for f in range(RHS):
+            V[1, f, jnp.where(high, X + 6, 1), YP : YP + Y, :] = got[f * Y : (f + 1) * Y, :]
+        for row, (f, x, y) in enumerate(corner_cells(X, Y, high, False)):
+            value = got[RHS * Y + row : RHS * Y + row + 1, :]
             if f < 2:
-                V[0, f, x, y : y + 1, :] = corner[row : row + 1, :]
+                V[0, f, x, y : y + 1, :] = value
             else:
-                U[f - 2, x, y : y + 1, :] = corner[row : row + 1, :]
+                U[f - 2, x, y : y + 1, :] = value
     for begin in (YP - 8, YP + Y):
-        coefficient_rows(X, Y, U, A, [(1, 4), (X + 4, X + 7)], begin, 8)
+        coefficient_rows(X, Y, U, A, [(2, 4), (X + 4, X + 6)], begin, 8)
     for k in range(1, S + 1):
-        power_rows(V, V4, A, k, near_x(X, k), beside_y(Y, k), 4)
-    pieces = [(row, at, 8) for row in (0, X - 4) for at in (0, Y - 8)]
-    (line,) = local_factor(V, V4, Q, 4, pieces, before, packed=True)
+        power_rows(V, V4, A, k, near_x(X, k), beside_y(Y, k), 3)
+        if k > 1:
+            power_rows(V, V4, A, k, nearest_x(X, k), [(YP, Y)], 1)
+    ends = [(row, at, Y // 2) for row in (0, X - 1) for at in (0, Y // 2)]
+    sides = [(row, at, 8) for row in (1, X - 4) for at in (0, Y - 8)]
+    (line,) = local_factor(V, V4, Q, [(1, ends), (3, sides)], before, packed=True)
     packed[...] = jnp.broadcast_to(line, packed.shape)
 
 
@@ -466,7 +486,7 @@
         return lax.ppermute(value, axis, pairs + [(j, i) for i, j in pairs])
 
     v_shape, u_shape = ((S, RHS, XE, YE, Z), PIN), ((4, XE, YE, Z), PIN)
-    x_slab, y_slab = ((20, Y, Z), PIN), ((24 * X, Z), PIN)
+    x_slab, y_slab = ((14, Y, Z), PIN), ((24 * X, Z), PIN)
     x0, x1, y0, y1, V, U = call(
         functools.partial(pack_kernel, X, Y),
         "pack",
@@ -488,13 +508,13 @@
         aliases={0: 0},
         limit=8,
     )
-    strip = ((2 * CORNER_ROWS, Z), PIN)
+    strip = ((RHS * Y + 2 * CORNER_ROWS, Z), PIN)
     V, U, c0, c1 = call(
         functools.partial(place_y_kernel, X, Y),
         "place_y",
-        [(y0, PIN), (y1, PIN), (V, PIN), (U, PIN)],
+        [(a, PIN) for a in (y0, y1, A, V, U)],
         [v_shape, u_shape, strip, strip],
-        aliases={2: 0, 3: 1},
+        aliases={3: 0, 4: 1},
     )
     c0, c1 = swap(c0, "gx", 0), swap(c1, "gx", 1)
     V, V4, A = call(

time: 62.8 us -> 59.3 us (0.944)
  blocking collectives: 29.4 us -> 26.4 us
    all_to_all x1, blocking collectives: 29.4 us -> 26.4 us  [body(): gathered = lax.all_to_all(packed, ('gx', 'gy'), 0, 0, tiled=True)]
where the time goes in v7:
time: 59.3 us; the launch traced here: 59.1 us
  blocking collectives  26.4 us (45%)
  Pallas kernels  19 us (32%)
  starting transfers between devices  12.9 us (22%)
  between operations  0.73 us (1%)
    all_to_all x1, blocking collectives, body(): gathered = lax.all_to_all(packed, ('gx', 'gy'), 0, 0, tiled=True)  26.4 us
    pallas_call x7, Pallas kernels, call(): pl.pallas_call(kernel, out_shape=tuple((pltpu.VMEM(o, F32) if place == PI...  19 us
    ppermute x6, starting transfers between devices, swap(): return lax.ppermute(value, axis, pairs + [(j, i) for i, j in pairs])  12.9 us
  transfers between devices with their start and end apart: 6, of which 0 were waited for; matrix products, arithmetic and copies ran while one was open for 0% of the time, Pallas kernels for 17%

profile of v7, /device:TPU:1, one launch (start us, length us, event | category | flops | bytes accessed | tf_op | source)
XLA Modules:
  0.0 59.1 jit_solution(12164257668624691004)
XLA Ops:
  0.6 2.0 %pack.1 = (f32[14,64,128]{2,1,0:T(8,128)S(1)}, f32[14,64,128]{2,1,0:T(8,128)S(1)}, f32[384,128]{1,0:T(8,128)S(1)}, f32[384,128]{1,0:T(8,128)S(1)}, f32[4,2,24,96...) custom-call(f32[2,16,64,128]{3,2,1,0:T(8,128)} %rhs.1, f32[3,16,64,128]{3,2,1,0:T(8,128)} %vel.1, f32[16,64,128]{2,1,0:T(8,128)} %diag.1), custom_call_target="tpu_custom_call" | custom-call | tf_op jit(solution)/shard_map/pack/pallas_call | solution.py:456
  2.6 2.6 %collective-permute-start.4 = (f32[14,64,128]{2,1,0:T(8,128)S(1)}, f32[14,64,128]{2,1,0:T(8,128)S(1)}, u32[]{:S(2)}, u32[]{:S(2)}) collective-permute-start(f32[14,64,128]{2,1,0:T(8,128)S(1)} %get-tuple-element.36), channel_id=1, source_target_pairs={{0,8},{16,24},{32,40},{48,56},{64,72},{80,88},{96,104},{112,120},{... | collective-permute-start | bytes 1376264 | tf_op jit(solution)/shard_map/ppermute | solution.py:486
  5.2 0.7 %collective-permute-start.5 = (f32[14,64,128]{2,1,0:T(8,128)S(1)}, f32[14,64,128]{2,1,0:T(8,128)S(1)}, u32[]{:S(2)}, u32[]{:S(2)}) collective-permute-start(f32[14,64,128]{2,1,0:T(8,128)S(1)} %get-tuple-element.37), channel_id=1, source_target_pairs={{8,16},{24,32},{40,48},{56,64},{72,80},{88,96},{104,112},{120,128}... | collective-permute-start | bytes 1376264 | tf_op jit(solution)/shard_map/ppermute | solution.py:486
  5.9 1.0 %collective-permute-start = (f32[384,128]{1,0:T(8,128)S(1)}, f32[384,128]{1,0:T(8,128)S(1)}, u32[]{:S(2)}, u32[]{:S(2)}) collective-permute-start(f32[384,128]{1,0:T(8,128)S(1)} %get-tuple-element.28), channel_id=1, source_target_pairs={{0,1},{2,3},{4,5},{6,7},{1,0},{3,2},{5,4},{7,6},{8,9},{10,11},{12,... | collective-permute-start | bytes 589832 | tf_op jit(solution)/shard_map/ppermute | solution.py:486
  6.9 3.1 %collective-permute-start.1 = (f32[384,128]{1,0:T(8,128)S(1)}, f32[384,128]{1,0:T(8,128)S(1)}, u32[]{:S(2)}, u32[]{:S(2)}) collective-permute-start(f32[384,128]{1,0:T(8,128)S(1)} %get-tuple-element.29), channel_id=1, source_target_pairs={{1,2},{3,4},{5,6},{2,1},{4,3},{6,5},{9,10},{11,12},{13,14},{10,9},... | collective-permute-start | bytes 589832 | tf_op jit(solution)/shard_map/ppermute | solution.py:486
  10.0 4.6 %inner.1 = (f32[4,2,24,96,128]{4,3,2,1,0:T(8,128)S(1)}, f32[2,16,64,128]{3,2,1,0:T(8,128)S(1)}, f32[6,24,96,128]{3,2,1,0:T(8,128)S(1)}, f32[16,128]{1,0:T(8,128)S(1)}) custom-call(f32[4,2,24,96,128]{4,3,2,1,0:T(8,128)S(1)} %get-tuple-element.30.V_in, f32[4,24,96,128]{3,2,1,0:T(8,128)S(1)} %get-tuple-element.31.U.U_in), custom_call_target="tpu_custom_call", output_to_operand_aliasing={{0}: (0, {})} | custom-call | tf_op jit(solution)/shard_map/inner/pallas_call | solution.py:456
  14.6 0.0 collective-permute-done.y0
  14.6 0.0 collective-permute-done.1.y1
  14.7 0.1 place_y.1
  14.8 4.9 %collective-permute-start.2 = (f32[176,128]{1,0:T(8,128)S(1)}, f32[176,128]{1,0:T(8,128)S(1)}, u32[]{:S(2)}, u32[]{:S(2)}) collective-permute-start(f32[176,128]{1,0:T(8,128)S(1)} %get-tuple-element.34), channel_id=1, source_target_pairs={{0,8},{16,24},{32,40},{48,56},{64,72},{80,88},{96,104},{112,120},{... | collective-permute-start | bytes 270344 | tf_op jit(solution)/shard_map/ppermute | solution.py:486
  19.7 0.7 %collective-permute-start.3 = (f32[176,128]{1,0:T(8,128)S(1)}, f32[176,128]{1,0:T(8,128)S(1)}, u32[]{:S(2)}, u32[]{:S(2)}) collective-permute-start(f32[176,128]{1,0:T(8,128)S(1)} %get-tuple-element.35), channel_id=1, source_target_pairs={{8,16},{24,32},{40,48},{56,64},{72,80},{88,96},{104,112},{120,128}... | collective-permute-start | bytes 270344 | tf_op jit(solution)/shard_map/ppermute | solution.py:486
  20.3 1.9 %edge.1 = (f32[4,2,24,96,128]{4,3,2,1,0:T(8,128)S(1)}, f32[2,16,64,128]{3,2,1,0:T(8,128)S(1)}, f32[6,24,96,128]{3,2,1,0:T(8,128)S(1)}) custom-call(f32[4,24,96,128]{3,2,1,0:T(8,128)S(1)} %get-tuple-element.39.U.U_in, f32[4,2,24,96,128]{4,3,2,1,0:T(8,128)S(1)} %get-tuple-element.40.V_in, ...), custom_call_target="tpu_custom_call", output_to_operand_aliasing={{0}: (1, {}), {1}: (2, {}), {2}: (3, {})} | custom-call | tf_op jit(solution)/shard_map/edge/pallas_call | solution.py:456
  22.2 0.0 collective-permute-done.4.x0
  22.2 0.0 collective-permute-done.5.x1
  22.2 3.2 %face.1 = (f32[4,2,24,96,128]{4,3,2,1,0:T(8,128)S(1)}, f32[2,16,64,128]{3,2,1,0:T(8,128)S(1)}, f32[6,24,96,128]{3,2,1,0:T(8,128)S(1)}, f32[4,24,96,128]{3,2,1,0:T(8,128)S(1)}, f32[16,128]{1,0:T(8,128)S(1)}) custom-call(f32[14,64,128]{2,1,0:T(8,128)S(1)} %collective-permute-done.4.x0, ...), custom_call_target="tpu_custom_call", output_to_operand_aliasing={{0}: (3, {}), {1}: (4, {}), {2}: (5, {}), {3}: (6, {})} | custom-call | tf_op jit(solution)/shard_map/face/pallas_call | solution.py:456
  25.5 0.0 collective-permute-done.2.c0
  25.5 0.0 collective-permute-done.3.c1
  25.5 2.1 %corner.1 = (f32[4,2,24,96,128]{4,3,2,1,0:T(8,128)S(1)}, f32[2,16,64,128]{3,2,1,0:T(8,128)S(1)}, f32[6,24,96,128]{3,2,1,0:T(8,128)S(1)}, f32[4,24,96,128]{3,2,1,0:T(8,128)S(1)}, f32[256,128]{1,0:T(8,128)S(1)}) custom-call(f32[176,128]{1,0:T(8,128)S(1)} %collective-permute-done.2.c0, ...), custom_call_target="tpu_custom_call", output_to_operand_aliasing={{0}: (3, {}), {1}: (4, {}), {2}: (5, {}), {3}: (6, {})} | custom-call | tf_op jit(solution)/shard_map/corner/pallas_call | solution.py:456
  27.6 26.4 %all_to_all.11 = f32[256,1,128]{2,1,0:T(1,128)S(1)} all-to-all(f32[256,1,128]{2,1,0:T(1,128)S(1)} %bitcast.5), channel_id=1, replica_groups=mesh['gx'=32,'gy'=8] {'gx','gy'}, dimensions={0} | all-to-all | bytes 262144 | tf_op jit(solution)/shard_map/all_to_all | solution.py:546
  54.0 5.1 %combine.1 = (f32[10,16,64,128]{3,2,1,0:T(8,128)}, f32[10,10]{1,0:T(8,128)}, f32[2,16,64,128]{3,2,1,0:T(8,128)}) custom-call(f32[256,128]{1,0:T(8,128)S(1)} %bitcast.4, f32[4,2,24,96,128]{4,3,2,1,0:T(8,128)S(1)} %get-tuple-element.51.V, f32[2,16,64,128]{3,2,1,0:T(8,128)S(1)} %get-tuple-element.52.V4), custom_call_target="tpu_custom_call" | custom-call | tf_op jit(solution)/shard_map/combine/pallas_call | solution.py:456
Async XLA Ops:
  2.6 19.6 %collective-permute-start.4 = (f32[14,64,128]{2,1,0:T(8,128)S(1)}, f32[14,64,128]{2,1,0:T(8,128)S(1)}, u32[]{:S(2)}, u32[]{:S(2)}) collective-permute-start(f32[14,64,128]{2,1,0:T(8,128)S(1)} %get-tuple-element.36), channel_id=1, source_target_pairs={{0,8},{16,24},{32,40},{48,56},{64,72},{80,88},{96,104},{112,120},{... | collective-permute-start | bytes 1376264 | tf_op jit(solution)/shard_map/ppermute | solution.py:486
  5.2 17.0 %collective-permute-start.5 = (f32[14,64,128]{2,1,0:T(8,128)S(1)}, f32[14,64,128]{2,1,0:T(8,128)S(1)}, u32[]{:S(2)}, u32[]{:S(2)}) collective-permute-start(f32[14,64,128]{2,1,0:T(8,128)S(1)} %get-tuple-element.37), channel_id=1, source_target_pairs={{8,16},{24,32},{40,48},{56,64},{72,80},{88,96},{104,112},{120,128}... | collective-permute-start | bytes 1376264 | tf_op jit(solution)/shard_map/ppermute | solution.py:486
  5.9 8.8 %collective-permute-start = (f32[384,128]{1,0:T(8,128)S(1)}, f32[384,128]{1,0:T(8,128)S(1)}, u32[]{:S(2)}, u32[]{:S(2)}) collective-permute-start(f32[384,128]{1,0:T(8,128)S(1)} %get-tuple-element.28), channel_id=1, source_target_pairs={{0,1},{2,3},{4,5},{6,7},{1,0},{3,2},{5,4},{7,6},{8,9},{10,11},{12,... | collective-permute-start | bytes 589832 | tf_op jit(solution)/shard_map/ppermute | solution.py:486
  6.9 7.7 %collective-permute-start.1 = (f32[384,128]{1,0:T(8,128)S(1)}, f32[384,128]{1,0:T(8,128)S(1)}, u32[]{:S(2)}, u32[]{:S(2)}) collective-permute-start(f32[384,128]{1,0:T(8,128)S(1)} %get-tuple-element.29), channel_id=1, source_target_pairs={{1,2},{3,4},{5,6},{2,1},{4,3},{6,5},{9,10},{11,12},{13,14},{10,9},... | collective-permute-start | bytes 589832 | tf_op jit(solution)/shard_map/ppermute | solution.py:486
  14.8 10.7 %collective-permute-start.2 = (f32[176,128]{1,0:T(8,128)S(1)}, f32[176,128]{1,0:T(8,128)S(1)}, u32[]{:S(2)}, u32[]{:S(2)}) collective-permute-start(f32[176,128]{1,0:T(8,128)S(1)} %get-tuple-element.34), channel_id=1, source_target_pairs={{0,8},{16,24},{32,40},{48,56},{64,72},{80,88},{96,104},{112,120},{... | collective-permute-start | bytes 270344 | tf_op jit(solution)/shard_map/ppermute | solution.py:486
  19.7 5.8 %collective-permute-start.3 = (f32[176,128]{1,0:T(8,128)S(1)}, f32[176,128]{1,0:T(8,128)S(1)}, u32[]{:S(2)}, u32[]{:S(2)}) collective-permute-start(f32[176,128]{1,0:T(8,128)S(1)} %get-tuple-element.35), channel_id=1, source_target_pairs={{8,16},{24,32},{40,48},{56,64},{72,80},{88,96},{104,112},{120,128}... | collective-permute-start | bytes 270344 | tf_op jit(solution)/shard_map/ppermute | solution.py:486

commit v8 on v7

--- a/solution.py
+++ b/solution.py
@@ -26,6 +26,13 @@
 
 def toward_high(axis, pairing):
     return lax.axis_index(axis) % 2 == pairing
+
+
+def within(axis, pairing, value):
+    if pairing == 0:
+        return value
+    i = lax.axis_index(axis)
+    return jnp.where((i == 0) | (i == lax.axis_size(axis) - 1), 0.0, value)
 
 
 def pack_kernel(X, Y, rhs, vel, diag, x0, x1, y0, y1, V, U, sems):
@@ -77,7 +84,7 @@
     for f in range(6):
         for x in range(X):
             at = 4 * (f * X + x)
-            a, b = y0[at : at + 4, :], y1[at : at + 4, :]
+            a, b = y0[at : at + 4, :], within("gy", 1, y1[at : at + 4, :])
             field = V.at[0, f, 4 + x] if f < 2 else U.at[f - 2, 4 + x]
             field[YP - 4 : YP, :] = jnp.where(first_high, b, a)
             field[YP + Y : YP + Y + 4, :] = jnp.where(first_high, a, b)
@@ -269,7 +276,7 @@
         at3, at2 = jnp.where(high, X + 4, 1), jnp.where(high, X + 4, 2)
         for i in range(3):
             for f in range(RHS):
-                V[0, f, at3 + i, YP : YP + Y, :] = got[3 * f + i]
+                V[0, f, at3 + i, YP : YP + Y, :] = within("gx", pairing, got[3 * f + i])
         for i in range(2):
             for c in range(4):
                 U[c, at2 + i, YP : YP + Y, :] = got[6 + 2 * c + i]
@@ -287,9 +294,10 @@
     for pairing, got in enumerate((c0, c1)):
         high = toward_high("gx", pairing)
         for f in range(RHS):
-            V[1, f, jnp.where(high, X + 6, 1), YP : YP + Y, :] = got[f * Y : (f + 1) * Y, :]
+            third = within("gx", pairing, got[f * Y : (f + 1) * Y, :])
+            V[1, f, jnp.where(high, X + 6, 1), YP : YP + Y, :] = third
         for row, (f, x, y) in enumerate(corner_cells(X, Y, high, False)):
-            value = got[RHS * Y + row : RHS * Y + row + 1, :]
+            value = within("gx", pairing, got[RHS * Y + row : RHS * Y + row + 1, :])
             if f < 2:
                 V[0, f, x, y : y + 1, :] = value
             else:
@@ -482,7 +490,7 @@
 
     def swap(value, axis, pairing):
         size = lax.axis_size(axis)
-        pairs = [(i, i + 1) for i in range(pairing, size - 1, 2)]
+        pairs = [(i, (i + 1) % size) for i in range(pairing, size, 2)]
         return lax.ppermute(value, axis, pairs + [(j, i) for i, j in pairs])
 
     v_shape, u_shape = ((S, RHS, XE, YE, Z), PIN), ((4, XE, YE, Z), PIN)

time: 59.3 us -> 57.5 us (0.970)
  blocking collectives: 26.4 us -> 23.6 us
    all_to_all x1, blocking collectives: 26.4 us -> 23.6 us  [body(): gathered = lax.all_to_all(packed, ('gx', 'gy'), 0, 0, tiled=True)]
  transfers between devices with their start and end apart: 6 -> 6, of which waited for: 0 -> 1; matrix products, arithmetic and copies ran while one was open for 0% -> 0% of each run, Pallas kernels for 17% -> 17%
where the time goes in v8:
time: 57.5 us; the launch traced here: 57.3 us
  blocking collectives  23.6 us (41%)
  Pallas kernels  19 us (33%)
  starting transfers between devices  13.4 us (23%)
  between operations  0.87 us (2%)
    all_to_all x1, blocking collectives, body(): gathered = lax.all_to_all(packed, ('gx', 'gy'), 0, 0, tiled=True)  23.6 us
    pallas_call x7, Pallas kernels, call(): pl.pallas_call(kernel, out_shape=tuple((pltpu.VMEM(o, F32) if place == PI...  19 us
    ppermute x6, starting transfers between devices, swap(): return lax.ppermute(value, axis, pairs + [(j, i) for i, j in pairs])  13.4 us
  transfers between devices with their start and end apart: 6, of which 1 were waited for; matrix products, arithmetic and copies ran while one was open for 0% of the time, Pallas kernels for 17%

profile of v8, /device:TPU:1, one launch (start us, length us, event | category | flops | bytes accessed | tf_op | source)
XLA Modules:
  0.0 57.3 jit_solution(9548542245601914810)
XLA Ops:
  0.6 2.0 %pack.1 = (f32[14,64,128]{2,1,0:T(8,128)S(1)}, f32[14,64,128]{2,1,0:T(8,128)S(1)}, f32[384,128]{1,0:T(8,128)S(1)}, f32[384,128]{1,0:T(8,128)S(1)}, f32[4,2,24,96...) custom-call(f32[2,16,64,128]{3,2,1,0:T(8,128)} %rhs.1, f32[3,16,64,128]{3,2,1,0:T(8,128)} %vel.1, f32[16,64,128]{2,1,0:T(8,128)} %diag.1), custom_call_target="tpu_custom_call" | custom-call | tf_op jit(solution)/shard_map/pack/pallas_call | solution.py:464
  2.6 2.6 %collective-permute-start.4 = (f32[14,64,128]{2,1,0:T(8,128)S(1)}, f32[14,64,128]{2,1,0:T(8,128)S(1)}, u32[]{:S(2)}, u32[]{:S(2)}) collective-permute-start(f32[14,64,128]{2,1,0:T(8,128)S(1)} %get-tuple-element.36), channel_id=1, source_target_pairs={{0,8},{16,24},{32,40},{48,56},{64,72},{80,88},{96,104},{112,120},{... | collective-permute-start | bytes 1376264 | tf_op jit(solution)/shard_map/ppermute | solution.py:494
  5.2 6.9 %collective-permute-start.5 = (f32[14,64,128]{2,1,0:T(8,128)S(1)}, f32[14,64,128]{2,1,0:T(8,128)S(1)}, u32[]{:S(2)}, u32[]{:S(2)}) collective-permute-start(f32[14,64,128]{2,1,0:T(8,128)S(1)} %get-tuple-element.37), channel_id=1, source_target_pairs={{8,16},{24,32},{40,48},{56,64},{72,80},{88,96},{104,112},{120,128}... | collective-permute-start | bytes 1376264 | tf_op jit(solution)/shard_map/ppermute | solution.py:494
  12.0 1.2 %collective-permute-start = (f32[384,128]{1,0:T(8,128)S(1)}, f32[384,128]{1,0:T(8,128)S(1)}, u32[]{:S(2)}, u32[]{:S(2)}) collective-permute-start(f32[384,128]{1,0:T(8,128)S(1)} %get-tuple-element.28), channel_id=1, source_target_pairs={{0,1},{2,3},{4,5},{6,7},{1,0},{3,2},{5,4},{7,6},{8,9},{10,11},{12,... | collective-permute-start | bytes 589832 | tf_op jit(solution)/shard_map/ppermute | solution.py:494
  13.3 1.2 %collective-permute-start.1 = (f32[384,128]{1,0:T(8,128)S(1)}, f32[384,128]{1,0:T(8,128)S(1)}, u32[]{:S(2)}, u32[]{:S(2)}) collective-permute-start(f32[384,128]{1,0:T(8,128)S(1)} %get-tuple-element.29), channel_id=1, source_target_pairs={{1,2},{3,4},{5,6},{7,0},{2,1},{4,3},{6,5},{0,7},{9,10},{11,12},{13... | collective-permute-start | bytes 589832 | tf_op jit(solution)/shard_map/ppermute | solution.py:494
  14.5 4.6 %inner.1 = (f32[4,2,24,96,128]{4,3,2,1,0:T(8,128)S(1)}, f32[2,16,64,128]{3,2,1,0:T(8,128)S(1)}, f32[6,24,96,128]{3,2,1,0:T(8,128)S(1)}, f32[16,128]{1,0:T(8,128)S(1)}) custom-call(f32[4,2,24,96,128]{4,3,2,1,0:T(8,128)S(1)} %get-tuple-element.30.V_in, f32[4,24,96,128]{3,2,1,0:T(8,128)S(1)} %get-tuple-element.31.U.U_in), custom_call_target="tpu_custom_call", output_to_operand_aliasing={{0}: (0, {})} | custom-call | tf_op jit(solution)/shard_map/inner/pallas_call | solution.py:464
  19.1 0.0 collective-permute-done.y0
  19.1 0.0 collective-permute-done.1.y1
  19.1 0.2 place_y.1
  19.2 0.1 collective-permute-start.2
  19.3 1.4 %collective-permute-start.3 = (f32[176,128]{1,0:T(8,128)S(1)}, f32[176,128]{1,0:T(8,128)S(1)}, u32[]{:S(2)}, u32[]{:S(2)}) collective-permute-start(f32[176,128]{1,0:T(8,128)S(1)} %get-tuple-element.35), channel_id=1, source_target_pairs={{8,16},{24,32},{40,48},{56,64},{72,80},{88,96},{104,112},{120,128}... | collective-permute-start | bytes 270344 | tf_op jit(solution)/shard_map/ppermute | solution.py:494
  20.8 1.9 %edge.1 = (f32[4,2,24,96,128]{4,3,2,1,0:T(8,128)S(1)}, f32[2,16,64,128]{3,2,1,0:T(8,128)S(1)}, f32[6,24,96,128]{3,2,1,0:T(8,128)S(1)}) custom-call(f32[4,24,96,128]{3,2,1,0:T(8,128)S(1)} %get-tuple-element.39.U.U_in, f32[4,2,24,96,128]{4,3,2,1,0:T(8,128)S(1)} %get-tuple-element.40.V_in, ...), custom_call_target="tpu_custom_call", output_to_operand_aliasing={{0}: (1, {}), {1}: (2, {}), {2}: (3, {})} | custom-call | tf_op jit(solution)/shard_map/edge/pallas_call | solution.py:464
  22.6 0.0 collective-permute-done.4.x0
  22.7 0.0 collective-permute-done.5.x1
  22.7 3.2 %face.1 = (f32[4,2,24,96,128]{4,3,2,1,0:T(8,128)S(1)}, f32[2,16,64,128]{3,2,1,0:T(8,128)S(1)}, f32[6,24,96,128]{3,2,1,0:T(8,128)S(1)}, f32[4,24,96,128]{3,2,1,0:T(8,128)S(1)}, f32[16,128]{1,0:T(8,128)S(1)}) custom-call(f32[14,64,128]{2,1,0:T(8,128)S(1)} %collective-permute-done.4.x0, ...), custom_call_target="tpu_custom_call", output_to_operand_aliasing={{0}: (3, {}), {1}: (4, {}), {2}: (5, {}), {3}: (6, {})} | custom-call | tf_op jit(solution)/shard_map/face/pallas_call | solution.py:464
  25.9 0.0 collective-permute-done.2.c0
  25.9 0.4 collective-permute-done.3.c1
  26.3 2.1 %corner.1 = (f32[4,2,24,96,128]{4,3,2,1,0:T(8,128)S(1)}, f32[2,16,64,128]{3,2,1,0:T(8,128)S(1)}, f32[6,24,96,128]{3,2,1,0:T(8,128)S(1)}, f32[4,24,96,128]{3,2,1,0:T(8,128)S(1)}, f32[256,128]{1,0:T(8,128)S(1)}) custom-call(f32[176,128]{1,0:T(8,128)S(1)} %collective-permute-done.2.c0, ...), custom_call_target="tpu_custom_call", output_to_operand_aliasing={{0}: (3, {}), {1}: (4, {}), {2}: (5, {}), {3}: (6, {})} | custom-call | tf_op jit(solution)/shard_map/corner/pallas_call | solution.py:464
  28.5 23.6 %all_to_all.11 = f32[256,1,128]{2,1,0:T(1,128)S(1)} all-to-all(f32[256,1,128]{2,1,0:T(1,128)S(1)} %bitcast.5), channel_id=1, replica_groups=mesh['gx'=32,'gy'=8] {'gx','gy'}, dimensions={0} | all-to-all | bytes 262144 | tf_op jit(solution)/shard_map/all_to_all | solution.py:554
  52.1 5.1 %combine.1 = (f32[10,16,64,128]{3,2,1,0:T(8,128)}, f32[10,10]{1,0:T(8,128)}, f32[2,16,64,128]{3,2,1,0:T(8,128)}) custom-call(f32[256,128]{1,0:T(8,128)S(1)} %bitcast.4, f32[4,2,24,96,128]{4,3,2,1,0:T(8,128)S(1)} %get-tuple-element.51.V, f32[2,16,64,128]{3,2,1,0:T(8,128)S(1)} %get-tuple-element.52.V4), custom_call_target="tpu_custom_call" | custom-call | tf_op jit(solution)/shard_map/combine/pallas_call | solution.py:464
Async XLA Ops:
  2.6 20.0 %collective-permute-start.4 = (f32[14,64,128]{2,1,0:T(8,128)S(1)}, f32[14,64,128]{2,1,0:T(8,128)S(1)}, u32[]{:S(2)}, u32[]{:S(2)}) collective-permute-start(f32[14,64,128]{2,1,0:T(8,128)S(1)} %get-tuple-element.36), channel_id=1, source_target_pairs={{0,8},{16,24},{32,40},{48,56},{64,72},{80,88},{96,104},{112,120},{... | collective-permute-start | bytes 1376264 | tf_op jit(solution)/shard_map/ppermute | solution.py:494
  5.2 17.5 %collective-permute-start.5 = (f32[14,64,128]{2,1,0:T(8,128)S(1)}, f32[14,64,128]{2,1,0:T(8,128)S(1)}, u32[]{:S(2)}, u32[]{:S(2)}) collective-permute-start(f32[14,64,128]{2,1,0:T(8,128)S(1)} %get-tuple-element.37), channel_id=1, source_target_pairs={{8,16},{24,32},{40,48},{56,64},{72,80},{88,96},{104,112},{120,128}... | collective-permute-start | bytes 1376264 | tf_op jit(solution)/shard_map/ppermute | solution.py:494
  12.0 7.0 %collective-permute-start = (f32[384,128]{1,0:T(8,128)S(1)}, f32[384,128]{1,0:T(8,128)S(1)}, u32[]{:S(2)}, u32[]{:S(2)}) collective-permute-start(f32[384,128]{1,0:T(8,128)S(1)} %get-tuple-element.28), channel_id=1, source_target_pairs={{0,1},{2,3},{4,5},{6,7},{1,0},{3,2},{5,4},{7,6},{8,9},{10,11},{12,... | collective-permute-start | bytes 589832 | tf_op jit(solution)/shard_map/ppermute | solution.py:494
  13.3 5.8 %collective-permute-start.1 = (f32[384,128]{1,0:T(8,128)S(1)}, f32[384,128]{1,0:T(8,128)S(1)}, u32[]{:S(2)}, u32[]{:S(2)}) collective-permute-start(f32[384,128]{1,0:T(8,128)S(1)} %get-tuple-element.29), channel_id=1, source_target_pairs={{1,2},{3,4},{5,6},{7,0},{2,1},{4,3},{6,5},{0,7},{9,10},{11,12},{13... | collective-permute-start | bytes 589832 | tf_op jit(solution)/shard_map/ppermute | solution.py:494
  19.2 6.7 %collective-permute-start.2 = (f32[176,128]{1,0:T(8,128)S(1)}, f32[176,128]{1,0:T(8,128)S(1)}, u32[]{:S(2)}, u32[]{:S(2)}) collective-permute-start(f32[176,128]{1,0:T(8,128)S(1)} %get-tuple-element.34), channel_id=1, source_target_pairs={{0,8},{16,24},{32,40},{48,56},{64,72},{80,88},{96,104},{112,120},{... | collective-permute-start | bytes 270344 | tf_op jit(solution)/shard_map/ppermute | solution.py:494
  19.3 7.0 %collective-permute-start.3 = (f32[176,128]{1,0:T(8,128)S(1)}, f32[176,128]{1,0:T(8,128)S(1)}, u32[]{:S(2)}, u32[]{:S(2)}) collective-permute-start(f32[176,128]{1,0:T(8,128)S(1)} %get-tuple-element.35), channel_id=1, source_target_pairs={{8,16},{24,32},{40,48},{56,64},{72,80},{88,96},{104,112},{120,128}... | collective-permute-start | bytes 270344 | tf_op jit(solution)/shard_map/ppermute | solution.py:494

commit v9 on v8

--- a/solution.py
+++ b/solution.py
@@ -490,8 +490,9 @@
 
     def swap(value, axis, pairing):
         size = lax.axis_size(axis)
-        pairs = [(i, (i + 1) % size) for i in range(pairing, size, 2)]
-        return lax.ppermute(value, axis, pairs + [(j, i) for i, j in pairs])
+        pairs = [(i, i + 1) for i in range(pairing, size - 1, 2)]
+        ends = [(0, 0), (size - 1, size - 1)] if pairing else []
+        return lax.ppermute(value, axis, pairs + [(j, i) for i, j in pairs] + ends)
 
     v_shape, u_shape = ((S, RHS, XE, YE, Z), PIN), ((4, XE, YE, Z), PIN)
     x_slab, y_slab = ((14, Y, Z), PIN), ((24 * X, Z), PIN)

time: 57.5 us -> 59.5 us (1.035)
  blocking collectives: 23.6 us -> 26.4 us
    all_to_all x1, blocking collectives: 23.6 us -> 26.4 us  [body(): gathered = lax.all_to_all(packed, ('gx', 'gy'), 0, 0, tiled=True)]
  transfers between devices with their start and end apart: 6 -> 6, of which waited for: 1 -> 0; matrix products, arithmetic and copies ran while one was open for 0% -> 0% of each run, Pallas kernels for 17% -> 17%
where the time goes in v9:
time: 59.5 us; the launch traced here: 59.3 us
  blocking collectives  26.4 us (44%)
  Pallas kernels  19.1 us (32%)
  starting transfers between devices  12.9 us (22%)
  between operations  0.89 us (1%)
    all_to_all x1, blocking collectives, body(): gathered = lax.all_to_all(packed, ('gx', 'gy'), 0, 0, tiled=True)  26.4 us
    pallas_call x7, Pallas kernels, call(): pl.pallas_call(kernel, out_shape=tuple((pltpu.VMEM(o, F32) if place == PI...  19.1 us
    ppermute x6, starting transfers between devices, swap(): return lax.ppermute(value, axis, pairs + [(j, i) for i, j in pairs] + ends)  12.9 us
  transfers between devices with their start and end apart: 6, of which 0 were waited for; matrix products, arithmetic and copies ran while one was open for 0% of the time, Pallas kernels for 17%

profile of v9, /device:TPU:1, one launch (start us, length us, event | category | flops | bytes accessed | tf_op | source)
XLA Modules:
  0.0 59.3 jit_solution(17281536635961186483)
XLA Ops:
  0.6 2.0 %pack.1 = (f32[14,64,128]{2,1,0:T(8,128)S(1)}, f32[14,64,128]{2,1,0:T(8,128)S(1)}, f32[384,128]{1,0:T(8,128)S(1)}, f32[384,128]{1,0:T(8,128)S(1)}, f32[4,2,24,96...) custom-call(f32[2,16,64,128]{3,2,1,0:T(8,128)} %rhs.1, f32[3,16,64,128]{3,2,1,0:T(8,128)} %vel.1, f32[16,64,128]{2,1,0:T(8,128)} %diag.1), custom_call_target="tpu_custom_call" | custom-call | tf_op jit(solution)/shard_map/pack/pallas_call | solution.py:464
  2.6 2.6 %collective-permute-start.4 = (f32[14,64,128]{2,1,0:T(8,128)S(1)}, f32[14,64,128]{2,1,0:T(8,128)S(1)}, u32[]{:S(2)}, u32[]{:S(2)}) collective-permute-start(f32[14,64,128]{2,1,0:T(8,128)S(1)} %get-tuple-element.36), channel_id=1, source_target_pairs={{0,8},{16,24},{32,40},{48,56},{64,72},{80,88},{96,104},{112,120},{... | collective-permute-start | bytes 1376264 | tf_op jit(solution)/shard_map/ppermute | solution.py:495
  5.2 0.7 %collective-permute-start.5 = (f32[14,64,128]{2,1,0:T(8,128)S(1)}, f32[14,64,128]{2,1,0:T(8,128)S(1)}, u32[]{:S(2)}, u32[]{:S(2)}) collective-permute-start(f32[14,64,128]{2,1,0:T(8,128)S(1)} %get-tuple-element.37), channel_id=1, source_target_pairs={{8,16},{24,32},{40,48},{56,64},{72,80},{88,96},{104,112},{120,128}... | collective-permute-start | bytes 1376264 | tf_op jit(solution)/shard_map/ppermute | solution.py:495
  5.9 1.0 %collective-permute-start = (f32[384,128]{1,0:T(8,128)S(1)}, f32[384,128]{1,0:T(8,128)S(1)}, u32[]{:S(2)}, u32[]{:S(2)}) collective-permute-start(f32[384,128]{1,0:T(8,128)S(1)} %get-tuple-element.28), channel_id=1, source_target_pairs={{0,1},{2,3},{4,5},{6,7},{1,0},{3,2},{5,4},{7,6},{8,9},{10,11},{12,... | collective-permute-start | bytes 589832 | tf_op jit(solution)/shard_map/ppermute | solution.py:495
  6.9 3.1 %collective-permute-start.1 = (f32[384,128]{1,0:T(8,128)S(1)}, f32[384,128]{1,0:T(8,128)S(1)}, u32[]{:S(2)}, u32[]{:S(2)}) collective-permute-start(f32[384,128]{1,0:T(8,128)S(1)} %get-tuple-element.29), channel_id=1, source_target_pairs={{1,2},{3,4},{5,6},{2,1},{4,3},{6,5},{0,0},{7,7},{9,10},{11,12},{13... | collective-permute-start | bytes 589832 | tf_op jit(solution)/shard_map/ppermute | solution.py:495
  10.0 4.6 %inner.1 = (f32[4,2,24,96,128]{4,3,2,1,0:T(8,128)S(1)}, f32[2,16,64,128]{3,2,1,0:T(8,128)S(1)}, f32[6,24,96,128]{3,2,1,0:T(8,128)S(1)}, f32[16,128]{1,0:T(8,128)S(1)}) custom-call(f32[4,2,24,96,128]{4,3,2,1,0:T(8,128)S(1)} %get-tuple-element.30.V_in, f32[4,24,96,128]{3,2,1,0:T(8,128)S(1)} %get-tuple-element.31.U.U_in), custom_call_target="tpu_custom_call", output_to_operand_aliasing={{0}: (0, {})} | custom-call | tf_op jit(solution)/shard_map/inner/pallas_call | solution.py:464
  14.6 0.0 collective-permute-done.y0
  14.6 0.0 collective-permute-done.1.y1
  14.7 0.2 place_y.1
  14.8 4.9 %collective-permute-start.2 = (f32[176,128]{1,0:T(8,128)S(1)}, f32[176,128]{1,0:T(8,128)S(1)}, u32[]{:S(2)}, u32[]{:S(2)}) collective-permute-start(f32[176,128]{1,0:T(8,128)S(1)} %get-tuple-element.34), channel_id=1, source_target_pairs={{0,8},{16,24},{32,40},{48,56},{64,72},{80,88},{96,104},{112,120},{... | collective-permute-start | bytes 270344 | tf_op jit(solution)/shard_map/ppermute | solution.py:495
  19.7 0.7 %collective-permute-start.3 = (f32[176,128]{1,0:T(8,128)S(1)}, f32[176,128]{1,0:T(8,128)S(1)}, u32[]{:S(2)}, u32[]{:S(2)}) collective-permute-start(f32[176,128]{1,0:T(8,128)S(1)} %get-tuple-element.35), channel_id=1, source_target_pairs={{8,16},{24,32},{40,48},{56,64},{72,80},{88,96},{104,112},{120,128}... | collective-permute-start | bytes 270344 | tf_op jit(solution)/shard_map/ppermute | solution.py:495
  20.3 1.9 %edge.1 = (f32[4,2,24,96,128]{4,3,2,1,0:T(8,128)S(1)}, f32[2,16,64,128]{3,2,1,0:T(8,128)S(1)}, f32[6,24,96,128]{3,2,1,0:T(8,128)S(1)}) custom-call(f32[4,24,96,128]{3,2,1,0:T(8,128)S(1)} %get-tuple-element.39.U.U_in, f32[4,2,24,96,128]{4,3,2,1,0:T(8,128)S(1)} %get-tuple-element.40.V_in, ...), custom_call_target="tpu_custom_call", output_to_operand_aliasing={{0}: (1, {}), {1}: (2, {}), {2}: (3, {})} | custom-call | tf_op jit(solution)/shard_map/edge/pallas_call | solution.py:464
  22.2 0.0 collective-permute-done.4.x0
  22.2 0.0 collective-permute-done.5.x1
  22.2 3.2 %face.1 = (f32[4,2,24,96,128]{4,3,2,1,0:T(8,128)S(1)}, f32[2,16,64,128]{3,2,1,0:T(8,128)S(1)}, f32[6,24,96,128]{3,2,1,0:T(8,128)S(1)}, f32[4,24,96,128]{3,2,1,0:T(8,128)S(1)}, f32[16,128]{1,0:T(8,128)S(1)}) custom-call(f32[14,64,128]{2,1,0:T(8,128)S(1)} %collective-permute-done.4.x0, ...), custom_call_target="tpu_custom_call", output_to_operand_aliasing={{0}: (3, {}), {1}: (4, {}), {2}: (5, {}), {3}: (6, {})} | custom-call | tf_op jit(solution)/shard_map/face/pallas_call | solution.py:464
  25.5 0.0 collective-permute-done.2.c0
  25.5 0.0 collective-permute-done.3.c1
  25.5 2.2 %corner.1 = (f32[4,2,24,96,128]{4,3,2,1,0:T(8,128)S(1)}, f32[2,16,64,128]{3,2,1,0:T(8,128)S(1)}, f32[6,24,96,128]{3,2,1,0:T(8,128)S(1)}, f32[4,24,96,128]{3,2,1,0:T(8,128)S(1)}, f32[256,128]{1,0:T(8,128)S(1)}) custom-call(f32[176,128]{1,0:T(8,128)S(1)} %collective-permute-done.2.c0, ...), custom_call_target="tpu_custom_call", output_to_operand_aliasing={{0}: (3, {}), {1}: (4, {}), {2}: (5, {}), {3}: (6, {})} | custom-call | tf_op jit(solution)/shard_map/corner/pallas_call | solution.py:464
  27.6 26.4 %all_to_all.11 = f32[256,1,128]{2,1,0:T(1,128)S(1)} all-to-all(f32[256,1,128]{2,1,0:T(1,128)S(1)} %bitcast.5), channel_id=1, replica_groups=mesh['gx'=32,'gy'=8] {'gx','gy'}, dimensions={0} | all-to-all | bytes 262144 | tf_op jit(solution)/shard_map/all_to_all | solution.py:555
  54.1 5.1 %combine.1 = (f32[10,16,64,128]{3,2,1,0:T(8,128)}, f32[10,10]{1,0:T(8,128)}, f32[2,16,64,128]{3,2,1,0:T(8,128)}) custom-call(f32[256,128]{1,0:T(8,128)S(1)} %bitcast.4, f32[4,2,24,96,128]{4,3,2,1,0:T(8,128)S(1)} %get-tuple-element.51.V, f32[2,16,64,128]{3,2,1,0:T(8,128)S(1)} %get-tuple-element.52.V4), custom_call_target="tpu_custom_call" | custom-call | tf_op jit(solution)/shard_map/combine/pallas_call | solution.py:464
Async XLA Ops:
  2.6 19.6 %collective-permute-start.4 = (f32[14,64,128]{2,1,0:T(8,128)S(1)}, f32[14,64,128]{2,1,0:T(8,128)S(1)}, u32[]{:S(2)}, u32[]{:S(2)}) collective-permute-start(f32[14,64,128]{2,1,0:T(8,128)S(1)} %get-tuple-element.36), channel_id=1, source_target_pairs={{0,8},{16,24},{32,40},{48,56},{64,72},{80,88},{96,104},{112,120},{... | collective-permute-start | bytes 1376264 | tf_op jit(solution)/shard_map/ppermute | solution.py:495
  5.2 17.1 %collective-permute-start.5 = (f32[14,64,128]{2,1,0:T(8,128)S(1)}, f32[14,64,128]{2,1,0:T(8,128)S(1)}, u32[]{:S(2)}, u32[]{:S(2)}) collective-permute-start(f32[14,64,128]{2,1,0:T(8,128)S(1)} %get-tuple-element.37), channel_id=1, source_target_pairs={{8,16},{24,32},{40,48},{56,64},{72,80},{88,96},{104,112},{120,128}... | collective-permute-start | bytes 1376264 | tf_op jit(solution)/shard_map/ppermute | solution.py:495
  5.9 8.8 %collective-permute-start = (f32[384,128]{1,0:T(8,128)S(1)}, f32[384,128]{1,0:T(8,128)S(1)}, u32[]{:S(2)}, u32[]{:S(2)}) collective-permute-start(f32[384,128]{1,0:T(8,128)S(1)} %get-tuple-element.28), channel_id=1, source_target_pairs={{0,1},{2,3},{4,5},{6,7},{1,0},{3,2},{5,4},{7,6},{8,9},{10,11},{12,... | collective-permute-start | bytes 589832 | tf_op jit(solution)/shard_map/ppermute | solution.py:495
  6.9 7.7 %collective-permute-start.1 = (f32[384,128]{1,0:T(8,128)S(1)}, f32[384,128]{1,0:T(8,128)S(1)}, u32[]{:S(2)}, u32[]{:S(2)}) collective-permute-start(f32[384,128]{1,0:T(8,128)S(1)} %get-tuple-element.29), channel_id=1, source_target_pairs={{1,2},{3,4},{5,6},{2,1},{4,3},{6,5},{0,0},{7,7},{9,10},{11,12},{13... | collective-permute-start | bytes 589832 | tf_op jit(solution)/shard_map/ppermute | solution.py:495
  14.8 10.7 %collective-permute-start.2 = (f32[176,128]{1,0:T(8,128)S(1)}, f32[176,128]{1,0:T(8,128)S(1)}, u32[]{:S(2)}, u32[]{:S(2)}) collective-permute-start(f32[176,128]{1,0:T(8,128)S(1)} %get-tuple-element.34), channel_id=1, source_target_pairs={{0,8},{16,24},{32,40},{48,56},{64,72},{80,88},{96,104},{112,120},{... | collective-permute-start | bytes 270344 | tf_op jit(solution)/shard_map/ppermute | solution.py:495
  19.7 5.8 %collective-permute-start.3 = (f32[176,128]{1,0:T(8,128)S(1)}, f32[176,128]{1,0:T(8,128)S(1)}, u32[]{:S(2)}, u32[]{:S(2)}) collective-permute-start(f32[176,128]{1,0:T(8,128)S(1)} %get-tuple-element.35), channel_id=1, source_target_pairs={{8,16},{24,32},{40,48},{56,64},{72,80},{88,96},{104,112},{120,128}... | collective-permute-start | bytes 270344 | tf_op jit(solution)/shard_map/ppermute | solution.py:495

commit v10 on v8

--- a/solution.py
+++ b/solution.py
@@ -491,6 +491,10 @@
     def swap(value, axis, pairing):
         size = lax.axis_size(axis)
         pairs = [(i, (i + 1) % size) for i in range(pairing, size, 2)]
+        if axis == "gx" and pairing == 1:
+            pairs = [(i * ny + j, (i + 1) * ny + j) for i in range(1, nx - 1, 2) for j in range(ny)]
+            pairs += [(i * ny + j, i * ny + j + 1) for i in (0, nx - 1) for j in range(0, ny, 2)]
+            axis = ("gx", "gy")
         return lax.ppermute(value, axis, pairs + [(j, i) for i, j in pairs])
 
     v_shape, u_shape = ((S, RHS, XE, YE, Z), PIN), ((4, XE, YE, Z), PIN)

time: 57.5 us -> 57 us (level)
  starting transfers between devices: 13.4 us -> 10.6 us
  blocking collectives: 23.6 us -> 26.4 us
    ppermute x6, starting transfers between devices: 13.4 us -> 10.6 us  [swap(): return lax.ppermute(value, axis, pairs + [(j, i) for i, j in pairs])]
    all_to_all x1, blocking collectives: 23.6 us -> 26.4 us  [body(): gathered = lax.all_to_all(packed, ('gx', 'gy'), 0, 0, tiled=True)]
  transfers between devices with their start and end apart: 6 -> 6, of which waited for: 1 -> 0; matrix products, arithmetic and copies ran while one was open for 0% -> 0% of each run, Pallas kernels for 17% -> 17%
where the time goes in v10:
time: 57 us; the launch traced here: 56.8 us
  blocking collectives  26.4 us (46%)
  Pallas kernels  19 us (33%)
  starting transfers between devices  10.6 us (19%)
  between operations  0.87 us (2%)
    all_to_all x1, blocking collectives, body(): gathered = lax.all_to_all(packed, ('gx', 'gy'), 0, 0, tiled=True)  26.4 us
    pallas_call x7, Pallas kernels, call(): pl.pallas_call(kernel, out_shape=tuple((pltpu.VMEM(o, F32) if place == PI...  19 us
    ppermute x6, starting transfers between devices, swap(): return lax.ppermute(value, axis, pairs + [(j, i) for i, j in pairs])  10.6 us
  transfers between devices with their start and end apart: 6, of which 0 were waited for; matrix products, arithmetic and copies ran while one was open for 0% of the time, Pallas kernels for 17%

profile of v10, /device:TPU:1, one launch (start us, length us, event | category | flops | bytes accessed | tf_op | source)
XLA Modules:
  0.0 56.8 jit_solution(13885389938036238721)
XLA Ops:
  0.6 2.0 %pack.1 = (f32[14,64,128]{2,1,0:T(8,128)S(1)}, f32[14,64,128]{2,1,0:T(8,128)S(1)}, f32[384,128]{1,0:T(8,128)S(1)}, f32[384,128]{1,0:T(8,128)S(1)}, f32[4,2,24,96...) custom-call(f32[2,16,64,128]{3,2,1,0:T(8,128)} %rhs.1, f32[3,16,64,128]{3,2,1,0:T(8,128)} %vel.1, f32[16,64,128]{2,1,0:T(8,128)} %diag.1), custom_call_target="tpu_custom_call" | custom-call | tf_op jit(solution)/shard_map/pack/pallas_call | solution.py:464
  2.6 2.6 %collective-permute-start.4 = (f32[14,64,128]{2,1,0:T(8,128)S(1)}, f32[14,64,128]{2,1,0:T(8,128)S(1)}, u32[]{:S(2)}, u32[]{:S(2)}) collective-permute-start(f32[14,64,128]{2,1,0:T(8,128)S(1)} %get-tuple-element.36), channel_id=1, source_target_pairs={{0,8},{16,24},{32,40},{48,56},{64,72},{80,88},{96,104},{112,120},{... | collective-permute-start | bytes 1376264 | tf_op jit(solution)/shard_map/ppermute | solution.py:498
  5.2 1.0 %collective-permute-start.5 = (f32[14,64,128]{2,1,0:T(8,128)S(1)}, f32[14,64,128]{2,1,0:T(8,128)S(1)}, u32[]{:S(2)}, u32[]{:S(2)}) collective-permute-start(f32[14,64,128]{2,1,0:T(8,128)S(1)} %get-tuple-element.37), channel_id=1, source_target_pairs={{8,16},{9,17},{10,18},{11,19},{12,20},{13,21},{14,22},{15,23},{24,... | collective-permute-start | bytes 1376264 | tf_op jit(solution)/shard_map/ppermute | solution.py:498
  6.1 0.0 collective-permute-start
  6.2 1.7 %collective-permute-start.1 = (f32[384,128]{1,0:T(8,128)S(1)}, f32[384,128]{1,0:T(8,128)S(1)}, u32[]{:S(2)}, u32[]{:S(2)}) collective-permute-start(f32[384,128]{1,0:T(8,128)S(1)} %get-tuple-element.29), channel_id=1, source_target_pairs={{1,2},{3,4},{5,6},{7,0},{2,1},{4,3},{6,5},{0,7},{9,10},{11,12},{13... | collective-permute-start | bytes 589832 | tf_op jit(solution)/shard_map/ppermute | solution.py:498
  7.8 4.6 %inner.1 = (f32[4,2,24,96,128]{4,3,2,1,0:T(8,128)S(1)}, f32[2,16,64,128]{3,2,1,0:T(8,128)S(1)}, f32[6,24,96,128]{3,2,1,0:T(8,128)S(1)}, f32[16,128]{1,0:T(8,128)S(1)}) custom-call(f32[4,2,24,96,128]{4,3,2,1,0:T(8,128)S(1)} %get-tuple-element.30.V_in, f32[4,24,96,128]{3,2,1,0:T(8,128)S(1)} %get-tuple-element.31.U.U_in), custom_call_target="tpu_custom_call", output_to_operand_aliasing={{0}: (0, {})} | custom-call | tf_op jit(solution)/shard_map/inner/pallas_call | solution.py:464
  12.4 0.0 collective-permute-done.y0
  12.4 0.0 collective-permute-done.1.y1
  12.5 0.2 place_y.1
  12.6 3.1 %collective-permute-start.2 = (f32[176,128]{1,0:T(8,128)S(1)}, f32[176,128]{1,0:T(8,128)S(1)}, u32[]{:S(2)}, u32[]{:S(2)}) collective-permute-start(f32[176,128]{1,0:T(8,128)S(1)} %get-tuple-element.34), channel_id=1, source_target_pairs={{0,8},{16,24},{32,40},{48,56},{64,72},{80,88},{96,104},{112,120},{... | collective-permute-start | bytes 270344 | tf_op jit(solution)/shard_map/ppermute | solution.py:498
  15.7 2.2 %collective-permute-start.3 = (f32[176,128]{1,0:T(8,128)S(1)}, f32[176,128]{1,0:T(8,128)S(1)}, u32[]{:S(2)}, u32[]{:S(2)}) collective-permute-start(f32[176,128]{1,0:T(8,128)S(1)} %get-tuple-element.35), channel_id=1, source_target_pairs={{8,16},{9,17},{10,18},{11,19},{12,20},{13,21},{14,22},{15,23},{24,... | collective-permute-start | bytes 270344 | tf_op jit(solution)/shard_map/ppermute | solution.py:498
  18.0 1.9 %edge.1 = (f32[4,2,24,96,128]{4,3,2,1,0:T(8,128)S(1)}, f32[2,16,64,128]{3,2,1,0:T(8,128)S(1)}, f32[6,24,96,128]{3,2,1,0:T(8,128)S(1)}) custom-call(f32[4,24,96,128]{3,2,1,0:T(8,128)S(1)} %get-tuple-element.39.U.U_in, f32[4,2,24,96,128]{4,3,2,1,0:T(8,128)S(1)} %get-tuple-element.40.V_in, ...), custom_call_target="tpu_custom_call", output_to_operand_aliasing={{0}: (1, {}), {1}: (2, {}), {2}: (3, {})} | custom-call | tf_op jit(solution)/shard_map/edge/pallas_call | solution.py:464
  19.8 0.0 collective-permute-done.4.x0
  19.8 0.0 collective-permute-done.5.x1
  19.9 3.2 %face.1 = (f32[4,2,24,96,128]{4,3,2,1,0:T(8,128)S(1)}, f32[2,16,64,128]{3,2,1,0:T(8,128)S(1)}, f32[6,24,96,128]{3,2,1,0:T(8,128)S(1)}, f32[4,24,96,128]{3,2,1,0:T(8,128)S(1)}, f32[16,128]{1,0:T(8,128)S(1)}) custom-call(f32[14,64,128]{2,1,0:T(8,128)S(1)} %collective-permute-done.4.x0, ...), custom_call_target="tpu_custom_call", output_to_operand_aliasing={{0}: (3, {}), {1}: (4, {}), {2}: (5, {}), {3}: (6, {})} | custom-call | tf_op jit(solution)/shard_map/face/pallas_call | solution.py:464
  23.1 0.0 collective-permute-done.2.c0
  23.1 0.0 collective-permute-done.3.c1
  23.1 2.2 %corner.1 = (f32[4,2,24,96,128]{4,3,2,1,0:T(8,128)S(1)}, f32[2,16,64,128]{3,2,1,0:T(8,128)S(1)}, f32[6,24,96,128]{3,2,1,0:T(8,128)S(1)}, f32[4,24,96,128]{3,2,1,0:T(8,128)S(1)}, f32[256,128]{1,0:T(8,128)S(1)}) custom-call(f32[176,128]{1,0:T(8,128)S(1)} %collective-permute-done.2.c0, ...), custom_call_target="tpu_custom_call", output_to_operand_aliasing={{0}: (3, {}), {1}: (4, {}), {2}: (5, {}), {3}: (6, {})} | custom-call | tf_op jit(solution)/shard_map/corner/pallas_call | solution.py:464
  25.3 26.4 %all_to_all.11 = f32[256,1,128]{2,1,0:T(1,128)S(1)} all-to-all(f32[256,1,128]{2,1,0:T(1,128)S(1)} %bitcast.5), channel_id=1, replica_groups=mesh['gx'=32,'gy'=8] {'gx','gy'}, dimensions={0} | all-to-all | bytes 262144 | tf_op jit(solution)/shard_map/all_to_all | solution.py:558
  51.6 5.1 %combine.1 = (f32[10,16,64,128]{3,2,1,0:T(8,128)}, f32[10,10]{1,0:T(8,128)}, f32[2,16,64,128]{3,2,1,0:T(8,128)}) custom-call(f32[256,128]{1,0:T(8,128)S(1)} %bitcast.4, f32[4,2,24,96,128]{4,3,2,1,0:T(8,128)S(1)} %get-tuple-element.51.V, f32[2,16,64,128]{3,2,1,0:T(8,128)S(1)} %get-tuple-element.52.V4), custom_call_target="tpu_custom_call" | custom-call | tf_op jit(solution)/shard_map/combine/pallas_call | solution.py:464
Async XLA Ops:
  2.6 17.2 %collective-permute-start.4 = (f32[14,64,128]{2,1,0:T(8,128)S(1)}, f32[14,64,128]{2,1,0:T(8,128)S(1)}, u32[]{:S(2)}, u32[]{:S(2)}) collective-permute-start(f32[14,64,128]{2,1,0:T(8,128)S(1)} %get-tuple-element.36), channel_id=1, source_target_pairs={{0,8},{16,24},{32,40},{48,56},{64,72},{80,88},{96,104},{112,120},{... | collective-permute-start | bytes 1376264 | tf_op jit(solution)/shard_map/ppermute | solution.py:498
  5.2 14.7 %collective-permute-start.5 = (f32[14,64,128]{2,1,0:T(8,128)S(1)}, f32[14,64,128]{2,1,0:T(8,128)S(1)}, u32[]{:S(2)}, u32[]{:S(2)}) collective-permute-start(f32[14,64,128]{2,1,0:T(8,128)S(1)} %get-tuple-element.37), channel_id=1, source_target_pairs={{8,16},{9,17},{10,18},{11,19},{12,20},{13,21},{14,22},{15,23},{24,... | collective-permute-start | bytes 1376264 | tf_op jit(solution)/shard_map/ppermute | solution.py:498
  6.1 6.3 %collective-permute-start = (f32[384,128]{1,0:T(8,128)S(1)}, f32[384,128]{1,0:T(8,128)S(1)}, u32[]{:S(2)}, u32[]{:S(2)}) collective-permute-start(f32[384,128]{1,0:T(8,128)S(1)} %get-tuple-element.28), channel_id=1, source_target_pairs={{0,1},{2,3},{4,5},{6,7},{1,0},{3,2},{5,4},{7,6},{8,9},{10,11},{12,... | collective-permute-start | bytes 589832 | tf_op jit(solution)/shard_map/ppermute | solution.py:498
  6.2 6.3 %collective-permute-start.1 = (f32[384,128]{1,0:T(8,128)S(1)}, f32[384,128]{1,0:T(8,128)S(1)}, u32[]{:S(2)}, u32[]{:S(2)}) collective-permute-start(f32[384,128]{1,0:T(8,128)S(1)} %get-tuple-element.29), channel_id=1, source_target_pairs={{1,2},{3,4},{5,6},{7,0},{2,1},{4,3},{6,5},{0,7},{9,10},{11,12},{13... | collective-permute-start | bytes 589832 | tf_op jit(solution)/shard_map/ppermute | solution.py:498
  12.6 10.5 %collective-permute-start.2 = (f32[176,128]{1,0:T(8,128)S(1)}, f32[176,128]{1,0:T(8,128)S(1)}, u32[]{:S(2)}, u32[]{:S(2)}) collective-permute-start(f32[176,128]{1,0:T(8,128)S(1)} %get-tuple-element.34), channel_id=1, source_target_pairs={{0,8},{16,24},{32,40},{48,56},{64,72},{80,88},{96,104},{112,120},{... | collective-permute-start | bytes 270344 | tf_op jit(solution)/shard_map/ppermute | solution.py:498
  15.7 7.4 %collective-permute-start.3 = (f32[176,128]{1,0:T(8,128)S(1)}, f32[176,128]{1,0:T(8,128)S(1)}, u32[]{:S(2)}, u32[]{:S(2)}) collective-permute-start(f32[176,128]{1,0:T(8,128)S(1)} %get-tuple-element.35), channel_id=1, source_target_pairs={{8,16},{9,17},{10,18},{11,19},{12,20},{13,21},{14,22},{15,23},{24,... | collective-permute-start | bytes 270344 | tf_op jit(solution)/shard_map/ppermute | solution.py:498
